TPU v7x, 32 devices: a whole 2x2x4 slice. The times are simulated.
32 devices in a mesh: seq: 8 (over z, x), tp: 4 (over y, core).
Axes of the slice: x: 2, y: 2, z: 4, core: 2. Of those that a mesh axis runs over, the one named last changes fastest.
Arguments:
- tokens: bfloat16 [4096, 2048], P('seq', 'tp'), may hold values from -6 to 6
- norm_gain: float32 [2048], replicated, may hold values from 0.1 to 1.9
- w_query: bfloat16 [2048, 2048], P(None, 'tp'), may hold values from -0.125 to 0.125
- w_keyval: bfloat16 [2048, 256], replicated, may hold values from -0.125 to 0.125
- w_out: bfloat16 [2048, 2048], P('tp'), may hold values from -0.5 to 0.5
- span_lens: int32 [8], P('seq'), may hold values from 1 to 512, 3072 in all
- cached_lens: int32 [8], P('seq'), may hold values from 1 to 1536, 6144 in all
- old_table: int32 [8, 8], P('seq'), may hold values from 0 to 7, each once within a row
- new_table: int32 [8, 8], P('seq'), may hold values from 0 to 7, each once within a row
- old_cache: bfloat16 [64, 256, 256], P('seq', 'tp'), may hold values from -720 to 720
Outputs:
- mixed: bfloat16 [4096, 2048], P('seq', 'tp')
- new_cache: bfloat16 [64, 256, 256], P('seq', 'tp')
Inputs may be any that keep to these rules, and one draw needn't show every extreme that they name: Request r's new tokens are the first span_lens[r] of its 512 rows. `old_table`: each row names every device once: each device holds exactly one block of every request. `new_table`: each row names every device once: each device receives exactly one block of every request.
All inputs are finite; a program needn't handle non-finite values. No bound on the sum of `span_lens` or of `cached_lens` on one device may be relied on, other than what follows from the above.
Results may differ from a plain program's by a relative error of at most 0.012.
The roundings to bfloat16 on the way count: a program that leaves them out, or rounds other values in their place, can miss the bound.
Values may be sent and summed in bfloat16 or wider, within the bound.
No kernel may reach another device: no remote copies, remote signals or barrier semaphores. Data moves between devices by JAX's collectives and lax.ppermute only.
A program may use at most 128 MiB of HBM per device.

v0:
```python
import jax
import jax.numpy as jnp
from jax import lax
from jax.sharding import PartitionSpec as P

EPSILON = 1e-05
MASKED = -1e30


def normalize(rows, norm_gain):
    values = rows.astype(jnp.float32)
    average = jnp.mean(values, axis=1, keepdims=True)
    centred = values - average
    spread = jnp.mean(centred * centred, axis=1, keepdims=True)
    return (centred * lax.rsqrt(spread + EPSILON) * norm_gain).astype(jnp.bfloat16)


def body(
    tokens,
    norm_gain,
    w_query,
    w_keyval,
    w_out,
    span_lens,
    cached_lens,
    old_table,
    new_table,
    old_cache,
):
    full_rows = lax.all_gather(tokens, "tp", axis=1, tiled=True)
    normed = normalize(full_rows, norm_gain)
    query = jnp.dot(normed, w_query, preferred_element_type=jnp.float32).astype(jnp.bfloat16)
    keyval = jnp.dot(normed, w_keyval, preferred_element_type=jnp.float32).astype(jnp.bfloat16)
    groups = lax.axis_size("seq")
    tp_count = lax.axis_size("tp")
    holders = old_table[0]
    pooled = lax.all_gather(old_cache, "tp", axis=1, tiled=True)
    arrived = lax.all_to_all(pooled, "seq", split_axis=0, concat_axis=0, tiled=True)
    ordered = jnp.take(arrived, holders, axis=0)
    block_rows = ordered.shape[1]
    width = ordered.shape[2]
    capacity = groups * block_rows
    cached = ordered.reshape(capacity, width)
    held_len = cached_lens[0]
    span_len = span_lens[0]
    tok_rows = tokens.shape[0]
    share = block_rows // tp_count
    targets = new_table[0]
    device_ids = lax.broadcasted_iota(jnp.int32, (groups, groups), 0)
    block_ids = lax.broadcasted_iota(jnp.int32, (groups, groups), 1)
    matches = targets[None, :] == device_ids
    sources = jnp.sum(jnp.where(matches, block_ids, 0), axis=1)
    positions = lax.broadcasted_iota(jnp.int32, (capacity, 1), 0)
    placed = lax.dynamic_update_slice(cached, keyval, (held_len, jnp.int32(0)))
    fresh = jnp.where(positions < held_len + span_len, placed, jnp.zeros_like(placed))
    head_size = width // 2
    keys = fresh[:, :head_size]
    values = fresh[:, head_size:]
    local_heads = query.shape[1] // head_size
    query3 = query.reshape(tok_rows, local_heads, head_size)
    scores = jnp.einsum(
        "thd,kd->htk", query3, keys, preferred_element_type=jnp.float32
    ) * head_size ** (-0.5)
    row_pos = lax.broadcasted_iota(jnp.int32, (tok_rows, 1), 0)
    key_pos = lax.broadcasted_iota(jnp.int32, (1, capacity), 1)
    allowed = key_pos <= held_len + row_pos
    scores = jnp.where(allowed[None], scores, MASKED)
    top = jnp.max(scores, axis=2, keepdims=True)
    weights = jnp.exp(scores - top)
    probs = (weights / jnp.sum(weights, axis=2, keepdims=True)).astype(jnp.bfloat16)
    context = jnp.einsum("htk,kd->thd", probs, values, preferred_element_type=jnp.float32).astype(
        jnp.bfloat16
    )
    context = context.reshape(tok_rows, local_heads * head_size)
    partial_out = jnp.dot(context, w_out, preferred_element_type=jnp.float32)
    summed = lax.psum_scatter(
        partial_out.astype(jnp.bfloat16), "tp", scatter_dimension=1, tiled=True
    ).astype(jnp.float32)
    total = tokens.astype(jnp.float32) + summed
    mixed = jnp.where(row_pos < span_len, total, jnp.zeros_like(total)).astype(jnp.bfloat16)
    mine_part = lax.dynamic_slice_in_dim(
        fresh.reshape(groups, block_rows, width), lax.axis_index("tp") * share, share, 1
    )
    new_cache = lax.all_to_all(
        jnp.take(mine_part, sources, axis=0), "seq", split_axis=0, concat_axis=0, tiled=True
    )
    return (mixed, new_cache)


def solution(mesh):
    in_specs = (
        P("seq", "tp"),
        P(),
        P(None, "tp"),
        P(),
        P("tp", None),
        P("seq"),
        P("seq"),
        P("seq", None),
        P("seq", None),
        P("seq", "tp", None),
    )
    out_specs = (P("seq", "tp"), P("seq", "tp", None))
    return jax.shard_map(body, mesh=mesh, in_specs=in_specs, out_specs=out_specs, check_vma=False)
```

profile of v0, /device:TPU:0, one launch (start us, length us, event | category | flops | bytes accessed | tf_op | source)
XLA Modules:
  0.0 128.8 jit_solution(5370773024699491548)
XLA Ops:
  8.0 0.7 all-gather.5.cloned.1.call-update
  11.4 1.8 %iota_compare_fusion = pred[512,2048]{0,1:T(8,128)(4,1)} fusion(s32[512]{0:T(512)S(1)} %iota_add_fusion), kind=kLoop, calls=%fused_computation.18 | loop fusion | flops 1048576 | bytes 1050624 | tf_op jit(solution)/shard_map/le | solution.py:66
  13.2 15.8 %all-gather.3.cloned.1.call-done = bf16[8,256,256]{2,1,0:T(8,128)(2,1)} async-done(((bf16[8,64,256]{2,1,0:T(8,128)(2,1)}), bf16[8,256,256]{2,1,0:T(8,128)(2,1)}) %all-gather.3.cloned.1.call-update) | async-done | bytes 1048592 | tf_op jit(solution)/shard_map/all_gather | solution.py:37
  29.0 5.5 %all-to-all-start = ((bf16[8,256,256]{2,1,0:T(8,128)(2,1)}), bf16[8,256,256]{2,1,0:T(8,128)(2,1)S(1)}, u32[]{:S(2)}, u32[]{:S(2)}) async-start(bf16[8,256,256]{2,1,0:T(8,128)(2,1)} %all-gather.3.cloned.1.call-done), calls=%async_computation | async-start | bytes 2097152 | tf_op jit(solution)/shard_map/all_to_all | solution.py:38
  34.6 18.6 %all-gather.5.cloned.1.call-done = bf16[512,2048]{1,0:T(8,128)(2,1)} async-done(((bf16[512,512]{1,0:T(8,128)(2,1)}), bf16[512,2048]{1,0:T(8,128)(2,1)}) %all-gather.5.cloned.1.call-update) | async-done | bytes 2097168 | tf_op jit(solution)/shard_map/all_gather | solution.py:30
  53.2 2.1 %convert_reduce_fusion = f32[512]{0:T(512)S(1)} fusion(bf16[512,2048]{1,0:T(8,128)(2,1)} %all-gather.5.cloned.1.call-done), kind=kLoop, calls=%fused_computation.12 | loop fusion | flops 2096640 | bytes 2099200 | tf_op jit(solution)/shard_map/reduce_sum | solution.py:12
  55.3 2.3 %fusion.8 = f32[512]{0:T(512)S(1)} fusion(bf16[512,2048]{1,0:T(8,128)(2,1)} %all-gather.5.cloned.1.call-done, f32[512]{0:T(512)S(1)} %broadcast_multiply_fusion), kind=kLoop, calls=%fused_computation.15 | loop fusion | flops 4193792 | bytes 2101248 | tf_op jit(solution)/shard_map/reduce_sum | solution.py:14
  57.6 0.7 fusion.10
  58.4 0.7 convolution_convert_fusion.2
  59.2 2.1 %convolution_convert_fusion.1 = bf16[512,512]{0,1:T(8,128)(2,1)} fusion(bf16[512,2048]{1,0:T(8,128)(2,1)S(1)} %fusion.10, bf16[2048,512]{1,0:T(8,128)(2,1)S(1)} %copy-done.5), kind=kOutput, calls=%fused_computation.21 | convolution fusion | flops 1074003968 | bytes 4718592 | tf_op jit(solution)/shard_map/dot_general | solution.py:32
  61.3 1.6 %gather_fusion = bf16[8,256,256]{2,1,0:T(8,128)(2,1)} fusion(bf16[8,256,256]{2,1,0:T(8,128)(2,1)S(1)} %all-to-all-done, s32[1024]{0:T(1024)S(1)} %pad_clamp_fusion.1), kind=kCustom, calls=%fused_computation | custom fusion | bytes 2097184 | tf_op jit(solution)/shard_map/jit(_take)/gather | solution.py:39
  62.9 1.5 %bitcast_select_fusion.4 = bf16[2048,256]{1,0:T(8,128)(2,1)S(1)} fusion(bf16[8,256,256]{2,1,0:T(8,128)(2,1)} %gather_fusion, pred[2048]{0:T(1024)(128)(4,1)S(1)} %broadcast_in_dim.71), kind=kLoop, calls=%fused_computation.24 | loop fusion | flops 524288 | bytes 2099200 | tf_op jit(solution)/shard_map/jit(_take)/select_n | solution.py:39
  64.4 1.7 %dynamic_update_slice.3 = bf16[2048,256]{1,0:T(8,128)(2,1)S(1)} dynamic-update-slice(bf16[2048,256]{1,0:T(8,128)(2,1)S(1)} %bitcast_select_fusion.4, bf16[512,256]{1,0:T(8,128)(2,1)S(1)} %convolution_convert_fusion.2, s32[]{:T(128)S(6)} %select_n.65, s32[]{:T(128)} %constant.15.clone.1) | dynamic-update-slice | bytes 524292 | tf_op jit(solution)/shard_map/dynamic_update_slice | solution.py:54
  66.1 1.2 broadcast_select_fusion
  67.3 10.7 %fusion.19 = (f32[4,512]{1,0:T(4,128)S(1)}, f32[4,512,2048]{1,2,0:T(8,128)}) fusion(pred[512,2048]{0,1:T(8,128)(4,1)} %iota_compare_fusion, bf16[512,4,128]{0,2,1:T(8,128)(2,1)} %bitcast.63, bf16[2048,256]{1,0:T(8,128)(2,1)} %broadcast_select_fusion), kind=kOutput, calls=%fused_computation.51 | convolution fusion | flops 1090521088 | bytes 18882560 | tf_op jit(solution)/shard_map/sub | solution.py:69
  78.0 7.0 %fusion.13 = bf16[128,4,512]{2,0,1:T(8,128)(2,1)S(1)} fusion(f32[4,512,2048]{1,2,0:T(8,128)} %get-tuple-element.3, f32[4,512]{1,0:T(4,128)S(1)} %get-tuple-element.2, bf16[2048,256]{1,0:T(8,128)(2,1)S(1)} %copy-done.3), kind=kOutput, calls=%fused_computation.22 | convolution fusion | flops 1082392576 | bytes 17833984 | tf_op jit(solution)/shard_map/htk,kd->thd/dot_general | solution.py:71
  85.1 2.6 %convolution_convert_fusion = bf16[512,2048]{1,0:T(8,128)(2,1)} fusion(bf16[512,512]{0,1:T(8,128)(2,1)S(1)} %bitcast.64, bf16[512,2048]{1,0:T(8,128)(2,1)S(1)} %copy-done), kind=kOutput, calls=%fused_computation.19 | convolution fusion | flops 1074790400 | bytes 4718592 | tf_op jit(solution)/shard_map/dot_general | solution.py:75
  87.9 1.0 constant_dynamic-slice_fusion
  89.4 0.8 broadcast_select_fusion.1
  90.2 5.7 %all-to-all-start.1 = ((bf16[8,64,256]{2,1,0:T(8,128)(2,1)}), bf16[8,64,256]{2,1,0:T(8,128)(2,1)S(1)}, u32[]{:S(2)}, u32[]{:S(2)}) async-start(bf16[8,64,256]{2,1,0:T(8,128)(2,1)} %broadcast_select_fusion.1), calls=%async_computation.2 | async-start | bytes 524288 | tf_op jit(solution)/shard_map/all_to_all | solution.py:84
  96.0 9.3 %all-to-all-done.1 = bf16[8,64,256]{2,1,0:T(8,128)(2,1)S(1)} async-done(((bf16[8,64,256]{2,1,0:T(8,128)(2,1)}), bf16[8,64,256]{2,1,0:T(8,128)(2,1)S(1)}, u32[]{:S(2)}, u32[]{:S(2)}) %all-to-all-start.1) | async-done | bytes 262176 | tf_op jit(solution)/shard_map/all_to_all | solution.py:84
  105.3 14.2 %reduce-scatter.2.cloned.1.call-done = bf16[512,512]{1,0:T(8,128)(2,1)} async-done(((bf16[512,2048]{1,0:T(8,128)(2,1)}), bf16[512,512]{1,0:T(8,128)(2,1)}) %reduce-scatter.2.cloned.1.call-update) | async-done | bytes 524304 | tf_op jit(solution)/shard_map/reduce_scatter | solution.py:76
  119.5 2.0 %select_convert_fusion = bf16[512,512]{1,0:T(8,128)(2,1)} fusion(bf16[512,512]{1,0:T(8,128)(2,1)} %reduce-scatter.2.cloned.1.call-done, bf16[512,512]{1,0:T(8,128)(2,1)S(1)} %copy-done.2, pred[512]{0:T(512)(128)(4,1)S(1)} %iota_compare_fusion.3), kind=kLoop, calls=%fused_computation.25 | loop fusion | flops 1310720 | bytes 1573376 | tf_op jit(solution)/shard_map/convert_element_type | solution.py:80
  121.5 0.7 copy.29
  (37 shorter events, 3.1 us)
Async XLA Ops:
  7.2 77.9 %copy-start = (bf16[512,2048]{1,0:T(8,128)(2,1)S(1)}, bf16[512,2048]{1,0:T(8,128)(2,1)}, u32[]{:S(2)}) copy-start(bf16[512,2048]{1,0:T(8,128)(2,1)} %param.14) | copy-start | bytes 6291460
  7.2 50.5 %copy-start.4 = (f32[2048]{0:T(1024)S(1)}, f32[2048]{0:T(1024)}, u32[]{:S(2)}) copy-start(f32[2048]{0:T(1024)} %param.11) | copy-start | bytes 24580
  7.2 21.9 %all-gather.3.cloned.1.call-start = ((), (), s32[]{:S(2)}) async-start(), calls=%async_computation.3 | async-start | bytes 1310720 | tf_op jit(solution)/shard_map/all_gather | solution.py:37
  7.9 45.3 %all-gather.5.cloned.1.call-start = ((), (), s32[]{:S(2)}) async-start(), calls=%async_computation.4 | async-start | bytes 2621440 | tf_op jit(solution)/shard_map/all_gather | solution.py:30
  29.0 32.3 %all-to-all-start = ((bf16[8,256,256]{2,1,0:T(8,128)(2,1)}), bf16[8,256,256]{2,1,0:T(8,128)(2,1)S(1)}, u32[]{:S(2)}, u32[]{:S(2)}) async-start(bf16[8,256,256]{2,1,0:T(8,128)(2,1)} %all-gather.3.cloned.1.call-done), calls=%async_computation | async-start | bytes 2097152 | tf_op jit(solution)/shard_map/all_to_all | solution.py:38
  34.6 85.0 %reduce-scatter.2.cloned.1.call-start = ((), (), s32[]{:S(2)}) async-start(), calls=%async_computation.5 | async-start | bytes 2621440 | tf_op jit(solution)/shard_map/reduce_scatter | solution.py:76
  53.2 4.4 %copy-start.1 = (bf16[512,2048]{1,0:T(8,128)(2,1)S(1)}, bf16[512,2048]{1,0:T(8,128)(2,1)}, u32[]{:S(2)}) copy-start(bf16[512,2048]{1,0:T(8,128)(2,1)} %all-gather.5.cloned.1.call-done) | copy-start | bytes 6291460
  53.2 5.1 %copy-start.6 = (bf16[2048,256]{1,0:T(8,128)(2,1)S(1)}, bf16[2048,256]{1,0:T(8,128)(2,1)}, u32[]{:S(2)}) copy-start(bf16[2048,256]{1,0:T(8,128)(2,1)} %param.13) | copy-start | bytes 3145732
  57.6 1.6 %copy-start.5 = (bf16[2048,512]{1,0:T(8,128)(2,1)S(1)}, bf16[2048,512]{1,0:T(8,128)(2,1)}, u32[]{:S(2)}) copy-start(bf16[2048,512]{1,0:T(8,128)(2,1)} %param.12) | copy-start | bytes 6291460
  67.3 10.7 %copy-start.3 = (bf16[2048,256]{1,0:T(8,128)(2,1)S(1)}, bf16[2048,256]{1,0:T(8,128)(2,1)}, u32[]{:S(2)}) copy-start(bf16[2048,256]{1,0:T(8,128)(2,1)} %broadcast_select_fusion) | copy-start | bytes 3145732
  85.1 2.7 %copy-start.7 = (s32[1,8]{1,0:T(1,128)S(1)}, s32[1,8]{1,0:T(1,128)}, u32[]{:S(2)}) copy-start(s32[1,8]{1,0:T(1,128)} %param.18) | copy-start | bytes 100
  85.1 34.5 %copy-start.2 = (bf16[512,512]{1,0:T(8,128)(2,1)S(1)}, bf16[512,512]{1,0:T(8,128)(2,1)}, u32[]{:S(2)}) copy-start(bf16[512,512]{1,0:T(8,128)(2,1)} %param.10) | copy-start | bytes 1572868
  90.2 15.1 %all-to-all-start.1 = ((bf16[8,64,256]{2,1,0:T(8,128)(2,1)}), bf16[8,64,256]{2,1,0:T(8,128)(2,1)S(1)}, u32[]{:S(2)}, u32[]{:S(2)}) async-start(bf16[8,64,256]{2,1,0:T(8,128)(2,1)} %broadcast_select_fusion.1), calls=%async_computation.2 | async-start | bytes 524288 | tf_op jit(solution)/shard_map/all_to_all | solution.py:84
Sparse Core Ops, SparseCore 0:
  9.6 19.4 all-gather.2
  30.6 22.5 all-gather.4
  87.8 31.6 reduce-scatter.1
where the time goes:
time: 129 us
  waiting for transfers between devices  59.4 us (46%)
  matrix products  23.2 us (18%)
  between operations  15.2 us (12%)
  other arithmetic  13.9 us (11%)
  starting transfers between devices  11.4 us (9%)
  local copies, waits for them, and re-layouts  5.73 us (4%)
    all_gather x1, waiting for transfers between devices, body(): full_rows = lax.all_gather(tokens, 'tp', axis=1, tiled=True)  18.6 us
    all_gather x1, waiting for transfers between devices, body(): pooled = lax.all_gather(old_cache, 'tp', axis=1, tiled=True)  15.8 us
    reduce_scatter x1, waiting for transfers between devices, body(): lax.psum_scatter(partial_out.astype(jnp.bfloat16), 'tp', scatter_dimensio...  14.2 us
    sub x1, matrix products, body(): weights = jnp.exp(scores - top)  10.7 us
    all_to_all x1, waiting for transfers between devices, body(): lax.all_to_all(jnp.take(mine_part, sources, axis=0), 'seq', split_axis=0,...  9.32 us
    dot_general x1, matrix products, body(): jnp.einsum('htk,kd->thd', probs, values, preferred_element_type=jnp.float32)  7.05 us
    all_to_all x1, starting transfers between devices, body(): lax.all_to_all(jnp.take(mine_part, sources, axis=0), 'seq', split_axis=0,...  5.73 us
    all_to_all x1, starting transfers between devices, body(): lax.all_to_all(pooled, 'seq', split_axis=0, concat_axis=0, tiled=True)  5.51 us
  transfers between devices with their start and end apart: 5, of which 4 were waited for; matrix products, arithmetic and copies ran while one was open for 11% of the time, Pallas kernels for 0%

commit v1 on v0

v1 whole, which is shorter than its diff:
```python
import functools
import math

import jax
import jax.numpy as jnp
from jax import lax
from jax.experimental import pallas as pl
from jax.experimental.pallas import tpu as pltpu
from jax.sharding import PartitionSpec as P

EPSILON = 1e-05
MASKED = -1e30
CHUNKS = 2
ROW_TILE = 128
NORM_ROWS = 64
F32 = jnp.float32
BF16 = jnp.bfloat16

VMEM = pl.BlockSpec(memory_space=pltpu.VMEM)
SMEM = pl.BlockSpec(memory_space=pltpu.SMEM)


def dot(a, b):
    return lax.dot_general(a, b, (((1,), (0,)), ((), ())), preferred_element_type=F32)


def dot_t(a, b):
    return lax.dot_general(a, b, (((1,), (1,)), ((), ())), preferred_element_type=F32)


def order_kernel(share, table_ref, arrived_ref, out_ref):
    rows, count = out_ref.shape[0], arrived_ref.shape[0]
    row = lax.broadcasted_iota(jnp.int32, (rows, 128), 0)
    block = row // share
    holder = jnp.zeros_like(block)
    for b in range(rows // share):
        holder = jnp.where(block == b, table_ref[0, b], holder)
    index = (holder * share + row % share)[:, :1]
    column = lax.broadcasted_iota(jnp.int32, (rows, count), 1)
    pick = jnp.where(column == index, 1.0, 0.0).astype(BF16)
    out_ref[...] = dot(pick, arrived_ref[...]).astype(BF16)


def extend_kernel(share, block_rows, old_ref, new_ref, held_ref, span_ref, arrived_ref, *refs):
    kv_refs, out_ref = refs[:-1], refs[-1]
    rows = arrived_ref.shape[0]
    groups = rows // share
    held, span = held_ref[0], span_ref[0]
    row = lax.broadcasted_iota(jnp.int32, (rows, 128), 0)
    target = row // share
    block, holder = jnp.zeros_like(row), jnp.zeros_like(row)
    for b in range(groups):
        hit = target == new_ref[0, b]
        block = jnp.where(hit, b, block)
        holder = jnp.where(hit, old_ref[0, b], holder)
    position = block * block_rows + lax.axis_index("tp") * share + row % share
    old_row = jnp.where(position < held, holder * share + row % share, -1)[:, :1]
    fresh = position - held
    new_row = jnp.where((fresh >= 0) & (fresh < span), fresh, -1)[:, :1]
    column = lax.broadcasted_iota(jnp.int32, (rows, rows), 1)
    total = dot(jnp.where(column == old_row, 1.0, 0.0).astype(BF16), arrived_ref[...])
    at = 0
    for kv_ref in kv_refs:
        count = kv_ref.shape[0]
        column = lax.broadcasted_iota(jnp.int32, (rows, count), 1) + at
        total += dot(jnp.where(column == new_row, 1.0, 0.0).astype(BF16), kv_ref[...])
        at += count
    out_ref[...] = total.astype(BF16)


def project_kernel(x0, x1, x2, x3, gain_ref, wq_ref, wkv_ref, q_ref, kv_ref, normed):
    pieces = (x0, x1, x2, x3)
    me = lax.axis_index("tp")
    rows, width = x0.shape
    features = width * len(pieces)

    def norm(step, carry):
        at = pl.ds(pl.multiple_of(step * NORM_ROWS, NORM_ROWS), NORM_ROWS)
        values = [piece[at, :].astype(F32) for piece in pieces]
        average = sum(jnp.sum(v, axis=1, keepdims=True) for v in values) / features
        centred = [v - average for v in values]
        spread = sum(jnp.sum(v * v, axis=1, keepdims=True) for v in centred) / features
        scale = lax.rsqrt(spread + EPSILON)
        for j, v in enumerate(centred):
            normed[j, at, :] = (v * scale * gain_ref[me ^ j]).astype(BF16)
        return carry

    lax.fori_loop(0, rows // NORM_ROWS, norm, 0)
    q_ref[...] = sum(dot(normed[j], wq_ref[me ^ j]) for j in range(len(pieces))).astype(BF16)
    kv_ref[...] = sum(dot(normed[j], wkv_ref[me ^ j]) for j in range(len(pieces))).astype(BF16)


def attend_kernel(share, block_rows, held_ref, q_ref, c0, c1, c2, c3, wout_ref, *refs):
    kv_refs, (far_ref, near_ref, keys, values, context) = refs[:-5], refs[-5:]
    pieces = (c0, c1, c2, c3)
    me = lax.axis_index("tp")
    held = held_ref[0]
    rows = q_ref.shape[0]
    piece_rows, width = c0.shape
    hd = width // 2
    heads = q_ref.shape[1] // hd
    cached = piece_rows * len(pieces)
    before = sum(ref.shape[0] for ref in kv_refs) - rows
    ones = jnp.ones((piece_rows, hd), BF16)

    spare = kv_refs[0][0:1, :hd]
    row = lax.broadcasted_iota(jnp.int32, (piece_rows, hd), 0)
    place = row // share * block_rows + row % share
    for j, piece in enumerate(pieces):
        at = pl.ds(j * piece_rows, piece_rows)
        used = place + (me ^ j) * share < held
        keys[at, :] = jnp.where(used, piece[:, :hd].astype(F32), spare.astype(F32)).astype(BF16)
        values[at, hd:] = jnp.where(used, piece[:, hd:].astype(F32), 0.0).astype(BF16)
        values[at, :hd] = jnp.where(used, 1.0, 0.0).astype(BF16)
    top = cached
    for ref in kv_refs:
        at = pl.ds(top, ref.shape[0])
        keys[at, :] = ref[:, :hd]
        values[at, hd:] = ref[:, hd:]
        values[at, :hd] = ones[:1].astype(F32).astype(BF16) * jnp.ones((ref.shape[0], hd), BF16)
        top += ref.shape[0]

    factor = hd ** (-0.5) * math.log2(math.e)
    tile = min(ROW_TILE, rows)
    for start in range(0, rows, tile):
        stop = cached + before + start
        q4 = jnp.concatenate(
            [q_ref[pl.ds(start, tile), h * hd : (h + 1) * hd] for h in range(heads)], axis=0
        )
        done = dot_t(q4, keys[pl.ds(0, stop), :])
        last = dot_t(q4, keys[pl.ds(stop, tile), :])
        own = lax.broadcasted_iota(jnp.int32, (heads * tile, tile), 0) % tile
        other = lax.broadcasted_iota(jnp.int32, (heads * tile, tile), 1)
        last = jnp.where(other <= own, last, MASKED)
        high = jnp.maximum(
            jnp.max(done, axis=1, keepdims=True), jnp.max(last, axis=1, keepdims=True)
        )
        p_done = jnp.exp2((done - high) * factor).astype(BF16)
        p_last = jnp.exp2((last - high) * factor).astype(BF16)
        both = dot(p_done, values[pl.ds(0, stop), :]) + dot(p_last, values[pl.ds(stop, tile), :])
        out = (both[:, hd:] / both[:, :hd]).astype(BF16)
        for h in range(heads):
            context[pl.ds(start, tile), h * hd : (h + 1) * hd] = out[h * tile : (h + 1) * tile]

    share_cols = wout_ref.shape[1] // 4
    for k in range(4):
        columns = pl.ds(pl.multiple_of((me ^ k) * share_cols, share_cols), share_cols)
        part = dot(context[...], wout_ref[:, columns]).astype(BF16)
        if k & 1:
            far_ref[k >> 1] = part
        else:
            near_ref[k >> 1] = part


def call(kernel, out_shape, in_specs, args, flops, scratch=(), exps=0, name=None):
    outs = out_shape if isinstance(out_shape, (list, tuple)) else [out_shape]
    moved = sum(a.size * a.dtype.itemsize for a in list(args) + list(outs))
    return pl.pallas_call(
        kernel,
        out_shape=out_shape,
        in_specs=in_specs,
        out_specs=jax.tree.map(lambda _: VMEM, out_shape),
        scratch_shapes=list(scratch),
        cost_estimate=pl.CostEstimate(flops=flops, bytes_accessed=moved, transcendentals=exps),
        compiler_params=pltpu.CompilerParams(vmem_limit_bytes=32 * 1024 * 1024),
        name=name,
    )(*args)


def body(
    tokens,
    norm_gain,
    w_query,
    w_keyval,
    w_out,
    span_lens,
    cached_lens,
    old_table,
    new_table,
    old_cache,
):
    tp = lax.axis_size("tp")
    groups, share, width = old_cache.shape
    block_rows = share * tp
    capacity = groups * block_rows
    rows, cols = tokens.shape
    q_cols = w_query.shape[1]
    features = w_query.shape[0]
    hd = width // 2
    most_held = capacity - rows
    piece_rows = most_held // tp

    def swap(x, bit):
        return lax.ppermute(x, "tp", [(i, i ^ bit) for i in range(tp)])

    with jax.named_scope("tokens_gather"):
        part = rows // CHUNKS
        own = [tokens[c * part : (c + 1) * part] for c in range(CHUNKS)]
        across = [swap(x, 2) for x in own]
        beside = [swap(x, 1) for x in own]
        corner = [swap(x, 1) for x in across]

    with jax.named_scope("cache_gather"):
        arrived = lax.all_to_all(old_cache, "seq", split_axis=0, concat_axis=0, tiled=True)
        arrived = arrived.reshape(groups * share, width)
        ordered = call(
            functools.partial(order_kernel, share),
            jax.ShapeDtypeStruct((piece_rows, width), BF16),
            [SMEM, VMEM],
            (old_table, arrived),
            flops=2 * piece_rows * groups * share * width,
            name="order",
        )
        c_across = swap(ordered, 2)
        cached = (ordered, swap(ordered, 1), c_across, swap(c_across, 1))

    gain = norm_gain.reshape(tp, 1, cols)
    wq = w_query.reshape(tp, cols, q_cols)
    wkv = w_keyval.reshape(tp, cols, width)
    queries, keyvals = [], []
    with jax.named_scope("project"):
        for c in range(CHUNKS):
            q, kv = call(
                project_kernel,
                [
                    jax.ShapeDtypeStruct((part, q_cols), BF16),
                    jax.ShapeDtypeStruct((part, width), BF16),
                ],
                [VMEM] * 7,
                (own[c], beside[c], across[c], corner[c], gain, wq, wkv),
                flops=2 * part * features * (q_cols + width),
                scratch=[pltpu.VMEM((tp, part, cols), BF16)],
                name="project",
            )
            queries.append(q)
            keyvals.append(kv)

    with jax.named_scope("extend"):
        sent = call(
            functools.partial(extend_kernel, share, block_rows),
            jax.ShapeDtypeStruct((groups * share, width), BF16),
            [SMEM] * 4 + [VMEM] * (1 + CHUNKS),
            (old_table, new_table, cached_lens, span_lens, arrived, *keyvals),
            flops=4 * groups * share * groups * share * width,
            name="extend",
        )
        new_cache = lax.all_to_all(
            sent.reshape(groups, share, width), "seq", split_axis=0, concat_axis=0, tiled=True
        )

    mixed = []
    for c in range(CHUNKS):
        with jax.named_scope("attend"):
            seen = most_held + (c + 1) * part
            far, near = call(
                functools.partial(attend_kernel, share, block_rows),
                [jax.ShapeDtypeStruct((2, part, cols), BF16)] * 2,
                [SMEM] + [VMEM] * (6 + c + 1),
                (cached_lens, queries[c], *cached, w_out, *keyvals[: c + 1]),
                flops=4 * part * seen * q_cols + 2 * part * q_cols * features,
                exps=part * seen * (q_cols // hd),
                scratch=[
                    pltpu.VMEM((seen, hd), BF16),
                    pltpu.VMEM((seen, width), BF16),
                    pltpu.VMEM((part, q_cols), BF16),
                ],
                name="attend",
            )
        with jax.named_scope("reduce"):
            got = swap(far[1], 1)
            pair = (near[1].astype(F32) + got.astype(F32)).astype(BF16)
            crossed = swap(pair, 2)
            kept = near[0].astype(F32) + swap(far[0], 1).astype(F32)
            total = own[c].astype(F32) + (kept + crossed.astype(F32))
            row = lax.broadcasted_iota(jnp.int32, (part, 1), 0) + c * part
            mixed.append(jnp.where(row < span_lens[0], total, 0.0).astype(BF16))
    return (jnp.concatenate(mixed, axis=0), new_cache)


def solution(mesh):
    in_specs = (
        P("seq", "tp"),
        P(),
        P(None, "tp"),
        P(),
        P("tp", None),
        P("seq"),
        P("seq"),
        P("seq", None),
        P("seq", None),
        P("seq", "tp", None),
    )
    out_specs = (P("seq", "tp"), P("seq", "tp", None))
    return jax.shard_map(body, mesh=mesh, in_specs=in_specs, out_specs=out_specs, check_vma=False)
```

time: 129 us -> 71.2 us (0.55)
  waiting for transfers between devices: 59.4 us -> 24.2 us
  matrix products: 23.2 us -> 0 us
  Pallas kernels: 0 us -> 16.1 us
  between operations: 15.2 us -> 2.11 us
  other arithmetic: 13.9 us -> 1.27 us
  starting transfers between devices: 11.4 us -> 21 us
    all_gather x2 -> x0, waiting for transfers between devices: 34.5 us -> none  [the longest x1 18.6 us: body(): full_rows = lax.all_gather(tokens, 'tp', axis=1, tiled=True)]
    ppermute x0 -> x15, waiting for transfers between devices: none -> 17.4 us  [swap(): return lax.ppermute(x, 'tp', [(i, i ^ bit) for i in range(tp)])]
    pallas_call x0 -> x6, Pallas kernels: none -> 16.1 us  [call(): pl.pallas_call(kernel, out_shape=out_shape, in_specs=in_specs, out_specs=...]
    reduce_scatter x1 -> x0, waiting for transfers between devices: 14.2 us -> none  [body(): lax.psum_scatter(partial_out.astype(jnp.bfloat16), 'tp', scatter_dimensio...]
    dot_general x4 -> x0, matrix products: 12.5 us -> none  [the longest x1 7.05 us: body(): jnp.einsum('htk,kd->thd', probs, values, preferred_element_type=jnp.float32)]
    sub x1 -> x0, matrix products: 10.7 us -> none  [body(): weights = jnp.exp(scores - top)]
    ppermute x0 -> x15, starting transfers between devices: none -> 7.6 us  [swap(): return lax.ppermute(x, 'tp', [(i, i ^ bit) for i in range(tp)])]
    reduce_sum x3 -> x0, other arithmetic: 4.48 us -> none  [the longest x1 2.27 us: normalize(): spread = jnp.mean(centred * centred, axis=1, keepdims=True)]
  transfers between devices with their start and end apart: 5 -> 17, of which waited for: 4 -> 6; matrix products, arithmetic and copies ran while one was open for 11% -> 3% of each run, Pallas kernels for 0% -> 17%
where the time goes in v1:
time: 71.2 us; the launch traced here: 70.8 us
  waiting for transfers between devices  24.2 us (34%)
  starting transfers between devices  21 us (29%)
  Pallas kernels  16.1 us (23%)
  local copies, waits for them, and re-layouts  6.21 us (9%)
  between operations  2.11 us (3%)
  other arithmetic  1.27 us (2%)
    ppermute x15, waiting for transfers between devices, swap(): return lax.ppermute(x, 'tp', [(i, i ^ bit) for i in range(tp)])  17.4 us
    pallas_call x6, Pallas kernels, call(): pl.pallas_call(kernel, out_shape=out_shape, in_specs=in_specs, out_specs=...  16.1 us
    ppermute x15, starting transfers between devices, swap(): return lax.ppermute(x, 'tp', [(i, i ^ bit) for i in range(tp)])  7.6 us
    all_to_all x1, starting transfers between devices, body(): lax.all_to_all(old_cache, 'seq', split_axis=0, concat_axis=0, tiled=True)  7.4 us
    all_to_all x1, waiting for transfers between devices, body(): lax.all_to_all(sent.reshape(groups, share, width), 'seq', split_axis=0, c...  6.76 us
    all_to_all x1, starting transfers between devices, body(): lax.all_to_all(sent.reshape(groups, share, width), 'seq', split_axis=0, c...  6.01 us
    unnamed x19, local copies, waits for them, and re-layouts  3.67 us
    squeeze x2, local copies, waits for them, and re-layouts, body(): kept = near[0].astype(F32) + swap(far[0], 1).astype(F32)  1.48 us
  transfers between devices with their start and end apart: 17, of which 6 were waited for; matrix products, arithmetic and copies ran while one was open for 3% of the time, Pallas kernels for 17%

profile of v1, /device:TPU:0, one launch (start us, length us, event | category | flops | bytes accessed | tf_op | source)
XLA Modules:
  0.0 70.8 jit_solution(11991725777877739198)
XLA Ops:
  0.6 7.4 %all-to-all-start = ((bf16[8,64,256]{2,1,0:T(8,128)(2,1)}), bf16[8,64,256]{2,1,0:T(8,128)(2,1)S(1)}, u32[]{:S(2)}, u32[]{:S(2)}) async-start(bf16[8,64,256]{2,1,0:T(8,128)(2,1)} %param.19), calls=%async_computation | async-start | bytes 524288 | tf_op jit(solution)/shard_map/cache_gather/all_to_all | solution.py:204
  8.0 1.1 %fusion.10 = (bf16[256,512]{1,0:T(8,128)(2,1)S(1)}, bf16[256,512]{1,0:T(8,128)(2,1)S(1)}) fusion(bf16[512,512]{1,0:T(8,128)(2,1)} %param.10), kind=kLoop, calls=%fused_computation.21 | loop fusion | bytes 1048576 | tf_op jit(solution)/shard_map/tokens_gather/slice | solution.py:198
  9.1 1.6 %collective-permute-start.1 = (bf16[256,512]{1,0:T(8,128)(2,1)S(1)}, bf16[256,512]{1,0:T(8,128)(2,1)S(1)}, u32[]{:S(2)}, u32[]{:S(2)}) collective-permute-start(bf16[256,512]{1,0:T(8,128)(2,1)S(1)} %get-tuple-element.24.x0), channel_id=1, source_target_pairs={{0,2},{1,3},{2,0},{3,1},{4,6},{5,7},{6,4},{7,5},{8,10},{9,11},{10,... | collective-permute-start | bytes 786440 | tf_op jit(solution)/shard_map/tokens_gather/ppermute | solution.py:194
  11.2 7.2 %collective-permute-done.1.x2 = bf16[256,512]{1,0:T(8,128)(2,1)S(1)} collective-permute-done((bf16[256,512]{1,0:T(8,128)(2,1)S(1)}, bf16[256,512]{1,0:T(8,128)(2,1)S(1)}, u32[]{:S(2)}, u32[]{:S(2)}) %collective-permute-start.1) | collective-permute-done | bytes 262176 | tf_op jit(solution)/shard_map/tokens_gather/ppermute | solution.py:194
  18.4 0.7 copy-done.4
  19.1 0.8 %order.1.c0 = bf16[384,256]{1,0:T(8,128)(2,1)S(1)} custom-call(s32[1,8]{1,0:T(1,128)S(1)} %copy-done.4, bf16[512,256]{1,0:T(8,128)(2,1)S(1)} %bitcast.31), custom_call_target="tpu_custom_call" | custom-call | flops 100663296 | bytes 458784 | tf_op jit(solution)/shard_map/cache_gather/order/pallas_call | solution.py:158
  19.9 1.6 %collective-permute-start.4 = (bf16[384,256]{1,0:T(8,128)(2,1)S(1)}, bf16[384,256]{1,0:T(8,128)(2,1)S(1)}, u32[]{:S(2)}, u32[]{:S(2)}) collective-permute-start(bf16[384,256]{1,0:T(8,128)(2,1)S(1)} %order.1.c0), channel_id=1, source_target_pairs={{0,2},{1,3},{2,0},{3,1},{4,6},{5,7},{6,4},{7,5},{8,10},{9,11},{10,... | collective-permute-start | bytes 589832 | tf_op jit(solution)/shard_map/cache_gather/ppermute | solution.py:194
  21.7 0.9 %collective-permute-done.10.x2 = bf16[256,512]{1,0:T(8,128)(2,1)S(1)} collective-permute-done((bf16[256,512]{1,0:T(8,128)(2,1)S(1)}, bf16[256,512]{1,0:T(8,128)(2,1)S(1)}, u32[]{:S(2)}, u32[]{:S(2)}) %collective-permute-start.10) | collective-permute-done | bytes 262176 | tf_op jit(solution)/shard_map/tokens_gather/ppermute | solution.py:194
  23.1 4.2 %collective-permute-done.4.c2 = bf16[384,256]{1,0:T(8,128)(2,1)S(1)} collective-permute-done((bf16[384,256]{1,0:T(8,128)(2,1)S(1)}, bf16[384,256]{1,0:T(8,128)(2,1)S(1)}, u32[]{:S(2)}, u32[]{:S(2)}) %collective-permute-start.4) | collective-permute-done | bytes 196640 | tf_op jit(solution)/shard_map/cache_gather/ppermute | solution.py:194
  28.6 1.6 %copy-done = bf16[2048,512]{1,0:T(8,128)(2,1)S(1)} copy-done((bf16[2048,512]{1,0:T(8,128)(2,1)S(1)}, bf16[2048,512]{1,0:T(8,128)(2,1)}, u32[]{:S(2)}) %copy-start) | copy-done | bytes 2097176
  30.2 0.7 copy-done.3
  30.9 2.2 %project.2 = (bf16[256,512]{1,0:T(8,128)(2,1)S(1)}, bf16[256,256]{1,0:T(8,128)(2,1)S(1)}) custom-call(bf16[256,512]{1,0:T(8,128)(2,1)S(1)} %get-tuple-element.24.x0, bf16[256,512]{1,0:T(8,128)(2,1)S(1)} %collective-permute-done.x1, bf16[256,512]{1,0:T(8,128)(2,1)S(1)} %collective-permute-done.1.x2, bf16[256,512]{1,0:T(8,128)(2,1)S(1)} %collective-permute-done.2.x3, ...), custom_call_target="tpu_custom_call" | custom-call | flops 805306368 | bytes 4595712 | tf_op jit(solution)/shard_map/project/project/pallas_call | solution.py:158
  33.1 2.2 %project.3 = (bf16[256,512]{1,0:T(8,128)(2,1)S(1)}, bf16[256,256]{1,0:T(8,128)(2,1)S(1)}) custom-call(bf16[256,512]{1,0:T(8,128)(2,1)S(1)} %get-tuple-element.25.x0, bf16[256,512]{1,0:T(8,128)(2,1)S(1)} %collective-permute-done.9.x1, bf16[256,512]{1,0:T(8,128)(2,1)S(1)} %collective-permute-done.10.x2, bf16[256,512]{1,0:T(8,128)(2,1)S(1)} %collective-permute-done.11.x3, ...), custom_call_target="tpu_custom_call" | custom-call | flops 805306368 | bytes 4595712 | tf_op jit(solution)/shard_map/project/project/pallas_call | solution.py:158
  35.3 4.2 %attend.2 = (bf16[2,256,512]{2,1,0:T(8,128)(2,1)S(1)}, bf16[2,256,512]{2,1,0:T(8,128)(2,1)S(1)}) custom-call(s32[1]{0:T(128)S(6)} %copy.14.held_ref, bf16[256,512]{1,0:T(8,128)(2,1)S(1)} %get-tuple-element.10.q_ref, bf16[384,256]{1,0:T(8,128)(2,1)S(1)} %order.1.c0, bf16[384,256]{1,0:T(8,128)(2,1)S(1)} %collective-permute-done.3.c1, ...), custom_call_target="tpu_custom_call" | custom-call | flops 1476395008 | bytes 4325380 | tf_op jit(solution)/shard_map/attend/attend/pallas_call | solution.py:158
  39.6 0.7 %slice_bitcast_fusion.3 = (bf16[256,512]{1,0:T(8,128)(2,1)}, bf16[256,512]{1,0:T(8,128)(2,1)S(1)}) fusion(bf16[2,256,512]{2,1,0:T(8,128)(2,1)S(1)} %get-tuple-element.13), kind=kLoop, calls=%fused_computation.18 | loop fusion | bytes 1048576 | tf_op jit(solution)/shard_map/reduce/squeeze | solution.py:273
  40.8 4.7 %attend.3 = (bf16[2,256,512]{2,1,0:T(8,128)(2,1)S(1)}, bf16[2,256,512]{2,1,0:T(8,128)(2,1)S(1)}) custom-call(s32[1]{0:T(128)S(6)} %copy.14.held_ref, bf16[256,512]{1,0:T(8,128)(2,1)S(1)} %get-tuple-element.14.q_ref, bf16[384,256]{1,0:T(8,128)(2,1)S(1)} %order.1.c0, bf16[384,256]{1,0:T(8,128)(2,1)S(1)} %collective-permute-done.3.c1, ...), custom_call_target="tpu_custom_call" | custom-call | flops 1610612736 | bytes 4456452 | tf_op jit(solution)/shard_map/attend/attend/pallas_call | solution.py:158
  45.6 0.7 %slice_bitcast_fusion.1 = (bf16[256,512]{1,0:T(8,128)(2,1)}, bf16[256,512]{1,0:T(8,128)(2,1)S(1)}) fusion(bf16[2,256,512]{2,1,0:T(8,128)(2,1)S(1)} %get-tuple-element.17), kind=kLoop, calls=%fused_computation.16 | loop fusion | bytes 1048576 | tf_op jit(solution)/shard_map/reduce/squeeze | solution.py:273
  46.3 1.9 %extend.1 = bf16[512,256]{1,0:T(8,128)(2,1)} custom-call(s32[1,8]{1,0:T(1,128)S(1)} %copy-done.5, s32[1,8]{1,0:T(1,128)S(1)} %copy-done.7, s32[1]{0:T(128)S(6)} %copy.14.held_ref, s32[1]{0:T(128)} %copy.13.span_ref, bf16[512,256]{1,0:T(8,128)(2,1)S(1)} %bitcast.32, bf16[256,256]{1,0:T(8,128)(2,1)S(1)} %get-tuple-element.11.refs_0_, ...), custom_call_target="tpu_custom_call" | custom-call | flops 268435456 | bytes 786504 | tf_op jit(solution)/shard_map/extend/extend/pallas_call | solution.py:158
  48.2 6.0 %all-to-all-start.1 = ((bf16[8,64,256]{2,1,0:T(8,128)(2,1)}), bf16[8,64,256]{2,1,0:T(8,128)(2,1)S(1)}, u32[]{:S(2)}, u32[]{:S(2)}) async-start(bf16[8,64,256]{2,1,0:T(8,128)(2,1)} %bitcast.13), calls=%async_computation.1 | async-start | bytes 524288 | tf_op jit(solution)/shard_map/extend/all_to_all | solution.py:247
  54.8 1.6 %collective-permute-start.8 = (bf16[256,512]{1,0:T(8,128)(2,1)S(1)}, bf16[256,512]{1,0:T(8,128)(2,1)S(1)}, u32[]{:S(2)}, u32[]{:S(2)}) collective-permute-start(bf16[256,512]{1,0:T(8,128)(2,1)S(1)} %fusion.5), channel_id=1, source_target_pairs={{0,2},{1,3},{2,0},{3,1},{4,6},{5,7},{6,4},{7,5},{8,10},{9,11},{10,... | collective-permute-start | bytes 786440 | tf_op jit(solution)/shard_map/reduce/ppermute | solution.py:194
  57.1 6.8 %all-to-all-done.1 = bf16[8,64,256]{2,1,0:T(8,128)(2,1)S(1)} async-done(((bf16[8,64,256]{2,1,0:T(8,128)(2,1)}), bf16[8,64,256]{2,1,0:T(8,128)(2,1)S(1)}, u32[]{:S(2)}, u32[]{:S(2)}) %all-to-all-start.1) | async-done | bytes 262176 | tf_op jit(solution)/shard_map/extend/all_to_all | solution.py:247
  64.0 4.9 %collective-permute-done.14 = bf16[256,512]{1,0:T(8,128)(2,1)S(1)} collective-permute-done((bf16[256,512]{1,0:T(8,128)(2,1)S(1)}, bf16[256,512]{1,0:T(8,128)(2,1)S(1)}, u32[]{:S(2)}, u32[]{:S(2)}) %collective-permute-start.14) | collective-permute-done | bytes 262176 | tf_op jit(solution)/shard_map/reduce/ppermute | solution.py:194
  69.3 0.8 %pad_maximum_fusion = bf16[512,512]{1,0:T(8,128)(2,1)} fusion(bf16[256,512]{1,0:T(8,128)(2,1)S(1)} %get-tuple-element.19, bf16[256,512]{1,0:T(8,128)(2,1)S(1)} %get-tuple-element.18), kind=kLoop, calls=%fused_computation | loop fusion | flops 1048576 | bytes 1048576 | tf_op jit(solution)/shard_map/concatenate | solution.py:277
  70.1 0.7 copy.15
  (43 shorter events, 3.5 us)
Async XLA Ops:
  0.6 27.9 %copy-start.2 = (bf16[2048,256]{1,0:T(8,128)(2,1)S(1)}, bf16[2048,256]{1,0:T(8,128)(2,1)}, u32[]{:S(2)}) copy-start(bf16[2048,256]{1,0:T(8,128)(2,1)} %param.13) | copy-start | bytes 3145732
  0.6 17.8 %all-to-all-start = ((bf16[8,64,256]{2,1,0:T(8,128)(2,1)}), bf16[8,64,256]{2,1,0:T(8,128)(2,1)S(1)}, u32[]{:S(2)}, u32[]{:S(2)}) async-start(bf16[8,64,256]{2,1,0:T(8,128)(2,1)} %param.19), calls=%async_computation | async-start | bytes 524288 | tf_op jit(solution)/shard_map/cache_gather/all_to_all | solution.py:204
  9.1 9.3 %collective-permute-start.1 = (bf16[256,512]{1,0:T(8,128)(2,1)S(1)}, bf16[256,512]{1,0:T(8,128)(2,1)S(1)}, u32[]{:S(2)}, u32[]{:S(2)}) collective-permute-start(bf16[256,512]{1,0:T(8,128)(2,1)S(1)} %get-tuple-element.24.x0), channel_id=1, source_target_pairs={{0,2},{1,3},{2,0},{3,1},{4,6},{5,7},{6,4},{7,5},{8,10},{9,11},{10,... | collective-permute-start | bytes 786440 | tf_op jit(solution)/shard_map/tokens_gather/ppermute | solution.py:194
  10.7 11.9 %collective-permute-start.10 = (bf16[256,512]{1,0:T(8,128)(2,1)S(1)}, bf16[256,512]{1,0:T(8,128)(2,1)S(1)}, u32[]{:S(2)}, u32[]{:S(2)}) collective-permute-start(bf16[256,512]{1,0:T(8,128)(2,1)S(1)} %get-tuple-element.25.x0), channel_id=1, source_target_pairs={{0,2},{1,3},{2,0},{3,1},{4,6},{5,7},{6,4},{7,5},{8,10},{9,11},{10,... | collective-permute-start | bytes 786440 | tf_op jit(solution)/shard_map/tokens_gather/ppermute | solution.py:194
  11.2 11.4 %collective-permute-start = (bf16[256,512]{1,0:T(8,128)(2,1)S(1)}, bf16[256,512]{1,0:T(8,128)(2,1)S(1)}, u32[]{:S(2)}, u32[]{:S(2)}) collective-permute-start(bf16[256,512]{1,0:T(8,128)(2,1)S(1)} %get-tuple-element.24.x0), channel_id=1, source_target_pairs={{0,1},{1,0},{2,3},{3,2},{4,5},{5,4},{6,7},{7,6},{8,9},{9,8},{10,11... | collective-permute-start | bytes 786440 | tf_op jit(solution)/shard_map/tokens_gather/ppermute | solution.py:194
  18.4 10.2 %collective-permute-start.2 = (bf16[256,512]{1,0:T(8,128)(2,1)S(1)}, bf16[256,512]{1,0:T(8,128)(2,1)S(1)}, u32[]{:S(2)}, u32[]{:S(2)}) collective-permute-start(bf16[256,512]{1,0:T(8,128)(2,1)S(1)} %collective-permute-done.1.x2), channel_id=1, source_target_pairs={{0,1},{1,0},{2,3},{3,2},{4,5},{5,4},{6,7},{7,6},{8,9},{9,8},{10,11... | collective-permute-start | bytes 786440 | tf_op jit(solution)/shard_map/tokens_gather/ppermute | solution.py:194
  19.9 7.4 %collective-permute-start.4 = (bf16[384,256]{1,0:T(8,128)(2,1)S(1)}, bf16[384,256]{1,0:T(8,128)(2,1)S(1)}, u32[]{:S(2)}, u32[]{:S(2)}) collective-permute-start(bf16[384,256]{1,0:T(8,128)(2,1)S(1)} %order.1.c0), channel_id=1, source_target_pairs={{0,2},{1,3},{2,0},{3,1},{4,6},{5,7},{6,4},{7,5},{8,10},{9,11},{10,... | collective-permute-start | bytes 589832 | tf_op jit(solution)/shard_map/cache_gather/ppermute | solution.py:194
  21.5 11.6 %collective-permute-start.9 = (bf16[256,512]{1,0:T(8,128)(2,1)S(1)}, bf16[256,512]{1,0:T(8,128)(2,1)S(1)}, u32[]{:S(2)}, u32[]{:S(2)}) collective-permute-start(bf16[256,512]{1,0:T(8,128)(2,1)S(1)} %get-tuple-element.25.x0), channel_id=1, source_target_pairs={{0,1},{1,0},{2,3},{3,2},{4,5},{5,4},{6,7},{7,6},{8,9},{9,8},{10,11... | collective-permute-start | bytes 786440 | tf_op jit(solution)/shard_map/tokens_gather/ppermute | solution.py:194
  22.6 10.5 %collective-permute-start.11 = (bf16[256,512]{1,0:T(8,128)(2,1)S(1)}, bf16[256,512]{1,0:T(8,128)(2,1)S(1)}, u32[]{:S(2)}, u32[]{:S(2)}) collective-permute-start(bf16[256,512]{1,0:T(8,128)(2,1)S(1)} %collective-permute-done.10.x2), channel_id=1, source_target_pairs={{0,1},{1,0},{2,3},{3,2},{4,5},{5,4},{6,7},{7,6},{8,9},{9,8},{10,11... | collective-permute-start | bytes 786440 | tf_op jit(solution)/shard_map/tokens_gather/ppermute | solution.py:194
  22.6 12.8 %collective-permute-start.3 = (bf16[384,256]{1,0:T(8,128)(2,1)S(1)}, bf16[384,256]{1,0:T(8,128)(2,1)S(1)}, u32[]{:S(2)}, u32[]{:S(2)}) collective-permute-start(bf16[384,256]{1,0:T(8,128)(2,1)S(1)} %order.1.c0), channel_id=1, source_target_pairs={{0,1},{1,0},{2,3},{3,2},{4,5},{5,4},{6,7},{7,6},{8,9},{9,8},{10,11... | collective-permute-start | bytes 589832 | tf_op jit(solution)/shard_map/cache_gather/ppermute | solution.py:194
  27.3 8.1 %collective-permute-start.5 = (bf16[384,256]{1,0:T(8,128)(2,1)S(1)}, bf16[384,256]{1,0:T(8,128)(2,1)S(1)}, u32[]{:S(2)}, u32[]{:S(2)}) collective-permute-start(bf16[384,256]{1,0:T(8,128)(2,1)S(1)} %collective-permute-done.4.c2), channel_id=1, source_target_pairs={{0,1},{1,0},{2,3},{3,2},{4,5},{5,4},{6,7},{7,6},{8,9},{9,8},{10,11... | collective-permute-start | bytes 589832 | tf_op jit(solution)/shard_map/cache_gather/ppermute | solution.py:194
  28.6 1.6 %copy-start = (bf16[2048,512]{1,0:T(8,128)(2,1)S(1)}, bf16[2048,512]{1,0:T(8,128)(2,1)}, u32[]{:S(2)}) copy-start(bf16[2048,512]{1,0:T(8,128)(2,1)} %param.12) | copy-start | bytes 6291460
  30.9 2.2 %copy-start.1 = (bf16[2048,512]{1,0:T(8,128)(2,1)S(1)}, bf16[2048,512]{1,0:T(8,128)(2,1)}, u32[]{:S(2)}) copy-start(bf16[2048,512]{1,0:T(8,128)(2,1)} %param.12) | copy-start | bytes 6291460
  33.1 2.3 %copy-start.6 = (bf16[512,2048]{1,0:T(8,128)(2,1)S(1)}, bf16[512,2048]{1,0:T(8,128)(2,1)}, u32[]{:S(2)}) copy-start(bf16[512,2048]{1,0:T(8,128)(2,1)} %wout_ref.3) | copy-start | bytes 6291460
  40.3 14.5 %collective-permute-start.7 = (bf16[256,512]{1,0:T(8,128)(2,1)S(1)}, bf16[256,512]{1,0:T(8,128)(2,1)S(1)}, u32[]{:S(2)}, u32[]{:S(2)}) collective-permute-start(bf16[256,512]{1,0:T(8,128)(2,1)S(1)} %get-tuple-element.21), channel_id=1, source_target_pairs={{0,1},{1,0},{2,3},{3,2},{4,5},{5,4},{6,7},{7,6},{8,9},{9,8},{10,11... | collective-permute-start | bytes 786440 | tf_op jit(solution)/shard_map/reduce/ppermute | solution.py:194
  40.8 5.5 %copy-start.5 = (s32[1,8]{1,0:T(1,128)S(1)}, s32[1,8]{1,0:T(1,128)}, u32[]{:S(2)}) copy-start(s32[1,8]{1,0:T(1,128)} %old_ref.1) | copy-start | bytes 100
  40.8 5.5 %copy-start.7 = (s32[1,8]{1,0:T(1,128)S(1)}, s32[1,8]{1,0:T(1,128)}, u32[]{:S(2)}) copy-start(s32[1,8]{1,0:T(1,128)} %new_ref.1) | copy-start | bytes 100
  45.6 23.4 %copy-start.8 = (bf16[512,512]{1,0:T(8,128)(2,1)S(1)}, bf16[512,512]{1,0:T(8,128)(2,1)}, u32[]{:S(2)}) copy-start(bf16[512,512]{1,0:T(8,128)(2,1)} %param.10) | copy-start | bytes 1572868
  46.3 10.1 %collective-permute-start.13 = (bf16[256,512]{1,0:T(8,128)(2,1)S(1)}, bf16[256,512]{1,0:T(8,128)(2,1)S(1)}, u32[]{:S(2)}, u32[]{:S(2)}) collective-permute-start(bf16[256,512]{1,0:T(8,128)(2,1)S(1)} %get-tuple-element.23), channel_id=1, source_target_pairs={{0,1},{1,0},{2,3},{3,2},{4,5},{5,4},{6,7},{7,6},{8,9},{9,8},{10,11... | collective-permute-start | bytes 786440 | tf_op jit(solution)/shard_map/reduce/ppermute | solution.py:194
  48.2 15.6 %all-to-all-start.1 = ((bf16[8,64,256]{2,1,0:T(8,128)(2,1)}), bf16[8,64,256]{2,1,0:T(8,128)(2,1)S(1)}, u32[]{:S(2)}, u32[]{:S(2)}) async-start(bf16[8,64,256]{2,1,0:T(8,128)(2,1)} %bitcast.13), calls=%async_computation.1 | async-start | bytes 524288 | tf_op jit(solution)/shard_map/extend/all_to_all | solution.py:247
  54.3 9.6 %collective-permute-start.6 = (bf16[256,512]{1,0:T(8,128)(2,1)}, bf16[256,512]{1,0:T(8,128)(2,1)S(1)}, u32[]{:S(2)}, u32[]{:S(2)}) collective-permute-start(bf16[256,512]{1,0:T(8,128)(2,1)} %get-tuple-element.20), channel_id=1, source_target_pairs={{0,1},{1,0},{2,3},{3,2},{4,5},{5,4},{6,7},{7,6},{8,9},{9,8},{10,11... | collective-permute-start | bytes 786440 | tf_op jit(solution)/shard_map/reduce/ppermute | solution.py:194
  54.5 9.4 %collective-permute-start.12 = (bf16[256,512]{1,0:T(8,128)(2,1)}, bf16[256,512]{1,0:T(8,128)(2,1)S(1)}, u32[]{:S(2)}, u32[]{:S(2)}) collective-permute-start(bf16[256,512]{1,0:T(8,128)(2,1)} %get-tuple-element.22), channel_id=1, source_target_pairs={{0,1},{1,0},{2,3},{3,2},{4,5},{5,4},{6,7},{7,6},{8,9},{9,8},{10,11... | collective-permute-start | bytes 786440 | tf_op jit(solution)/shard_map/reduce/ppermute | solution.py:194
  54.8 9.2 %collective-permute-start.8 = (bf16[256,512]{1,0:T(8,128)(2,1)S(1)}, bf16[256,512]{1,0:T(8,128)(2,1)S(1)}, u32[]{:S(2)}, u32[]{:S(2)}) collective-permute-start(bf16[256,512]{1,0:T(8,128)(2,1)S(1)} %fusion.5), channel_id=1, source_target_pairs={{0,2},{1,3},{2,0},{3,1},{4,6},{5,7},{6,4},{7,5},{8,10},{9,11},{10,... | collective-permute-start | bytes 786440 | tf_op jit(solution)/shard_map/reduce/ppermute | solution.py:194
  56.5 12.5 %collective-permute-start.14 = (bf16[256,512]{1,0:T(8,128)(2,1)S(1)}, bf16[256,512]{1,0:T(8,128)(2,1)S(1)}, u32[]{:S(2)}, u32[]{:S(2)}) collective-permute-start(bf16[256,512]{1,0:T(8,128)(2,1)S(1)} %fusion), channel_id=1, source_target_pairs={{0,2},{1,3},{2,0},{3,1},{4,6},{5,7},{6,4},{7,5},{8,10},{9,11},{10,... | collective-permute-start | bytes 786440 | tf_op jit(solution)/shard_map/reduce/ppermute | solution.py:194
  (2 other events, 1.4 us)

commit v2 on v1

v2 whole, which is shorter than its diff:
```python
import functools
import math

import jax
import jax.numpy as jnp
from jax import lax
from jax.experimental import pallas as pl
from jax.experimental.pallas import tpu as pltpu
from jax.sharding import PartitionSpec as P

EPSILON = 1e-05
MASKED = -1e30
CHUNKS = 2
ROW_TILE = 128
NORM_ROWS = 64
F32 = jnp.float32
BF16 = jnp.bfloat16

VMEM = pl.BlockSpec(memory_space=pltpu.VMEM)
SMEM = pl.BlockSpec(memory_space=pltpu.SMEM)


def dot(a, b):
    return lax.dot_general(a, b, (((1,), (0,)), ((), ())), preferred_element_type=F32)


def dot_t(a, b):
    return lax.dot_general(a, b, (((1,), (1,)), ((), ())), preferred_element_type=F32)


def pack_kernel(cache_ref, *out_refs):
    me = lax.axis_index("seq")
    for k, out_ref in enumerate(out_refs):
        out_ref[...] = cache_ref[me ^ (k + 1)]


def order_kernel(share, swapped, table_ref, cache_ref, *refs):
    arrived, me = gathered(swapped, cache_ref, refs[:-1])
    out_ref = refs[-1]
    rows, count = out_ref.shape[0], arrived.shape[0]
    row = lax.broadcasted_iota(jnp.int32, (rows, 128), 0)
    block = row // share
    holder = jnp.zeros_like(block)
    for b in range(rows // share):
        holder = jnp.where(block == b, table_ref[0, b] ^ me, holder)
    index = (holder * share + row % share)[:, :1]
    column = lax.broadcasted_iota(jnp.int32, (rows, count), 1)
    pick = jnp.where(column == index, 1.0, 0.0).astype(BF16)
    out_ref[...] = dot(pick, arrived).astype(BF16)


def gathered(swapped, cache_ref, refs):
    if swapped:
        me = lax.axis_index("seq")
        return jnp.concatenate([cache_ref[me]] + [ref[...] for ref in refs], axis=0), me
    return refs[0][...], 0


def extend_kernel(
    share, block_rows, swapped, old_ref, new_ref, held_ref, span_ref, kv_ref, cache_ref, *refs
):
    arrived_refs = refs[: len(refs) // 2] if swapped else refs[:1]
    out_refs = refs[len(arrived_refs) :]
    arrived, me = gathered(swapped, cache_ref, arrived_refs)
    rows = arrived.shape[0]
    groups = rows // share
    held, span = held_ref[0], span_ref[0]
    row = lax.broadcasted_iota(jnp.int32, (rows, 128), 0)
    target = row // share
    block, holder = jnp.zeros_like(row), jnp.zeros_like(row)
    for b in range(groups):
        hit = target == new_ref[0, b] ^ me
        block = jnp.where(hit, b, block)
        holder = jnp.where(hit, old_ref[0, b] ^ me, holder)
    position = block * block_rows + lax.axis_index("tp") * share + row % share
    old_row = jnp.where(position < held, holder * share + row % share, -1)[:, :1]
    fresh = position - held
    new_row = jnp.where((fresh >= 0) & (fresh < span), fresh, -1)[:, :1]
    column = lax.broadcasted_iota(jnp.int32, (rows, rows), 1)
    total = dot(jnp.where(column == old_row, 1.0, 0.0).astype(BF16), arrived)
    column = lax.broadcasted_iota(jnp.int32, (rows, kv_ref.shape[0]), 1)
    total += dot(jnp.where(column == new_row, 1.0, 0.0).astype(BF16), kv_ref[...])
    total = total.astype(BF16)
    count = rows // len(out_refs)
    for k, out_ref in enumerate(out_refs):
        out_ref[...] = total[k * count : (k + 1) * count]


def unpack_kernel(*refs):
    me = lax.axis_index("seq")
    for k, ref in enumerate(refs[:-1]):
        refs[-1][me ^ k] = ref[...]


def project_kernel(x0, x1, x2, x3, gain_ref, wq_ref, wkv_ref, q_ref, kv_ref, normed):
    pieces = (x0, x1, x2, x3)
    me = lax.axis_index("tp")
    rows, width = x0.shape
    features = width * len(pieces)

    def norm(step, carry):
        at = pl.ds(pl.multiple_of(step * NORM_ROWS, NORM_ROWS), NORM_ROWS)
        values = [piece[at, :].astype(F32) for piece in pieces]
        average = sum(jnp.sum(v, axis=1, keepdims=True) for v in values) / features
        centred = [v - average for v in values]
        spread = sum(jnp.sum(v * v, axis=1, keepdims=True) for v in centred) / features
        scale = lax.rsqrt(spread + EPSILON)
        for j, v in enumerate(centred):
            normed[j, at, :] = (v * scale * gain_ref[me ^ j]).astype(BF16)
        return carry

    lax.fori_loop(0, rows // NORM_ROWS, norm, 0)
    q_ref[...] = sum(dot(normed[j], wq_ref[me ^ j]) for j in range(len(pieces))).astype(BF16)
    kv_ref[...] = sum(dot(normed[j], wkv_ref[me ^ j]) for j in range(len(pieces))).astype(BF16)


def attend_kernel(share, block_rows, start_row, rows, held_ref, q_ref, kv_ref, c0, c1, c2, c3, *refs):
    wout_ref, far_refs, near_refs, (keys, values, context) = refs[0], refs[1:3], refs[3:5], refs[5:]
    pieces = (c0, c1, c2, c3)
    me = lax.axis_index("tp")
    held = held_ref[0]
    piece_rows, width = c0.shape
    hd = width // 2
    heads = q_ref.shape[1] // hd
    cached = piece_rows * len(pieces)
    known = start_row + rows

    spare = kv_ref[0:1, :hd].astype(F32)
    row = lax.broadcasted_iota(jnp.int32, (piece_rows, hd), 0)
    place = row // share * block_rows + row % share
    for j, piece in enumerate(pieces):
        at = pl.ds(j * piece_rows, piece_rows)
        used = place + (me ^ j) * share < held
        keys[at, :] = jnp.where(used, piece[:, :hd].astype(F32), spare).astype(BF16)
        values[at, hd:] = jnp.where(used, piece[:, hd:].astype(F32), 0.0).astype(BF16)
        values[at, :hd] = jnp.where(used, 1.0, 0.0).astype(BF16)
    at = pl.ds(cached, known)
    keys[at, :] = kv_ref[:known, :hd]
    values[at, hd:] = kv_ref[:known, hd:]
    values[at, :hd] = jnp.ones((known, hd), BF16)

    factor = hd ** (-0.5) * math.log2(math.e)
    tile = min(ROW_TILE, rows)
    for start in range(0, rows, tile):
        stop = cached + start_row + start
        q4 = jnp.concatenate(
            [
                q_ref[pl.ds(start_row + start, tile), h * hd : (h + 1) * hd]
                for h in range(heads)
            ],
            axis=0,
        )
        done = dot_t(q4, keys[pl.ds(0, stop), :])
        last = dot_t(q4, keys[pl.ds(stop, tile), :])
        own = lax.broadcasted_iota(jnp.int32, (heads * tile, tile), 0) % tile
        other = lax.broadcasted_iota(jnp.int32, (heads * tile, tile), 1)
        last = jnp.where(other <= own, last, MASKED)
        high = jnp.maximum(
            jnp.max(done, axis=1, keepdims=True), jnp.max(last, axis=1, keepdims=True)
        )
        p_done = jnp.exp2((done - high) * factor).astype(BF16)
        p_last = jnp.exp2((last - high) * factor).astype(BF16)
        both = dot(p_done, values[pl.ds(0, stop), :]) + dot(p_last, values[pl.ds(stop, tile), :])
        out = (both[:, hd:] / both[:, :hd]).astype(BF16)
        for h in range(heads):
            context[pl.ds(start, tile), h * hd : (h + 1) * hd] = out[h * tile : (h + 1) * tile]

    cols = wout_ref.shape[1] // 4
    for k in (3, 1, 2, 0):
        columns = pl.ds(pl.multiple_of((me ^ k) * cols, cols), cols)
        part = dot(context[...], wout_ref[:, columns]).astype(BF16)
        if k & 1:
            far_refs[k >> 1][...] = part
        else:
            near_refs[k >> 1][...] = part


def finish_kernel(rows, at, span_ref, tokens_ref, near_ref, got_ref, crossed_ref, *refs):
    out_ref = refs[-1]
    kept = near_ref[...].astype(F32) + got_ref[...].astype(F32)
    total = tokens_ref[...].astype(F32) + (kept + crossed_ref[...].astype(F32))
    row = lax.broadcasted_iota(jnp.int32, total.shape, 0) + at
    out_ref[...] = jnp.where(row < span_ref[0], total, 0.0).astype(BF16)


def call(kernel, out_shape, in_specs, args, flops, scratch=(), exps=0, name=None):
    outs = out_shape if isinstance(out_shape, (list, tuple)) else [out_shape]
    moved = sum(a.size * a.dtype.itemsize for a in list(args) + list(outs))
    return pl.pallas_call(
        kernel,
        out_shape=out_shape,
        in_specs=in_specs,
        out_specs=jax.tree.map(lambda _: VMEM, out_shape),
        scratch_shapes=list(scratch),
        cost_estimate=pl.CostEstimate(flops=flops, bytes_accessed=moved, transcendentals=exps),
        compiler_params=pltpu.CompilerParams(vmem_limit_bytes=32 * 1024 * 1024),
        name=name,
    )(*args)


def body(
    tokens,
    norm_gain,
    w_query,
    w_keyval,
    w_out,
    span_lens,
    cached_lens,
    old_table,
    new_table,
    old_cache,
):
    tp = lax.axis_size("tp")
    groups, share, width = old_cache.shape
    block_rows = share * tp
    capacity = groups * block_rows
    rows, cols = tokens.shape
    q_cols = w_query.shape[1]
    features = w_query.shape[0]
    hd = width // 2
    most_held = capacity - rows
    piece_rows = most_held // tp

    def swap(x, bit, axis="tp"):
        size = lax.axis_size(axis)
        return lax.ppermute(x, axis, [(i, i ^ bit) for i in range(size)])

    swapped = groups <= 8 and groups & (groups - 1) == 0
    block = jax.ShapeDtypeStruct((share, width), BF16)

    with jax.named_scope("tokens_gather"):
        across = swap(tokens, 2)
        beside = swap(tokens, 1)
        corner = swap(across, 1)

    with jax.named_scope("cache_gather"):
        if swapped:
            packed = call(
                pack_kernel, [block] * (groups - 1), [VMEM], (old_cache,), flops=0, name="pack"
            )
            arrived = [swap(x, k + 1, "seq") for k, x in enumerate(packed)]
        else:
            arrived = lax.all_to_all(old_cache, "seq", split_axis=0, concat_axis=0, tiled=True)
            arrived = [arrived.reshape(groups * share, width)]
        ordered = call(
            functools.partial(order_kernel, share, swapped),
            jax.ShapeDtypeStruct((piece_rows, width), BF16),
            [SMEM, VMEM] + [VMEM] * len(arrived),
            (old_table, old_cache, *arrived),
            flops=2 * piece_rows * groups * share * width,
            name="order",
        )
        c_across = swap(ordered, 2)
        cached = (ordered, swap(ordered, 1), c_across, swap(c_across, 1))

    with jax.named_scope("project"):
        query, keyval = call(
            project_kernel,
            [
                jax.ShapeDtypeStruct((rows, q_cols), BF16),
                jax.ShapeDtypeStruct((rows, width), BF16),
            ],
            [VMEM] * 7,
            (
                tokens,
                beside,
                across,
                corner,
                norm_gain.reshape(tp, 1, cols),
                w_query.reshape(tp, cols, q_cols),
                w_keyval.reshape(tp, cols, width),
            ),
            flops=2 * rows * features * (q_cols + width),
            scratch=[pltpu.VMEM((tp, rows, cols), BF16)],
            name="project",
        )

    with jax.named_scope("extend"):
        sent = call(
            functools.partial(extend_kernel, share, block_rows, swapped),
            [block] * groups if swapped else [jax.ShapeDtypeStruct((groups * share, width), BF16)],
            [SMEM] * 4 + [VMEM] * (2 + len(arrived)),
            (old_table, new_table, cached_lens, span_lens, keyval, old_cache, *arrived),
            flops=4 * groups * share * groups * share * width,
            name="extend",
        )
        if swapped:
            returned = [swap(x, k, "seq") if k else x for k, x in enumerate(sent)]
            new_cache = call(
                unpack_kernel,
                jax.ShapeDtypeStruct(old_cache.shape, BF16),
                [VMEM] * groups,
                returned,
                flops=0,
                name="unpack",
            )
        else:
            new_cache = lax.all_to_all(
                sent[0].reshape(groups, share, width), "seq", split_axis=0, concat_axis=0, tiled=True
            )

    part = rows // CHUNKS
    mixed = None
    for c in range(CHUNKS):
        with jax.named_scope("attend"):
            seen = most_held + (c + 1) * part
            far0, far1, near0, near1 = call(
                functools.partial(attend_kernel, share, block_rows, c * part, part),
                [jax.ShapeDtypeStruct((part, cols), BF16)] * 4,
                [SMEM] + [VMEM] * 7,
                (cached_lens, query, keyval, *cached, w_out),
                flops=4 * part * seen * q_cols + 2 * part * q_cols * features,
                exps=part * seen * (q_cols // hd),
                scratch=[
                    pltpu.VMEM((seen, hd), BF16),
                    pltpu.VMEM((seen, width), BF16),
                    pltpu.VMEM((part, q_cols), BF16),
                ],
                name="attend",
            )
        with jax.named_scope("reduce"):
            got1 = swap(far1, 1)
            pair = (near1.astype(F32) + got1.astype(F32)).astype(BF16)
            crossed = swap(pair, 2)
            got0 = swap(far0, 1)
            rows_at = pl.BlockSpec((part, cols), lambda i, c=c: (c, 0))
            whole = pl.BlockSpec((part, cols), lambda i: (0, 0))
            mixed = pl.pallas_call(
                functools.partial(finish_kernel, part, c * part),
                grid=(1,),
                out_shape=jax.ShapeDtypeStruct((rows, cols), BF16),
                in_specs=[SMEM, rows_at, whole, whole, whole]
                + [pl.BlockSpec(memory_space=pl.ANY)] * (c > 0),
                out_specs=rows_at,
                input_output_aliases={5: 0} if c else {},
                cost_estimate=pl.CostEstimate(
                    flops=4 * part * cols, bytes_accessed=10 * part * cols, transcendentals=0
                ),
                name="finish",
            )(span_lens, tokens, near0, got0, crossed, *([mixed] if c else []))
    return (mixed, new_cache)


def solution(mesh):
    in_specs = (
        P("seq", "tp"),
        P(),
        P(None, "tp"),
        P(),
        P("tp", None),
        P("seq"),
        P("seq"),
        P("seq", None),
        P("seq", None),
        P("seq", "tp", None),
    )
    out_specs = (P("seq", "tp"), P("seq", "tp", None))
    return jax.shard_map(body, mesh=mesh, in_specs=in_specs, out_specs=out_specs, check_vma=False)
```

time: 71.2 us -> 110 us (1.54)
  waiting for transfers between devices: 24.2 us -> 51.2 us
  starting transfers between devices: 21 us -> 27.8 us
  Pallas kernels: 16.1 us -> 20.1 us
  local copies, waits for them, and re-layouts: 6.21 us -> 8.5 us
  other arithmetic: 1.27 us -> 0.13 us
    ppermute x15 -> x26, waiting for transfers between devices: 17.4 us -> 51.2 us  [swap(): return lax.ppermute(x, axis, [(i, i ^ bit) for i in range(size)])]
    ppermute x15 -> x26, starting transfers between devices: 7.6 us -> 27.8 us  [swap(): return lax.ppermute(x, axis, [(i, i ^ bit) for i in range(size)])]
    all_to_all x2 -> x0, starting transfers between devices: 13.4 us -> none  [the longest x1 7.4 us: body(): lax.all_to_all(old_cache, 'seq', split_axis=0, concat_axis=0, tiled=True)]
    all_to_all x2 -> x0, waiting for transfers between devices: 6.76 us -> none  [the longest x1 6.76 us: body(): lax.all_to_all(sent.reshape(groups, share, width), 'seq', split_axis=0, c...]
    unnamed x19 -> x32, local copies, waits for them, and re-layouts: 3.67 us -> 8.5 us
    pallas_call x0 -> x2, Pallas kernels: none -> 4.09 us  [body(): pl.pallas_call(functools.partial(finish_kernel, part, c * part), grid=(1,...]
    squeeze x2 -> x0, local copies, waits for them, and re-layouts: 1.48 us -> none  [body(): kept = near[0].astype(F32) + swap(far[0], 1).astype(F32)]
    pallas_call x6 -> x7, Pallas kernels: 16.1 us -> 16 us  [call(): pl.pallas_call(kernel, out_shape=out_shape, in_specs=in_specs, out_specs=...]
  transfers between devices with their start and end apart: 17 -> 26, of which waited for: 6 -> 13; matrix products, arithmetic and copies ran while one was open for 3% -> 0% of each run, Pallas kernels for 17% -> 13%
where the time goes in v2:
time: 110 us
  waiting for transfers between devices  51.2 us (47%)
  starting transfers between devices  27.8 us (25%)
  Pallas kernels  20.1 us (18%)
  local copies, waits for them, and re-layouts  8.5 us (8%)
  between operations  2.13 us (2%)
    ppermute x26, waiting for transfers between devices, swap(): return lax.ppermute(x, axis, [(i, i ^ bit) for i in range(size)])  51.2 us
    ppermute x26, starting transfers between devices, swap(): return lax.ppermute(x, axis, [(i, i ^ bit) for i in range(size)])  27.8 us
    pallas_call x7, Pallas kernels, call(): pl.pallas_call(kernel, out_shape=out_shape, in_specs=in_specs, out_specs=...  16 us
    unnamed x32, local copies, waits for them, and re-layouts  8.5 us
    pallas_call x2, Pallas kernels, body(): pl.pallas_call(functools.partial(finish_kernel, part, c * part), grid=(1,...  4.09 us
  transfers between devices with their start and end apart: 26, of which 13 were waited for; matrix products, arithmetic and copies ran while one was open for 0% of the time, Pallas kernels for 13%

profile of v2, /device:TPU:0, one launch (start us, length us, event | category | flops | bytes accessed | tf_op | source)
XLA Modules:
  0.0 109.8 jit_solution(15663851253212994129)
XLA Ops:
  0.6 3.0 %collective-permute-start.1 = (bf16[512,512]{1,0:T(8,128)(2,1)}, bf16[512,512]{1,0:T(8,128)(2,1)S(1)}, u32[]{:S(2)}, u32[]{:S(2)}) collective-permute-start(bf16[512,512]{1,0:T(8,128)(2,1)} %tokens_ref.3), channel_id=1, source_target_pairs={{0,2},{1,3},{2,0},{3,1},{4,6},{5,7},{6,4},{7,5},{8,10},{9,11},{10,... | collective-permute-start | bytes 1572872 | tf_op jit(solution)/shard_map/tokens_gather/ppermute | solution.py:226
  3.7 12.1 %collective-permute-done.1.x2 = bf16[512,512]{1,0:T(8,128)(2,1)S(1)} collective-permute-done((bf16[512,512]{1,0:T(8,128)(2,1)}, bf16[512,512]{1,0:T(8,128)(2,1)S(1)}, u32[]{:S(2)}, u32[]{:S(2)}) %collective-permute-start.1) | collective-permute-done | bytes 524320 | tf_op jit(solution)/shard_map/tokens_gather/ppermute | solution.py:226
  16.8 1.8 %collective-permute-start.3 = (bf16[64,256]{1,0:T(8,128)(2,1)S(1)}, bf16[64,256]{1,0:T(8,128)(2,1)S(1)}, u32[]{:S(2)}, u32[]{:S(2)}) collective-permute-start(bf16[64,256]{1,0:T(8,128)(2,1)S(1)} %get-tuple-element.29), channel_id=1, source_target_pairs={{0,4},{4,0},{8,12},{12,8},{16,20},{20,16},{24,28},{28,24},{1,5},{5... | collective-permute-start | bytes 98312 | tf_op jit(solution)/shard_map/cache_gather/ppermute | solution.py:226
  20.8 2.8 %collective-permute-start.6 = (bf16[64,256]{1,0:T(8,128)(2,1)S(1)}, bf16[64,256]{1,0:T(8,128)(2,1)S(1)}, u32[]{:S(2)}, u32[]{:S(2)}) collective-permute-start(bf16[64,256]{1,0:T(8,128)(2,1)S(1)} %get-tuple-element.32), channel_id=1, source_target_pairs={{0,16},{4,20},{8,24},{12,28},{16,0},{20,4},{24,8},{28,12},{1,17},{... | collective-permute-start | bytes 98312 | tf_op jit(solution)/shard_map/cache_gather/ppermute | solution.py:226
  25.3 3.1 %collective-permute-start.8 = (bf16[64,256]{1,0:T(8,128)(2,1)S(1)}, bf16[64,256]{1,0:T(8,128)(2,1)S(1)}, u32[]{:S(2)}, u32[]{:S(2)}) collective-permute-start(bf16[64,256]{1,0:T(8,128)(2,1)S(1)} %get-tuple-element.34), channel_id=1, source_target_pairs={{0,24},{4,28},{8,16},{12,20},{16,8},{20,12},{24,0},{28,4},{1,25},{... | collective-permute-start | bytes 98312 | tf_op jit(solution)/shard_map/cache_gather/ppermute | solution.py:226
  28.4 2.5 %collective-permute-start.9 = (bf16[64,256]{1,0:T(8,128)(2,1)S(1)}, bf16[64,256]{1,0:T(8,128)(2,1)S(1)}, u32[]{:S(2)}, u32[]{:S(2)}) collective-permute-start(bf16[64,256]{1,0:T(8,128)(2,1)S(1)} %get-tuple-element.35), channel_id=1, source_target_pairs={{0,28},{4,24},{8,20},{12,16},{16,12},{20,8},{24,4},{28,0},{1,29},{... | collective-permute-start | bytes 98312 | tf_op jit(solution)/shard_map/cache_gather/ppermute | solution.py:226
  31.0 4.0 %collective-permute-done.9.refs_6_ = bf16[64,256]{1,0:T(8,128)(2,1)S(1)} collective-permute-done((bf16[64,256]{1,0:T(8,128)(2,1)S(1)}, bf16[64,256]{1,0:T(8,128)(2,1)S(1)}, u32[]{:S(2)}, u32[]{:S(2)}) %collective-permute-start.9) | collective-permute-done | bytes 32800 | tf_op jit(solution)/shard_map/cache_gather/ppermute | solution.py:226
  38.1 4.1 %collective-permute-done.11.c2 = bf16[384,256]{1,0:T(8,128)(2,1)S(1)} collective-permute-done((bf16[384,256]{1,0:T(8,128)(2,1)S(1)}, bf16[384,256]{1,0:T(8,128)(2,1)S(1)}, u32[]{:S(2)}, u32[]{:S(2)}) %collective-permute-start.11) | collective-permute-done | bytes 196640 | tf_op jit(solution)/shard_map/cache_gather/ppermute | solution.py:226
  44.0 1.6 %copy-done.7 = bf16[2048,512]{1,0:T(8,128)(2,1)S(1)} copy-done((bf16[2048,512]{1,0:T(8,128)(2,1)S(1)}, bf16[2048,512]{1,0:T(8,128)(2,1)}, u32[]{:S(2)}) %copy-start.7) | copy-done | bytes 2097176
  47.5 4.2 %project.1 = (bf16[512,512]{1,0:T(8,128)(2,1)S(1)}, bf16[512,256]{1,0:T(8,128)(2,1)S(1)}) custom-call(bf16[512,512]{1,0:T(8,128)(2,1)S(1)} %copy-done, bf16[512,512]{1,0:T(8,128)(2,1)S(1)} %collective-permute-done.x1, bf16[512,512]{1,0:T(8,128)(2,1)S(1)} %collective-permute-done.1.x2, bf16[512,512]{1,0:T(8,128)(2,1)S(1)} %collective-permute-done.2.x3, ...), custom_call_target="tpu_custom_call" | custom-call | flops 1610612736 | bytes 6037504 | tf_op jit(solution)/shard_map/project/project/pallas_call | solution.py:189
  51.8 4.2 %attend.3 = (bf16[256,512]{1,0:T(8,128)(2,1)S(1)}, bf16[256,512]{1,0:T(8,128)(2,1)S(1)}, bf16[256,512]{1,0:T(8,128)(2,1)S(1)}, bf16[256,512]{1,0:T(8,128)(2,1)S(1)}) custom-call(s32[1]{0:T(128)S(6)} %copy.15.held_ref, bf16[512,512]{1,0:T(8,128)(2,1)S(1)} %get-tuple-element.27.q_ref, bf16[512,256]{1,0:T(8,128)(2,1)S(1)} %get-tuple-element.28.kv_ref, ...), custom_call_target="tpu_custom_call" | custom-call | flops 1476395008 | bytes 4718596 | tf_op jit(solution)/shard_map/attend/attend/pallas_call | solution.py:189
  57.2 4.7 %attend.2 = (bf16[256,512]{1,0:T(8,128)(2,1)S(1)}, bf16[256,512]{1,0:T(8,128)(2,1)S(1)}, bf16[256,512]{1,0:T(8,128)(2,1)S(1)}, bf16[256,512]{1,0:T(8,128)(2,1)S(1)}) custom-call(s32[1]{0:T(128)S(6)} %copy.15.held_ref, bf16[512,512]{1,0:T(8,128)(2,1)S(1)} %get-tuple-element.27.q_ref, bf16[512,256]{1,0:T(8,128)(2,1)S(1)} %get-tuple-element.28.kv_ref, ...), custom_call_target="tpu_custom_call" | custom-call | flops 1610612736 | bytes 4718596 | tf_op jit(solution)/shard_map/attend/attend/pallas_call | solution.py:189
  62.7 1.6 %collective-permute-start.18 = (bf16[256,512]{1,0:T(8,128)(2,1)S(1)}, bf16[256,512]{1,0:T(8,128)(2,1)S(1)}, u32[]{:S(2)}, u32[]{:S(2)}) collective-permute-start(bf16[256,512]{1,0:T(8,128)(2,1)S(1)} %add_convert_fusion), channel_id=1, source_target_pairs={{0,2},{1,3},{2,0},{3,1},{4,6},{5,7},{6,4},{7,5},{8,10},{9,11},{10,... | collective-permute-start | bytes 786440 | tf_op jit(solution)/shard_map/reduce/ppermute | solution.py:226
  67.8 3.4 %collective-permute-done.19.refs_1_ = bf16[64,256]{1,0:T(8,128)(2,1)S(1)} collective-permute-done((bf16[64,256]{1,0:T(8,128)(2,1)S(1)}, bf16[64,256]{1,0:T(8,128)(2,1)S(1)}, u32[]{:S(2)}, u32[]{:S(2)}) %collective-permute-start.19) | collective-permute-done | bytes 32800 | tf_op jit(solution)/shard_map/extend/ppermute | solution.py:226
  71.2 3.9 %collective-permute-done.20.refs_2_ = bf16[64,256]{1,0:T(8,128)(2,1)S(1)} collective-permute-done((bf16[64,256]{1,0:T(8,128)(2,1)S(1)}, bf16[64,256]{1,0:T(8,128)(2,1)S(1)}, u32[]{:S(2)}, u32[]{:S(2)}) %collective-permute-start.20) | collective-permute-done | bytes 32800 | tf_op jit(solution)/shard_map/extend/ppermute | solution.py:226
  75.1 4.8 %collective-permute-done.21.refs_3_ = bf16[64,256]{1,0:T(8,128)(2,1)S(1)} collective-permute-done((bf16[64,256]{1,0:T(8,128)(2,1)S(1)}, bf16[64,256]{1,0:T(8,128)(2,1)S(1)}, u32[]{:S(2)}, u32[]{:S(2)}) %collective-permute-start.21) | collective-permute-done | bytes 32800 | tf_op jit(solution)/shard_map/extend/ppermute | solution.py:226
  80.2 5.0 %collective-permute-done.22.refs_4_ = bf16[64,256]{1,0:T(8,128)(2,1)S(1)} collective-permute-done((bf16[64,256]{1,0:T(8,128)(2,1)S(1)}, bf16[64,256]{1,0:T(8,128)(2,1)S(1)}, u32[]{:S(2)}, u32[]{:S(2)}) %collective-permute-start.22) | collective-permute-done | bytes 32800 | tf_op jit(solution)/shard_map/extend/ppermute | solution.py:226
  85.9 5.1 %collective-permute-done.23.refs_5_ = bf16[64,256]{1,0:T(8,128)(2,1)S(1)} collective-permute-done((bf16[64,256]{1,0:T(8,128)(2,1)S(1)}, bf16[64,256]{1,0:T(8,128)(2,1)S(1)}, u32[]{:S(2)}, u32[]{:S(2)}) %collective-permute-start.23) | collective-permute-done | bytes 32800 | tf_op jit(solution)/shard_map/extend/ppermute | solution.py:226
  91.0 2.0 %collective-permute-start.24 = (bf16[64,256]{1,0:T(8,128)(2,1)S(1)}, bf16[64,256]{1,0:T(8,128)(2,1)S(1)}, u32[]{:S(2)}, u32[]{:S(2)}) collective-permute-start(bf16[64,256]{1,0:T(8,128)(2,1)S(1)} %get-tuple-element.50), channel_id=1, source_target_pairs={{0,24},{4,28},{8,16},{12,20},{16,8},{20,12},{24,0},{28,4},{1,25},{... | collective-permute-start | bytes 98312 | tf_op jit(solution)/shard_map/extend/ppermute | solution.py:226
  93.0 3.7 %collective-permute-done.24.refs_6_ = bf16[64,256]{1,0:T(8,128)(2,1)S(1)} collective-permute-done((bf16[64,256]{1,0:T(8,128)(2,1)S(1)}, bf16[64,256]{1,0:T(8,128)(2,1)S(1)}, u32[]{:S(2)}, u32[]{:S(2)}) %collective-permute-start.24) | collective-permute-done | bytes 32800 | tf_op jit(solution)/shard_map/extend/ppermute | solution.py:226
  96.8 2.5 %collective-permute-start.25 = (bf16[64,256]{1,0:T(8,128)(2,1)S(1)}, bf16[64,256]{1,0:T(8,128)(2,1)S(1)}, u32[]{:S(2)}, u32[]{:S(2)}) collective-permute-start(bf16[64,256]{1,0:T(8,128)(2,1)S(1)} %get-tuple-element.51), channel_id=1, source_target_pairs={{0,28},{4,24},{8,20},{12,16},{16,12},{20,8},{24,4},{28,0},{1,29},{... | collective-permute-start | bytes 98312 | tf_op jit(solution)/shard_map/extend/ppermute | solution.py:226
  99.2 4.1 %collective-permute-done.25.refs_7_ = bf16[64,256]{1,0:T(8,128)(2,1)S(1)} collective-permute-done((bf16[64,256]{1,0:T(8,128)(2,1)S(1)}, bf16[64,256]{1,0:T(8,128)(2,1)S(1)}, u32[]{:S(2)}, u32[]{:S(2)}) %collective-permute-start.25) | collective-permute-done | bytes 32800 | tf_op jit(solution)/shard_map/extend/ppermute | solution.py:226
  104.9 2.0 %finish.2.refs_0_ = bf16[512,512]{1,0:T(8,128)(2,1)} custom-call(s32[1]{0:T(128)S(6)} %copy.14.span_ref, bf16[512,512]{1,0:T(8,128)(2,1)} %tokens_ref.3, bf16[256,512]{1,0:T(8,128)(2,1)} %copy-done.4, bf16[256,512]{1,0:T(8,128)(2,1)} %copy-done.14, bf16[256,512]{1,0:T(8,128)(2,1)} %copy-done.15), custom_call_target="tpu_custom_call" | custom-call | flops 524288 | bytes 1310720 | tf_op jit(solution)/shard_map/reduce/finish/pallas_call | solution.py:328
  107.8 2.0 %finish.3 = bf16[512,512]{1,0:T(8,128)(2,1)} custom-call(s32[1]{0:T(128)S(6)} %copy.14.span_ref, bf16[512,512]{1,0:T(8,128)(2,1)} %tokens_ref.3, bf16[256,512]{1,0:T(8,128)(2,1)} %copy-done.3, bf16[256,512]{1,0:T(8,128)(2,1)} %copy-done.12, bf16[256,512]{1,0:T(8,128)(2,1)} %copy-done.13, bf16[512,512]{1,0:T(8,128)(2,1)} %finish.2.refs_0_), custom_call_target="tpu_custom_call", output_to_operand_aliasing={{}: (5, {})} | custom-call | flops 524288 | bytes 1310720 | tf_op jit(solution)/shard_map/reduce/finish/pallas_call | solution.py:328
  (71 shorter events, 19.2 us)
Async XLA Ops:
  0.6 15.2 %collective-permute-start.1 = (bf16[512,512]{1,0:T(8,128)(2,1)}, bf16[512,512]{1,0:T(8,128)(2,1)S(1)}, u32[]{:S(2)}, u32[]{:S(2)}) collective-permute-start(bf16[512,512]{1,0:T(8,128)(2,1)} %tokens_ref.3), channel_id=1, source_target_pairs={{0,2},{1,3},{2,0},{3,1},{4,6},{5,7},{6,4},{7,5},{8,10},{9,11},{10,... | collective-permute-start | bytes 1572872 | tf_op jit(solution)/shard_map/tokens_gather/ppermute | solution.py:226
  3.7 39.3 %collective-permute-start = (bf16[512,512]{1,0:T(8,128)(2,1)}, bf16[512,512]{1,0:T(8,128)(2,1)S(1)}, u32[]{:S(2)}, u32[]{:S(2)}) collective-permute-start(bf16[512,512]{1,0:T(8,128)(2,1)} %tokens_ref.3), channel_id=1, source_target_pairs={{0,1},{1,0},{2,3},{3,2},{4,5},{5,4},{6,7},{7,6},{8,9},{9,8},{10,11... | collective-permute-start | bytes 1572872 | tf_op jit(solution)/shard_map/tokens_gather/ppermute | solution.py:226
  15.8 27.1 %collective-permute-start.2 = (bf16[512,512]{1,0:T(8,128)(2,1)S(1)}, bf16[512,512]{1,0:T(8,128)(2,1)S(1)}, u32[]{:S(2)}, u32[]{:S(2)}) collective-permute-start(bf16[512,512]{1,0:T(8,128)(2,1)S(1)} %collective-permute-done.1.x2), channel_id=1, source_target_pairs={{0,1},{1,0},{2,3},{3,2},{4,5},{5,4},{6,7},{7,6},{8,9},{9,8},{10,11... | collective-permute-start | bytes 1572872 | tf_op jit(solution)/shard_map/tokens_gather/ppermute | solution.py:226
  16.8 4.0 %collective-permute-start.3 = (bf16[64,256]{1,0:T(8,128)(2,1)S(1)}, bf16[64,256]{1,0:T(8,128)(2,1)S(1)}, u32[]{:S(2)}, u32[]{:S(2)}) collective-permute-start(bf16[64,256]{1,0:T(8,128)(2,1)S(1)} %get-tuple-element.29), channel_id=1, source_target_pairs={{0,4},{4,0},{8,12},{12,8},{16,20},{20,16},{24,28},{28,24},{1,5},{5... | collective-permute-start | bytes 98312 | tf_op jit(solution)/shard_map/cache_gather/ppermute | solution.py:226
  18.5 5.0 %collective-permute-start.4 = (bf16[64,256]{1,0:T(8,128)(2,1)S(1)}, bf16[64,256]{1,0:T(8,128)(2,1)S(1)}, u32[]{:S(2)}, u32[]{:S(2)}) collective-permute-start(bf16[64,256]{1,0:T(8,128)(2,1)S(1)} %get-tuple-element.30), channel_id=1, source_target_pairs={{0,8},{4,12},{8,0},{12,4},{16,24},{20,28},{24,16},{28,20},{1,9},{5... | collective-permute-start | bytes 98312 | tf_op jit(solution)/shard_map/cache_gather/ppermute | solution.py:226
  20.1 5.2 %collective-permute-start.5 = (bf16[64,256]{1,0:T(8,128)(2,1)S(1)}, bf16[64,256]{1,0:T(8,128)(2,1)S(1)}, u32[]{:S(2)}, u32[]{:S(2)}) collective-permute-start(bf16[64,256]{1,0:T(8,128)(2,1)S(1)} %get-tuple-element.31), channel_id=1, source_target_pairs={{0,12},{4,8},{8,4},{12,0},{16,28},{20,24},{24,20},{28,16},{1,13},{... | collective-permute-start | bytes 98312 | tf_op jit(solution)/shard_map/cache_gather/ppermute | solution.py:226
  20.8 7.7 %collective-permute-start.6 = (bf16[64,256]{1,0:T(8,128)(2,1)S(1)}, bf16[64,256]{1,0:T(8,128)(2,1)S(1)}, u32[]{:S(2)}, u32[]{:S(2)}) collective-permute-start(bf16[64,256]{1,0:T(8,128)(2,1)S(1)} %get-tuple-element.32), channel_id=1, source_target_pairs={{0,16},{4,20},{8,24},{12,28},{16,0},{20,4},{24,8},{28,12},{1,17},{... | collective-permute-start | bytes 98312 | tf_op jit(solution)/shard_map/cache_gather/ppermute | solution.py:226
  23.6 7.4 %collective-permute-start.7 = (bf16[64,256]{1,0:T(8,128)(2,1)S(1)}, bf16[64,256]{1,0:T(8,128)(2,1)S(1)}, u32[]{:S(2)}, u32[]{:S(2)}) collective-permute-start(bf16[64,256]{1,0:T(8,128)(2,1)S(1)} %get-tuple-element.33), channel_id=1, source_target_pairs={{0,20},{4,16},{8,28},{12,24},{16,4},{20,0},{24,12},{28,8},{1,21},{... | collective-permute-start | bytes 98312 | tf_op jit(solution)/shard_map/cache_gather/ppermute | solution.py:226
  25.3 5.7 %collective-permute-start.8 = (bf16[64,256]{1,0:T(8,128)(2,1)S(1)}, bf16[64,256]{1,0:T(8,128)(2,1)S(1)}, u32[]{:S(2)}, u32[]{:S(2)}) collective-permute-start(bf16[64,256]{1,0:T(8,128)(2,1)S(1)} %get-tuple-element.34), channel_id=1, source_target_pairs={{0,24},{4,28},{8,16},{12,20},{16,8},{20,12},{24,0},{28,4},{1,25},{... | collective-permute-start | bytes 98312 | tf_op jit(solution)/shard_map/cache_gather/ppermute | solution.py:226
  28.4 6.6 %collective-permute-start.9 = (bf16[64,256]{1,0:T(8,128)(2,1)S(1)}, bf16[64,256]{1,0:T(8,128)(2,1)S(1)}, u32[]{:S(2)}, u32[]{:S(2)}) collective-permute-start(bf16[64,256]{1,0:T(8,128)(2,1)S(1)} %get-tuple-element.35), channel_id=1, source_target_pairs={{0,28},{4,24},{8,20},{12,16},{16,12},{20,8},{24,4},{28,0},{1,29},{... | collective-permute-start | bytes 98312 | tf_op jit(solution)/shard_map/cache_gather/ppermute | solution.py:226
  36.5 5.7 %collective-permute-start.11 = (bf16[384,256]{1,0:T(8,128)(2,1)S(1)}, bf16[384,256]{1,0:T(8,128)(2,1)S(1)}, u32[]{:S(2)}, u32[]{:S(2)}) collective-permute-start(bf16[384,256]{1,0:T(8,128)(2,1)S(1)} %order.1.c0), channel_id=1, source_target_pairs={{0,2},{1,3},{2,0},{3,1},{4,6},{5,7},{6,4},{7,5},{8,10},{9,11},{10,... | collective-permute-start | bytes 589832 | tf_op jit(solution)/shard_map/cache_gather/ppermute | solution.py:226
  38.1 13.6 %collective-permute-start.10 = (bf16[384,256]{1,0:T(8,128)(2,1)S(1)}, bf16[384,256]{1,0:T(8,128)(2,1)S(1)}, u32[]{:S(2)}, u32[]{:S(2)}) collective-permute-start(bf16[384,256]{1,0:T(8,128)(2,1)S(1)} %order.1.c0), channel_id=1, source_target_pairs={{0,1},{1,0},{2,3},{3,2},{4,5},{5,4},{6,7},{7,6},{8,9},{9,8},{10,11... | collective-permute-start | bytes 589832 | tf_op jit(solution)/shard_map/cache_gather/ppermute | solution.py:226
  42.3 9.5 %collective-permute-start.12 = (bf16[384,256]{1,0:T(8,128)(2,1)S(1)}, bf16[384,256]{1,0:T(8,128)(2,1)S(1)}, u32[]{:S(2)}, u32[]{:S(2)}) collective-permute-start(bf16[384,256]{1,0:T(8,128)(2,1)S(1)} %collective-permute-done.11.c2), channel_id=1, source_target_pairs={{0,1},{1,0},{2,3},{3,2},{4,5},{5,4},{6,7},{7,6},{8,9},{9,8},{10,11... | collective-permute-start | bytes 589832 | tf_op jit(solution)/shard_map/cache_gather/ppermute | solution.py:226
  56.7 5.9 %collective-permute-start.17 = (bf16[256,512]{1,0:T(8,128)(2,1)S(1)}, bf16[256,512]{1,0:T(8,128)(2,1)S(1)}, u32[]{:S(2)}, u32[]{:S(2)}) collective-permute-start(bf16[256,512]{1,0:T(8,128)(2,1)S(1)} %get-tuple-element.43), channel_id=1, source_target_pairs={{0,1},{1,0},{2,3},{3,2},{4,5},{5,4},{6,7},{7,6},{8,9},{9,8},{10,11... | collective-permute-start | bytes 786440 | tf_op jit(solution)/shard_map/reduce/ppermute | solution.py:226
  62.1 42.0 %collective-permute-start.16 = (bf16[256,512]{1,0:T(8,128)(2,1)S(1)}, bf16[256,512]{1,0:T(8,128)(2,1)S(1)}, u32[]{:S(2)}, u32[]{:S(2)}) collective-permute-start(bf16[256,512]{1,0:T(8,128)(2,1)S(1)} %get-tuple-element.41), channel_id=1, source_target_pairs={{0,1},{1,0},{2,3},{3,2},{4,5},{5,4},{6,7},{7,6},{8,9},{9,8},{10,11... | collective-permute-start | bytes 786440 | tf_op jit(solution)/shard_map/reduce/ppermute | solution.py:226
  62.6 44.4 %collective-permute-start.13 = (bf16[256,512]{1,0:T(8,128)(2,1)S(1)}, bf16[256,512]{1,0:T(8,128)(2,1)S(1)}, u32[]{:S(2)}, u32[]{:S(2)}) collective-permute-start(bf16[256,512]{1,0:T(8,128)(2,1)S(1)} %get-tuple-element.37), channel_id=1, source_target_pairs={{0,1},{1,0},{2,3},{3,2},{4,5},{5,4},{6,7},{7,6},{8,9},{9,8},{10,11... | collective-permute-start | bytes 786440 | tf_op jit(solution)/shard_map/reduce/ppermute | solution.py:226
  62.7 41.4 %collective-permute-start.18 = (bf16[256,512]{1,0:T(8,128)(2,1)S(1)}, bf16[256,512]{1,0:T(8,128)(2,1)S(1)}, u32[]{:S(2)}, u32[]{:S(2)}) collective-permute-start(bf16[256,512]{1,0:T(8,128)(2,1)S(1)} %add_convert_fusion), channel_id=1, source_target_pairs={{0,2},{1,3},{2,0},{3,1},{4,6},{5,7},{6,4},{7,5},{8,10},{9,11},{10,... | collective-permute-start | bytes 786440 | tf_op jit(solution)/shard_map/reduce/ppermute | solution.py:226
  64.4 42.6 %collective-permute-start.15 = (bf16[256,512]{1,0:T(8,128)(2,1)S(1)}, bf16[256,512]{1,0:T(8,128)(2,1)S(1)}, u32[]{:S(2)}, u32[]{:S(2)}) collective-permute-start(bf16[256,512]{1,0:T(8,128)(2,1)S(1)} %add_convert_fusion.1), channel_id=1, source_target_pairs={{0,2},{1,3},{2,0},{3,1},{4,6},{5,7},{6,4},{7,5},{8,10},{9,11},{10,... | collective-permute-start | bytes 786440 | tf_op jit(solution)/shard_map/reduce/ppermute | solution.py:226
  67.2 4.0 %collective-permute-start.19 = (bf16[64,256]{1,0:T(8,128)(2,1)S(1)}, bf16[64,256]{1,0:T(8,128)(2,1)S(1)}, u32[]{:S(2)}, u32[]{:S(2)}) collective-permute-start(bf16[64,256]{1,0:T(8,128)(2,1)S(1)} %get-tuple-element.45), channel_id=1, source_target_pairs={{0,4},{4,0},{8,12},{12,8},{16,20},{20,16},{24,28},{28,24},{1,5},{5... | collective-permute-start | bytes 98312 | tf_op jit(solution)/shard_map/extend/ppermute | solution.py:226
  75.1 4.8 %collective-permute-start.21 = (bf16[64,256]{1,0:T(8,128)(2,1)S(1)}, bf16[64,256]{1,0:T(8,128)(2,1)S(1)}, u32[]{:S(2)}, u32[]{:S(2)}) collective-permute-start(bf16[64,256]{1,0:T(8,128)(2,1)S(1)} %get-tuple-element.47), channel_id=1, source_target_pairs={{0,12},{4,8},{8,4},{12,0},{16,28},{20,24},{24,20},{28,16},{1,13},{... | collective-permute-start | bytes 98312 | tf_op jit(solution)/shard_map/extend/ppermute | solution.py:226
  79.9 5.3 %collective-permute-start.22 = (bf16[64,256]{1,0:T(8,128)(2,1)S(1)}, bf16[64,256]{1,0:T(8,128)(2,1)S(1)}, u32[]{:S(2)}, u32[]{:S(2)}) collective-permute-start(bf16[64,256]{1,0:T(8,128)(2,1)S(1)} %get-tuple-element.48), channel_id=1, source_target_pairs={{0,16},{4,20},{8,24},{12,28},{16,0},{20,4},{24,8},{28,12},{1,17},{... | collective-permute-start | bytes 98312 | tf_op jit(solution)/shard_map/extend/ppermute | solution.py:226
  85.2 5.8 %collective-permute-start.23 = (bf16[64,256]{1,0:T(8,128)(2,1)S(1)}, bf16[64,256]{1,0:T(8,128)(2,1)S(1)}, u32[]{:S(2)}, u32[]{:S(2)}) collective-permute-start(bf16[64,256]{1,0:T(8,128)(2,1)S(1)} %get-tuple-element.49), channel_id=1, source_target_pairs={{0,20},{4,16},{8,28},{12,24},{16,4},{20,0},{24,12},{28,8},{1,21},{... | collective-permute-start | bytes 98312 | tf_op jit(solution)/shard_map/extend/ppermute | solution.py:226
  91.0 5.7 %collective-permute-start.24 = (bf16[64,256]{1,0:T(8,128)(2,1)S(1)}, bf16[64,256]{1,0:T(8,128)(2,1)S(1)}, u32[]{:S(2)}, u32[]{:S(2)}) collective-permute-start(bf16[64,256]{1,0:T(8,128)(2,1)S(1)} %get-tuple-element.50), channel_id=1, source_target_pairs={{0,24},{4,28},{8,16},{12,20},{16,8},{20,12},{24,0},{28,4},{1,25},{... | collective-permute-start | bytes 98312 | tf_op jit(solution)/shard_map/extend/ppermute | solution.py:226
  96.8 6.6 %collective-permute-start.25 = (bf16[64,256]{1,0:T(8,128)(2,1)S(1)}, bf16[64,256]{1,0:T(8,128)(2,1)S(1)}, u32[]{:S(2)}, u32[]{:S(2)}) collective-permute-start(bf16[64,256]{1,0:T(8,128)(2,1)S(1)} %get-tuple-element.51), channel_id=1, source_target_pairs={{0,28},{4,24},{8,20},{12,16},{16,12},{20,8},{24,4},{28,0},{1,29},{... | collective-permute-start | bytes 98312 | tf_op jit(solution)/shard_map/extend/ppermute | solution.py:226
  (18 other events, 53.2 us)

commit v3 on v1

v3 whole, which is shorter than its diff:
```python
import functools
import math

import jax
import jax.numpy as jnp
from jax import lax
from jax.experimental import pallas as pl
from jax.experimental.pallas import tpu as pltpu
from jax.sharding import PartitionSpec as P

EPSILON = 1e-05
MASKED = -1e30
CHUNKS = 2
ROW_TILE = 128
KEY_TILE = 128
NORM_STEPS = 4
F32 = jnp.float32
BF16 = jnp.bfloat16

VMEM = pl.BlockSpec(memory_space=pltpu.VMEM)
SMEM = pl.BlockSpec(memory_space=pltpu.SMEM)
HBM = pl.BlockSpec(memory_space=pltpu.HBM)


def dot(a, b):
    return lax.dot_general(a, b, (((1,), (0,)), ((), ())), preferred_element_type=F32)


def dot_t(a, b):
    return lax.dot_general(a, b, (((1,), (1,)), ((), ())), preferred_element_type=F32)


def order_kernel(share, table_ref, arrived_ref, out_ref):
    rows, count = out_ref.shape[0], arrived_ref.shape[0]
    row = lax.broadcasted_iota(jnp.int32, (rows, 128), 0)
    block = row // share
    holder = jnp.zeros_like(block)
    for b in range(rows // share):
        holder = jnp.where(block == b, table_ref[0, b], holder)
    index = (holder * share + row % share)[:, :1]
    column = lax.broadcasted_iota(jnp.int32, (rows, count), 1)
    pick = jnp.where(column == index, 1.0, 0.0).astype(BF16)
    out_ref[...] = dot(pick, arrived_ref[...]).astype(BF16)


def extend_kernel(
    share, block_rows, old_ref, new_ref, held_ref, span_ref, arrived_ref, kv_ref, out_ref
):
    rows = arrived_ref.shape[0]
    held, span = held_ref[0], span_ref[0]
    row = lax.broadcasted_iota(jnp.int32, (rows, 128), 0)
    target = row // share
    block, holder = jnp.zeros_like(row), jnp.zeros_like(row)
    for b in range(rows // share):
        hit = target == new_ref[0, b]
        block = jnp.where(hit, b, block)
        holder = jnp.where(hit, old_ref[0, b], holder)
    position = block * block_rows + lax.axis_index("tp") * share + row % share
    old_row = jnp.where(position < held, holder * share + row % share, -1)[:, :1]
    fresh = position - held
    new_row = jnp.where((fresh >= 0) & (fresh < span), fresh, -1)[:, :1]
    column = lax.broadcasted_iota(jnp.int32, (rows, rows), 1)
    total = dot(jnp.where(column == old_row, 1.0, 0.0).astype(BF16), arrived_ref[...])
    column = lax.broadcasted_iota(jnp.int32, (rows, kv_ref.shape[0]), 1)
    total += dot(jnp.where(column == new_row, 1.0, 0.0).astype(BF16), kv_ref[...])
    out_ref[...] = total.astype(BF16)


def project_kernel(
    x0, x1, x2, x3, gain_ref, wq_hbm, wkv_hbm, q_ref, kv_ref, normed, wq, wkv, q_acc, kv_acc, sems
):
    pieces = (x0, x1, x2, x3)
    me = lax.axis_index("tp")
    rows, width = x0.shape
    features = width * len(pieces)
    half = rows // 2
    step_rows = half // NORM_STEPS
    loads = [
        pltpu.make_async_copy(wq_hbm, wq, sems.at[0]),
        pltpu.make_async_copy(wkv_hbm, wkv, sems.at[1]),
    ]
    for load in loads:
        load.start()

    def norm(start):
        at = pl.ds(pl.multiple_of(start, step_rows), step_rows)
        values = [piece[at, :].astype(F32) for piece in pieces]
        average = jnp.sum(sum(values), axis=1, keepdims=True) / features
        centred = [v - average for v in values]
        spread = jnp.sum(sum(v * v for v in centred), axis=1, keepdims=True) / features
        scale = lax.rsqrt(spread + EPSILON)
        for j, v in enumerate(centred):
            normed[j, at, :] = (v * scale * gain_ref[me ^ j]).astype(BF16)

    def multiply(j, start):
        left = normed[j, pl.ds(start, half), :]
        q_acc[...] += dot(left, wq[me ^ j])
        kv_acc[...] += dot(left, wkv[me ^ j])

    def first(step, carry):
        norm(step * step_rows)
        return carry

    def both(step, carry):
        norm(half + step * step_rows)
        multiply(step, 0)
        return carry

    def last(step, carry):
        multiply(step, half)
        return carry

    lax.fori_loop(0, NORM_STEPS, first, 0)
    for load in loads:
        load.wait()
    for start, run in ((0, both), (half, last)):
        q_acc[...] = jnp.zeros_like(q_acc)
        kv_acc[...] = jnp.zeros_like(kv_acc)
        lax.fori_loop(0, len(pieces), run, 0)
        q_ref[pl.ds(start, half), :] = q_acc[...].astype(BF16)
        kv_ref[pl.ds(start, half), :] = kv_acc[...].astype(BF16)


def attend_kernel(
    share, block_rows, start_row, rows, held_ref, span_ref, q_ref, kv_ref, c0, c1, c2, c3, *refs
):
    wout_hbm, far_refs, near_refs = refs[0], refs[1:3], refs[3:5]
    keys, values, context, wout, sem = refs[5:]
    pieces = (c0, c1, c2, c3)
    me = lax.axis_index("tp")
    held, span = held_ref[0], span_ref[0]
    piece_rows, width = c0.shape
    hd = width // 2
    heads = q_ref.shape[1] // hd
    cached = piece_rows * len(pieces)
    known = start_row + rows
    load = pltpu.make_async_copy(wout_hbm, wout, sem)
    load.start()

    spare = kv_ref[0:1, :hd].astype(F32)
    row = lax.broadcasted_iota(jnp.int32, (KEY_TILE, hd), 0)
    place = row // share * block_rows + row % share
    group = KEY_TILE * len(pieces)
    for i in range(piece_rows // KEY_TILE):
        for j, piece in enumerate(pieces):
            at = pl.ds(i * group + j * KEY_TILE, KEY_TILE)
            source = pl.ds(i * KEY_TILE, KEY_TILE)
            used = place + (me ^ j) * share + i * group < held
            keys[at, :] = jnp.where(used, piece[source, :hd].astype(F32), spare).astype(BF16)
            values[at, hd:] = jnp.where(used, piece[source, hd:].astype(F32), 0.0).astype(BF16)
            values[at, :hd] = jnp.where(used, 1.0, 0.0).astype(BF16)
    at = pl.ds(cached, known)
    keys[at, :] = kv_ref[:known, :hd]
    values[at, hd:] = kv_ref[:known, hd:]
    values[at, :hd] = jnp.ones((known, hd), BF16)

    factor = hd ** (-0.5) * math.log2(math.e)
    tile = min(ROW_TILE, rows)

    def soften(start, used):
        parts = [pl.ds(0, used)]
        if start_row + start:
            parts.append(pl.ds(cached, start_row + start))
        own = pl.ds(cached + start_row + start, tile)
        q4 = jnp.concatenate(
            [
                q_ref[pl.ds(start_row + start, tile), h * hd : (h + 1) * hd]
                for h in range(heads)
            ],
            axis=0,
        )
        scores = [dot_t(q4, keys[part, :]) for part in parts]
        last = dot_t(q4, keys[own, :])
        to = lax.broadcasted_iota(jnp.int32, (heads * tile, tile), 0) % tile
        by = lax.broadcasted_iota(jnp.int32, (heads * tile, tile), 1)
        scores.append(jnp.where(by <= to, last, MASKED))
        high = functools.reduce(jnp.maximum, [jnp.max(s, axis=1, keepdims=True) for s in scores])
        both = sum(
            dot(jnp.exp2((s - high) * factor).astype(BF16), values[part, :])
            for s, part in zip(scores, parts + [own])
        )
        out = (both[:, hd:] / both[:, :hd]).astype(BF16)
        for h in range(heads):
            context[pl.ds(start, tile), h * hd : (h + 1) * hd] = out[h * tile : (h + 1) * tile]

    context[...] = jnp.zeros_like(context)
    for start in range(0, rows, tile):
        for used in range(group, cached + 1, group):
            fits = held <= used if used < cached else True
            needed = (held > used - group) & fits & (start_row + start < span)
            pl.when(needed)(functools.partial(soften, start, used))

    load.wait()
    cols = wout.shape[1] // 4
    for k in (3, 1, 2, 0):
        columns = pl.ds(pl.multiple_of((me ^ k) * cols, cols), cols)
        part = dot(context[...], wout[:, columns]).astype(BF16)
        if k & 1:
            far_refs[k >> 1][...] = part
        else:
            near_refs[k >> 1][...] = part


def finish_kernel(span_ref, tokens_ref, *refs):
    out_ref = refs[-1]
    part = refs[0].shape[0]
    for c in range(len(refs) // 3):
        near, got, crossed = refs[3 * c : 3 * c + 3]
        at = pl.ds(c * part, part)
        kept = near[...].astype(F32) + got[...].astype(F32)
        total = tokens_ref[at, :].astype(F32) + (kept + crossed[...].astype(F32))
        row = lax.broadcasted_iota(jnp.int32, total.shape, 0) + c * part
        out_ref[at, :] = jnp.where(row < span_ref[0], total, 0.0).astype(BF16)


def call(kernel, out_shape, in_specs, args, mib, scratch=(), name=None):
    return pl.pallas_call(
        kernel,
        out_shape=out_shape,
        in_specs=in_specs,
        out_specs=jax.tree.map(lambda _: VMEM, out_shape),
        scratch_shapes=list(scratch),
        cost_estimate=pl.CostEstimate(flops=1024, bytes_accessed=1024, transcendentals=0),
        compiler_params=pltpu.CompilerParams(vmem_limit_bytes=mib * 1024 * 1024),
        name=name,
    )(*args)


def body(
    tokens,
    norm_gain,
    w_query,
    w_keyval,
    w_out,
    span_lens,
    cached_lens,
    old_table,
    new_table,
    old_cache,
):
    tp = lax.axis_size("tp")
    groups, share, width = old_cache.shape
    block_rows = share * tp
    capacity = groups * block_rows
    rows, cols = tokens.shape
    q_cols = w_query.shape[1]
    features = w_query.shape[0]
    hd = width // 2
    most_held = capacity - rows
    piece_rows = most_held // tp

    def swap(x, bit):
        return lax.ppermute(x, "tp", [(i, i ^ bit) for i in range(tp)])

    def exchange(x):
        return lax.all_to_all(x, "seq", split_axis=0, concat_axis=0, tiled=True)

    with jax.named_scope("tokens_gather"):
        across = swap(tokens, 2)
        beside = swap(tokens, 1)
        corner = swap(across, 1)

    with jax.named_scope("cache_gather"):
        beside, stored = lax.optimization_barrier((beside, old_cache))
        arrived = exchange(stored).reshape(groups * share, width)

    with jax.named_scope("project"):
        query, keyval = call(
            project_kernel,
            [
                jax.ShapeDtypeStruct((rows, q_cols), BF16),
                jax.ShapeDtypeStruct((rows, width), BF16),
            ],
            [VMEM] * 5 + [HBM] * 2,
            (
                tokens,
                beside,
                across,
                corner,
                norm_gain.reshape(tp, 1, cols),
                w_query.reshape(tp, cols, q_cols),
                w_keyval.reshape(tp, cols, width),
            ),
            mib=24,
            scratch=[
                pltpu.VMEM((tp, rows, cols), BF16),
                pltpu.VMEM((tp, cols, q_cols), BF16),
                pltpu.VMEM((tp, cols, width), BF16),
                pltpu.VMEM((rows // 2, q_cols), F32),
                pltpu.VMEM((rows // 2, width), F32),
                pltpu.SemaphoreType.DMA((2,)),
            ],
            name="project",
        )

    with jax.named_scope("cache_gather"):
        keyval, arrived = lax.optimization_barrier((keyval, arrived))
        ordered = call(
            functools.partial(order_kernel, share),
            jax.ShapeDtypeStruct((piece_rows, width), BF16),
            [SMEM, VMEM],
            (old_table, arrived),
            mib=8,
            name="order",
        )
        c_across = swap(ordered, 2)
        c_beside = swap(ordered, 1)

    with jax.named_scope("extend"):
        kv_later, c_beside = lax.optimization_barrier((keyval, c_beside))
        sent = call(
            functools.partial(extend_kernel, share, block_rows),
            jax.ShapeDtypeStruct((groups * share, width), BF16),
            [SMEM] * 4 + [VMEM] * 2,
            (old_table, new_table, cached_lens, span_lens, arrived, kv_later),
            mib=8,
            name="extend",
        )
        sent, c_across = lax.optimization_barrier((sent, c_across))
        new_cache = exchange(sent.reshape(groups, share, width))
        cached = (ordered, c_beside, c_across, swap(c_across, 1))

    part = rows // CHUNKS
    sums = []
    for c in range(CHUNKS):
        with jax.named_scope("attend"):
            seen = most_held + (c + 1) * part
            far0, far1, near0, near1 = call(
                functools.partial(attend_kernel, share, block_rows, c * part, part),
                [jax.ShapeDtypeStruct((part, cols), BF16)] * 4,
                [SMEM] * 2 + [VMEM] * 6 + [HBM],
                (cached_lens, span_lens, query, keyval, *cached, w_out),
                    mib=24,
                scratch=[
                    pltpu.VMEM((seen, hd), BF16),
                    pltpu.VMEM((seen, width), BF16),
                    pltpu.VMEM((part, q_cols), BF16),
                    pltpu.VMEM(w_out.shape, BF16),
                    pltpu.SemaphoreType.DMA,
                ],
                name="attend",
            )
        with jax.named_scope("reduce"):
            got1 = swap(far1, 1)
            pair = (near1.astype(F32) + got1.astype(F32)).astype(BF16)
            query, pair = lax.optimization_barrier((query, pair))
            sums += [near0, swap(far0, 1), swap(pair, 2)]
    with jax.named_scope("finish"):
        mixed = call(
            finish_kernel,
            jax.ShapeDtypeStruct((rows, cols), BF16),
            [SMEM] + [VMEM] * (1 + len(sums)),
            (span_lens, tokens, *sums),
            mib=8,
            name="finish",
        )
    return (mixed, new_cache)


def solution(mesh):
    in_specs = (
        P("seq", "tp"),
        P(),
        P(None, "tp"),
        P(),
        P("tp", None),
        P("seq"),
        P("seq"),
        P("seq", None),
        P("seq", None),
        P("seq", "tp", None),
    )
    out_specs = (P("seq", "tp"), P("seq", "tp", None))
    return jax.shard_map(body, mesh=mesh, in_specs=in_specs, out_specs=out_specs, check_vma=False)
```

time: 71.2 us -> 86.1 us (1.21)
  local copies, waits for them, and re-layouts: 6.21 us -> 14.1 us
  waiting for transfers between devices: 24.2 us -> 29.3 us
  starting transfers between devices: 21 us -> 23.2 us
  Pallas kernels: 16.1 us -> 17 us
    unnamed x19 -> x41, local copies, waits for them, and re-layouts: 3.67 us -> 14.1 us
    ppermute x15 -> x12, waiting for transfers between devices: 17.4 us -> 22.5 us  [swap(): return lax.ppermute(x, 'tp', [(i, i ^ bit) for i in range(tp)])]
    all_to_all x2, starting transfers between devices: 13.4 us -> 15.5 us  [exchange(): return lax.all_to_all(x, 'seq', split_axis=0, concat_axis=0, tiled=True)]
    squeeze x2 -> x0, local copies, waits for them, and re-layouts: 1.48 us -> none  [body(): kept = near[0].astype(F32) + swap(far[0], 1).astype(F32)]
    slice x1 -> x0, local copies, waits for them, and re-layouts: 1.06 us -> none  [body(): own = [tokens[c * part:(c + 1) * part] for c in range(CHUNKS)]]
    pallas_call x6, Pallas kernels: 16.1 us -> 17 us  [call(): pl.pallas_call(kernel, out_shape=out_shape, in_specs=in_specs, out_specs=...]
    ppermute x15 -> x12, starting transfers between devices: 7.6 us -> 7.7 us  [swap(): return lax.ppermute(x, 'tp', [(i, i ^ bit) for i in range(tp)])]
  transfers between devices with their start and end apart: 17 -> 14, of which waited for: 6 -> 7; matrix products, arithmetic and copies ran while one was open for 3% -> 0% of each run, Pallas kernels for 17% -> 8%
where the time goes in v3:
time: 86.1 us; the launch traced here: 86.5 us
  waiting for transfers between devices  29.3 us (34%)
  starting transfers between devices  23.2 us (27%)
  Pallas kernels  17 us (20%)
  local copies, waits for them, and re-layouts  14.1 us (16%)
  between operations  2.08 us (2%)
    ppermute x12, waiting for transfers between devices, swap(): return lax.ppermute(x, 'tp', [(i, i ^ bit) for i in range(tp)])  22.5 us
    pallas_call x6, Pallas kernels, call(): pl.pallas_call(kernel, out_shape=out_shape, in_specs=in_specs, out_specs=...  17 us
    all_to_all x2, starting transfers between devices, exchange(): return lax.all_to_all(x, 'seq', split_axis=0, concat_axis=0, tiled=True)  15.5 us
    unnamed x41, local copies, waits for them, and re-layouts  14.1 us
    ppermute x12, starting transfers between devices, swap(): return lax.ppermute(x, 'tp', [(i, i ^ bit) for i in range(tp)])  7.7 us
    all_to_all x2, waiting for transfers between devices, exchange(): return lax.all_to_all(x, 'seq', split_axis=0, concat_axis=0, tiled=True)  6.77 us
  transfers between devices with their start and end apart: 14, of which 7 were waited for; matrix products, arithmetic and copies ran while one was open for 0% of the time, Pallas kernels for 8%

profile of v3, /device:TPU:0, one launch (start us, length us, event | category | flops | bytes accessed | tf_op | source)
XLA Modules:
  0.0 86.5 jit_solution(4771406182177027477)
XLA Ops:
  0.6 3.0 %collective-permute-start.1 = (bf16[512,512]{1,0:T(8,128)(2,1)}, bf16[512,512]{1,0:T(8,128)(2,1)S(1)}, u32[]{:S(2)}, u32[]{:S(2)}) collective-permute-start(bf16[512,512]{1,0:T(8,128)(2,1)} %tokens_ref.1), channel_id=1, source_target_pairs={{0,2},{1,3},{2,0},{3,1},{4,6},{5,7},{6,4},{7,5},{8,10},{9,11},{10,... | collective-permute-start | bytes 1572872 | tf_op jit(solution)/shard_map/tokens_gather/ppermute | solution.py:253
  3.7 12.1 %collective-permute-done.1.x2 = bf16[512,512]{1,0:T(8,128)(2,1)S(1)} collective-permute-done((bf16[512,512]{1,0:T(8,128)(2,1)}, bf16[512,512]{1,0:T(8,128)(2,1)S(1)}, u32[]{:S(2)}, u32[]{:S(2)}) %collective-permute-start.1) | collective-permute-done | bytes 524320 | tf_op jit(solution)/shard_map/tokens_gather/ppermute | solution.py:253
  16.6 6.0 %all-to-all-start = ((bf16[8,64,256]{2,1,0:T(8,128)(2,1)}), bf16[8,64,256]{2,1,0:T(8,128)(2,1)S(1)}, u32[]{:S(2)}, u32[]{:S(2)}) async-start(bf16[8,64,256]{2,1,0:T(8,128)(2,1)} %param.19), calls=%async_computation | async-start | bytes 524288 | tf_op jit(solution)/shard_map/cache_gather/all_to_all | solution.py:256
  23.5 1.6 %copy-done.1 = bf16[2048,512]{1,0:T(8,128)(2,1)S(1)} copy-done((bf16[2048,512]{1,0:T(8,128)(2,1)S(1)}, bf16[2048,512]{1,0:T(8,128)(2,1)}, u32[]{:S(2)}) %copy-start.1) | copy-done | bytes 2097176
  25.1 1.0 %copy-done.2 = bf16[512,512]{1,0:T(8,128)(2,1)S(1)} copy-done((bf16[512,512]{1,0:T(8,128)(2,1)S(1)}, bf16[512,512]{1,0:T(8,128)(2,1)}, u32[]{:S(2)}) %copy-start.2) | copy-done | bytes 524312
  26.1 1.2 %copy-done.6 = bf16[2048,256]{1,0:T(8,128)(2,1)S(1)} copy-done((bf16[2048,256]{1,0:T(8,128)(2,1)S(1)}, bf16[2048,256]{1,0:T(8,128)(2,1)}, u32[]{:S(2)}) %copy-start.6) | copy-done | bytes 1048600
  27.3 1.0 %copy-done.8 = bf16[512,512]{1,0:T(8,128)(2,1)S(1)} copy-done((bf16[512,512]{1,0:T(8,128)(2,1)S(1)}, bf16[512,512]{1,0:T(8,128)(2,1)}, u32[]{:S(2)}) %copy-start.8) | copy-done | bytes 524312
  28.4 1.0 %copy-done.10 = bf16[512,512]{1,0:T(8,128)(2,1)S(1)} copy-done((bf16[512,512]{1,0:T(8,128)(2,1)S(1)}, bf16[512,512]{1,0:T(8,128)(2,1)}, u32[]{:S(2)}) %copy-start.10) | copy-done | bytes 524312
  29.4 1.0 %copy-done.12 = bf16[512,512]{1,0:T(8,128)(2,1)S(1)} copy-done((bf16[512,512]{1,0:T(8,128)(2,1)S(1)}, bf16[512,512]{1,0:T(8,128)(2,1)}, u32[]{:S(2)}) %copy-start.12) | copy-done | bytes 524312
  31.2 5.3 %project.1 = (bf16[512,512]{1,0:T(8,128)(2,1)S(1)}, bf16[512,256]{1,0:T(8,128)(2,1)S(1)}) custom-call(bf16[512,512]{1,0:T(8,128)(2,1)S(1)} %copy-done.2, bf16[512,512]{1,0:T(8,128)(2,1)S(1)} %copy-done.10, bf16[512,512]{1,0:T(8,128)(2,1)S(1)} %copy-done.8, bf16[512,512]{1,0:T(8,128)(2,1)S(1)} %copy-done.12, f32[4,1,512]{2,1,0:T(1,128)S(1)} %bitcast.9, ...), custom_call_target="tpu_custom_call" | custom-call | flops 1024 | bytes 1024 | tf_op jit(solution)/shard_map/project/project/pallas_call | solution.py:217
  37.6 1.5 %collective-permute-start.4 = (bf16[384,256]{1,0:T(8,128)(2,1)S(1)}, bf16[384,256]{1,0:T(8,128)(2,1)S(1)}, u32[]{:S(2)}, u32[]{:S(2)}) collective-permute-start(bf16[384,256]{1,0:T(8,128)(2,1)S(1)} %order.1.c0), channel_id=1, source_target_pairs={{0,2},{1,3},{2,0},{3,1},{4,6},{5,7},{6,4},{7,5},{8,10},{9,11},{10,... | collective-permute-start | bytes 589832 | tf_op jit(solution)/shard_map/cache_gather/ppermute | solution.py:253
  40.4 1.9 %extend.1 = bf16[512,256]{1,0:T(8,128)(2,1)} custom-call(s32[1,8]{1,0:T(1,128)S(1)} %copy-done.16, s32[1,8]{1,0:T(1,128)S(1)} %copy-done.17, s32[1]{0:T(128)S(6)} %copy.14.held_ref, s32[1]{0:T(128)S(6)} %copy.13.span_ref, bf16[512,256]{1,0:T(8,128)(2,1)S(1)} %bitcast.6, bf16[512,256]{1,0:T(8,128)(2,1)S(1)} %get-tuple-element.30.kv_ref), custom_call_target="tpu_custom_call" | custom-call | flops 1024 | bytes 1024 | tf_op jit(solution)/shard_map/extend/extend/pallas_call | solution.py:217
  42.3 2.4 %collective-permute-done.4.c2 = bf16[384,256]{1,0:T(8,128)(2,1)S(1)} collective-permute-done((bf16[384,256]{1,0:T(8,128)(2,1)S(1)}, bf16[384,256]{1,0:T(8,128)(2,1)S(1)}, u32[]{:S(2)}, u32[]{:S(2)}) %collective-permute-start.4) | collective-permute-done | bytes 196640 | tf_op jit(solution)/shard_map/cache_gather/ppermute | solution.py:253
  44.7 1.4 %collective-permute-done.5.c3 = bf16[384,256]{1,0:T(8,128)(2,1)S(1)} collective-permute-done((bf16[384,256]{1,0:T(8,128)(2,1)S(1)}, bf16[384,256]{1,0:T(8,128)(2,1)S(1)}, u32[]{:S(2)}, u32[]{:S(2)}) %collective-permute-start.5) | collective-permute-done | bytes 196640 | tf_op jit(solution)/shard_map/extend/ppermute | solution.py:253
  46.1 3.5 %attend.2 = (bf16[256,512]{1,0:T(8,128)(2,1)S(1)}, bf16[256,512]{1,0:T(8,128)(2,1)S(1)}, bf16[256,512]{1,0:T(8,128)(2,1)S(1)}, bf16[256,512]{1,0:T(8,128)(2,1)S(1)}) custom-call(s32[1]{0:T(128)S(6)} %copy.14.held_ref, s32[1]{0:T(128)S(6)} %copy.13.span_ref, bf16[512,512]{1,0:T(8,128)(2,1)S(1)} %get-tuple-element.37.q_ref, ...), custom_call_target="tpu_custom_call" | custom-call | flops 1024 | bytes 1024 | tf_op jit(solution)/shard_map/attend/attend/pallas_call | solution.py:217
  50.5 1.4 %collective-permute-done.7 = bf16[256,512]{1,0:T(8,128)(2,1)S(1)} collective-permute-done((bf16[256,512]{1,0:T(8,128)(2,1)S(1)}, bf16[256,512]{1,0:T(8,128)(2,1)S(1)}, u32[]{:S(2)}, u32[]{:S(2)}) %collective-permute-start.7) | collective-permute-done | bytes 262176 | tf_op jit(solution)/shard_map/reduce/ppermute | solution.py:253
  52.7 1.0 %copy-done.5 = bf16[512,512]{1,0:T(8,128)(2,1)S(1)} copy-done((bf16[512,512]{1,0:T(8,128)(2,1)S(1)}, bf16[512,512]{1,0:T(8,128)(2,1)}, u32[]{:S(2)}) %copy-start.5) | copy-done | bytes 524312
  53.7 4.4 %attend.3 = (bf16[256,512]{1,0:T(8,128)(2,1)S(1)}, bf16[256,512]{1,0:T(8,128)(2,1)}, bf16[256,512]{1,0:T(8,128)(2,1)S(1)}, bf16[256,512]{1,0:T(8,128)(2,1)S(1)}) custom-call(s32[1]{0:T(128)S(6)} %copy.14.held_ref, s32[1]{0:T(128)S(6)} %copy.13.span_ref, bf16[512,512]{1,0:T(8,128)(2,1)S(1)} %copy-done.5, bf16[512,256]{1,0:T(8,128)(2,1)S(1)} %get-tuple-element.30.kv_ref, ...), custom_call_target="tpu_custom_call" | custom-call | flops 1024 | bytes 1024 | tf_op jit(solution)/shard_map/attend/attend/pallas_call | solution.py:217
  59.7 9.4 %all-to-all-start.1 = ((bf16[8,64,256]{2,1,0:T(8,128)(2,1)}), bf16[8,64,256]{2,1,0:T(8,128)(2,1)S(1)}, u32[]{:S(2)}, u32[]{:S(2)}) async-start(bf16[8,64,256]{2,1,0:T(8,128)(2,1)} %bitcast.4), calls=%async_computation.1 | async-start | bytes 524288 | tf_op jit(solution)/shard_map/extend/all_to_all | solution.py:256
  69.6 1.5 %collective-permute-start.8 = (bf16[256,512]{1,0:T(8,128)(2,1)}, bf16[256,512]{1,0:T(8,128)(2,1)S(1)}, u32[]{:S(2)}, u32[]{:S(2)}) collective-permute-start(bf16[256,512]{1,0:T(8,128)(2,1)} %add_convert_fusion.1), channel_id=1, source_target_pairs={{0,2},{1,3},{2,0},{3,1},{4,6},{5,7},{6,4},{7,5},{8,10},{9,11},{10,... | collective-permute-start | bytes 786440 | tf_op jit(solution)/shard_map/reduce/ppermute | solution.py:253
  71.8 6.8 %all-to-all-done.1 = bf16[8,64,256]{2,1,0:T(8,128)(2,1)S(1)} async-done(((bf16[8,64,256]{2,1,0:T(8,128)(2,1)}), bf16[8,64,256]{2,1,0:T(8,128)(2,1)S(1)}, u32[]{:S(2)}, u32[]{:S(2)}) %all-to-all-start.1) | async-done | bytes 262176 | tf_op jit(solution)/shard_map/extend/all_to_all | solution.py:256
  79.0 4.7 %collective-permute-done.11.refs_5_ = bf16[256,512]{1,0:T(8,128)(2,1)S(1)} collective-permute-done((bf16[256,512]{1,0:T(8,128)(2,1)S(1)}, bf16[256,512]{1,0:T(8,128)(2,1)S(1)}, u32[]{:S(2)}, u32[]{:S(2)}) %collective-permute-start.11) | collective-permute-done | bytes 262176 | tf_op jit(solution)/shard_map/reduce/ppermute | solution.py:253
  83.8 0.9 %copy-done.14 = bf16[256,512]{1,0:T(8,128)(2,1)S(1)} copy-done((bf16[256,512]{1,0:T(8,128)(2,1)S(1)}, bf16[256,512]{1,0:T(8,128)(2,1)}, u32[]{:S(2)}) %copy-start.14) | copy-done | bytes 262168
  84.7 1.1 %finish.1 = bf16[512,512]{1,0:T(8,128)(2,1)} custom-call(s32[1]{0:T(128)S(6)} %copy.13.span_ref, bf16[512,512]{1,0:T(8,128)(2,1)S(1)} %copy-done.3, bf16[256,512]{1,0:T(8,128)(2,1)S(1)} %get-tuple-element.32.refs_0_, bf16[256,512]{1,0:T(8,128)(2,1)S(1)} %collective-permute-done.6.refs_1_, bf16[256,512]{1,0:T(8,128)(2,1)S(1)} %collective-permute-done.8.refs_2_, ...), custom_call_target="tpu_custom_call" | custom-call | flops 1024 | bytes 1024 | tf_op jit(solution)/shard_map/finish/finish/pallas_call | solution.py:217
  (53 shorter events, 8.9 us)
Async XLA Ops:
  0.6 15.2 %collective-permute-start.1 = (bf16[512,512]{1,0:T(8,128)(2,1)}, bf16[512,512]{1,0:T(8,128)(2,1)S(1)}, u32[]{:S(2)}, u32[]{:S(2)}) collective-permute-start(bf16[512,512]{1,0:T(8,128)(2,1)} %tokens_ref.1), channel_id=1, source_target_pairs={{0,2},{1,3},{2,0},{3,1},{4,6},{5,7},{6,4},{7,5},{8,10},{9,11},{10,... | collective-permute-start | bytes 1572872 | tf_op jit(solution)/shard_map/tokens_gather/ppermute | solution.py:253
  3.7 12.1 %collective-permute-start = (bf16[512,512]{1,0:T(8,128)(2,1)}, bf16[512,512]{1,0:T(8,128)(2,1)S(1)}, u32[]{:S(2)}, u32[]{:S(2)}) collective-permute-start(bf16[512,512]{1,0:T(8,128)(2,1)} %tokens_ref.1), channel_id=1, source_target_pairs={{0,1},{1,0},{2,3},{3,2},{4,5},{5,4},{6,7},{7,6},{8,9},{9,8},{10,11... | collective-permute-start | bytes 1572872 | tf_op jit(solution)/shard_map/tokens_gather/ppermute | solution.py:253
  15.8 7.7 %copy-start.7 = (bf16[512,512]{1,0:T(8,128)(2,1)}, bf16[512,512]{1,0:T(8,128)(2,1)S(1)}, u32[]{:S(2)}) copy-start(bf16[512,512]{1,0:T(8,128)(2,1)S(1)} %collective-permute-done.1.x2) | copy-start | bytes 1572868
  15.8 6.9 %collective-permute-start.2 = (bf16[512,512]{1,0:T(8,128)(2,1)S(1)}, bf16[512,512]{1,0:T(8,128)(2,1)S(1)}, u32[]{:S(2)}, u32[]{:S(2)}) collective-permute-start(bf16[512,512]{1,0:T(8,128)(2,1)S(1)} %collective-permute-done.1.x2), channel_id=1, source_target_pairs={{0,1},{1,0},{2,3},{3,2},{4,5},{5,4},{6,7},{7,6},{8,9},{9,8},{10,11... | collective-permute-start | bytes 1572872 | tf_op jit(solution)/shard_map/tokens_gather/ppermute | solution.py:253
  16.6 19.8 %all-to-all-start = ((bf16[8,64,256]{2,1,0:T(8,128)(2,1)}), bf16[8,64,256]{2,1,0:T(8,128)(2,1)S(1)}, u32[]{:S(2)}, u32[]{:S(2)}) async-start(bf16[8,64,256]{2,1,0:T(8,128)(2,1)} %param.19), calls=%async_computation | async-start | bytes 524288 | tf_op jit(solution)/shard_map/cache_gather/all_to_all | solution.py:256
  23.5 1.6 %copy-start.1 = (bf16[2048,512]{1,0:T(8,128)(2,1)S(1)}, bf16[2048,512]{1,0:T(8,128)(2,1)}, u32[]{:S(2)}) copy-start(bf16[2048,512]{1,0:T(8,128)(2,1)} %param.12) | copy-start | bytes 6291460
  25.1 1.0 %copy-start.2 = (bf16[512,512]{1,0:T(8,128)(2,1)S(1)}, bf16[512,512]{1,0:T(8,128)(2,1)}, u32[]{:S(2)}) copy-start(bf16[512,512]{1,0:T(8,128)(2,1)} %tokens_ref.1) | copy-start | bytes 1572868
  26.1 1.2 %copy-start.6 = (bf16[2048,256]{1,0:T(8,128)(2,1)S(1)}, bf16[2048,256]{1,0:T(8,128)(2,1)}, u32[]{:S(2)}) copy-start(bf16[2048,256]{1,0:T(8,128)(2,1)} %param.13) | copy-start | bytes 3145732
  27.3 1.0 %copy-start.8 = (bf16[512,512]{1,0:T(8,128)(2,1)S(1)}, bf16[512,512]{1,0:T(8,128)(2,1)}, u32[]{:S(2)}) copy-start(bf16[512,512]{1,0:T(8,128)(2,1)} %copy-done.7) | copy-start | bytes 1572868
  31.1 5.3 %copy-start.16 = (s32[1,8]{1,0:T(1,128)S(1)}, s32[1,8]{1,0:T(1,128)}, u32[]{:S(2)}) copy-start(s32[1,8]{1,0:T(1,128)} %old_ref.1) | copy-start | bytes 100
  31.2 9.2 %copy-start.17 = (s32[1,8]{1,0:T(1,128)S(1)}, s32[1,8]{1,0:T(1,128)}, u32[]{:S(2)}) copy-start(s32[1,8]{1,0:T(1,128)} %new_ref.1) | copy-start | bytes 100
  31.2 15.0 %copy-start = (bf16[512,2048]{1,0:T(8,128)(2,1)S(1)}, bf16[512,2048]{1,0:T(8,128)(2,1)}, u32[]{:S(2)}) copy-start(bf16[512,2048]{1,0:T(8,128)(2,1)} %refs_0_.3) | copy-start | bytes 6291460
  36.5 13.2 %copy-start.4 = (bf16[512,512]{1,0:T(8,128)(2,1)}, bf16[512,512]{1,0:T(8,128)(2,1)S(1)}, u32[]{:S(2)}) copy-start(bf16[512,512]{1,0:T(8,128)(2,1)S(1)} %get-tuple-element.37.q_ref) | copy-start | bytes 1572868
  37.3 3.1 %collective-permute-start.3 = (bf16[384,256]{1,0:T(8,128)(2,1)S(1)}, bf16[384,256]{1,0:T(8,128)(2,1)S(1)}, u32[]{:S(2)}, u32[]{:S(2)}) collective-permute-start(bf16[384,256]{1,0:T(8,128)(2,1)S(1)} %order.1.c0), channel_id=1, source_target_pairs={{0,1},{1,0},{2,3},{3,2},{4,5},{5,4},{6,7},{7,6},{8,9},{9,8},{10,11... | collective-permute-start | bytes 589832 | tf_op jit(solution)/shard_map/cache_gather/ppermute | solution.py:253
  37.6 7.1 %collective-permute-start.4 = (bf16[384,256]{1,0:T(8,128)(2,1)S(1)}, bf16[384,256]{1,0:T(8,128)(2,1)S(1)}, u32[]{:S(2)}, u32[]{:S(2)}) collective-permute-start(bf16[384,256]{1,0:T(8,128)(2,1)S(1)} %order.1.c0), channel_id=1, source_target_pairs={{0,2},{1,3},{2,0},{3,1},{4,6},{5,7},{6,4},{7,5},{8,10},{9,11},{10,... | collective-permute-start | bytes 589832 | tf_op jit(solution)/shard_map/cache_gather/ppermute | solution.py:253
  44.7 1.4 %collective-permute-start.5 = (bf16[384,256]{1,0:T(8,128)(2,1)S(1)}, bf16[384,256]{1,0:T(8,128)(2,1)S(1)}, u32[]{:S(2)}, u32[]{:S(2)}) collective-permute-start(bf16[384,256]{1,0:T(8,128)(2,1)S(1)} %collective-permute-done.4.c2), channel_id=1, source_target_pairs={{0,1},{1,0},{2,3},{3,2},{4,5},{5,4},{6,7},{7,6},{8,9},{9,8},{10,11... | collective-permute-start | bytes 589832 | tf_op jit(solution)/shard_map/extend/ppermute | solution.py:253
  50.4 1.5 %collective-permute-start.7 = (bf16[256,512]{1,0:T(8,128)(2,1)S(1)}, bf16[256,512]{1,0:T(8,128)(2,1)S(1)}, u32[]{:S(2)}, u32[]{:S(2)}) collective-permute-start(bf16[256,512]{1,0:T(8,128)(2,1)S(1)} %get-tuple-element.35), channel_id=1, source_target_pairs={{0,1},{1,0},{2,3},{3,2},{4,5},{5,4},{6,7},{7,6},{8,9},{9,8},{10,11... | collective-permute-start | bytes 786440 | tf_op jit(solution)/shard_map/reduce/ppermute | solution.py:253
  53.7 30.1 %copy-start.3 = (bf16[512,512]{1,0:T(8,128)(2,1)S(1)}, bf16[512,512]{1,0:T(8,128)(2,1)}, u32[]{:S(2)}) copy-start(bf16[512,512]{1,0:T(8,128)(2,1)} %tokens_ref.1) | copy-start | bytes 1572868
  59.5 11.6 %collective-permute-start.10 = (bf16[256,512]{1,0:T(8,128)(2,1)}, bf16[256,512]{1,0:T(8,128)(2,1)S(1)}, u32[]{:S(2)}, u32[]{:S(2)}) collective-permute-start(bf16[256,512]{1,0:T(8,128)(2,1)} %get-tuple-element.41), channel_id=1, source_target_pairs={{0,1},{1,0},{2,3},{3,2},{4,5},{5,4},{6,7},{7,6},{8,9},{9,8},{10,11... | collective-permute-start | bytes 786440 | tf_op jit(solution)/shard_map/reduce/ppermute | solution.py:253
  59.7 18.9 %all-to-all-start.1 = ((bf16[8,64,256]{2,1,0:T(8,128)(2,1)}), bf16[8,64,256]{2,1,0:T(8,128)(2,1)S(1)}, u32[]{:S(2)}, u32[]{:S(2)}) async-start(bf16[8,64,256]{2,1,0:T(8,128)(2,1)} %bitcast.4), calls=%async_computation.1 | async-start | bytes 524288 | tf_op jit(solution)/shard_map/extend/all_to_all | solution.py:256
  69.1 9.4 %collective-permute-start.6 = (bf16[256,512]{1,0:T(8,128)(2,1)}, bf16[256,512]{1,0:T(8,128)(2,1)S(1)}, u32[]{:S(2)}, u32[]{:S(2)}) collective-permute-start(bf16[256,512]{1,0:T(8,128)(2,1)} %copy-done.18), channel_id=1, source_target_pairs={{0,1},{1,0},{2,3},{3,2},{4,5},{5,4},{6,7},{7,6},{8,9},{9,8},{10,11... | collective-permute-start | bytes 786440 | tf_op jit(solution)/shard_map/reduce/ppermute | solution.py:253
  69.2 9.4 %collective-permute-start.9 = (bf16[256,512]{1,0:T(8,128)(2,1)}, bf16[256,512]{1,0:T(8,128)(2,1)S(1)}, u32[]{:S(2)}, u32[]{:S(2)}) collective-permute-start(bf16[256,512]{1,0:T(8,128)(2,1)} %copy-done.19), channel_id=1, source_target_pairs={{0,1},{1,0},{2,3},{3,2},{4,5},{5,4},{6,7},{7,6},{8,9},{9,8},{10,11... | collective-permute-start | bytes 786440 | tf_op jit(solution)/shard_map/reduce/ppermute | solution.py:253
  69.6 9.4 %collective-permute-start.8 = (bf16[256,512]{1,0:T(8,128)(2,1)}, bf16[256,512]{1,0:T(8,128)(2,1)S(1)}, u32[]{:S(2)}, u32[]{:S(2)}) collective-permute-start(bf16[256,512]{1,0:T(8,128)(2,1)} %add_convert_fusion.1), channel_id=1, source_target_pairs={{0,2},{1,3},{2,0},{3,1},{4,6},{5,7},{6,4},{7,5},{8,10},{9,11},{10,... | collective-permute-start | bytes 786440 | tf_op jit(solution)/shard_map/reduce/ppermute | solution.py:253
  71.2 12.5 %collective-permute-start.11 = (bf16[256,512]{1,0:T(8,128)(2,1)S(1)}, bf16[256,512]{1,0:T(8,128)(2,1)S(1)}, u32[]{:S(2)}, u32[]{:S(2)}) collective-permute-start(bf16[256,512]{1,0:T(8,128)(2,1)S(1)} %add_convert_fusion), channel_id=1, source_target_pairs={{0,2},{1,3},{2,0},{3,1},{4,6},{5,7},{6,4},{7,5},{8,10},{9,11},{10,... | collective-permute-start | bytes 786440 | tf_op jit(solution)/shard_map/reduce/ppermute | solution.py:253
  (10 other events, 8.5 us)

commit v4 on v3

--- a/solution.py
+++ b/solution.py
@@ -13,7 +13,8 @@
 CHUNKS = 2
 ROW_TILE = 128
 KEY_TILE = 128
-NORM_STEPS = 4
+NORM_ROWS = 128
+SAFE = 60.0
 F32 = jnp.float32
 BF16 = jnp.bfloat16
 
@@ -67,14 +68,12 @@
 
 
 def project_kernel(
-    x0, x1, x2, x3, gain_ref, wq_hbm, wkv_hbm, q_ref, kv_ref, normed, wq, wkv, q_acc, kv_acc, sems
+    x0, x1, x2, x3, gain_ref, wq_hbm, wkv_hbm, q_ref, kv_ref, normed, wq, wkv, sems
 ):
     pieces = (x0, x1, x2, x3)
     me = lax.axis_index("tp")
     rows, width = x0.shape
     features = width * len(pieces)
-    half = rows // 2
-    step_rows = half // NORM_STEPS
     loads = [
         pltpu.make_async_copy(wq_hbm, wq, sems.at[0]),
         pltpu.make_async_copy(wkv_hbm, wkv, sems.at[1]),
@@ -82,8 +81,7 @@
     for load in loads:
         load.start()
 
-    def norm(start):
-        at = pl.ds(pl.multiple_of(start, step_rows), step_rows)
+    def norm(at):
         values = [piece[at, :].astype(F32) for piece in pieces]
         average = jnp.sum(sum(values), axis=1, keepdims=True) / features
         centred = [v - average for v in values]
@@ -92,40 +90,24 @@
         for j, v in enumerate(centred):
             normed[j, at, :] = (v * scale * gain_ref[me ^ j]).astype(BF16)
 
-    def multiply(j, start):
-        left = normed[j, pl.ds(start, half), :]
-        q_acc[...] += dot(left, wq[me ^ j])
-        kv_acc[...] += dot(left, wkv[me ^ j])
-
-    def first(step, carry):
-        norm(step * step_rows)
-        return carry
-
-    def both(step, carry):
-        norm(half + step * step_rows)
-        multiply(step, 0)
-        return carry
-
-    def last(step, carry):
-        multiply(step, half)
-        return carry
-
-    lax.fori_loop(0, NORM_STEPS, first, 0)
-    for load in loads:
-        load.wait()
-    for start, run in ((0, both), (half, last)):
-        q_acc[...] = jnp.zeros_like(q_acc)
-        kv_acc[...] = jnp.zeros_like(kv_acc)
-        lax.fori_loop(0, len(pieces), run, 0)
-        q_ref[pl.ds(start, half), :] = q_acc[...].astype(BF16)
-        kv_ref[pl.ds(start, half), :] = kv_acc[...].astype(BF16)
+    half = rows // 2
+    for start in range(0, rows, half):
+        for step in range(start, start + half, NORM_ROWS):
+            norm(pl.ds(step, NORM_ROWS))
+        if start == 0:
+            for load in loads:
+                load.wait()
+        at = pl.ds(start, half)
+        left = [normed[j, at, :] for j in range(len(pieces))]
+        q_ref[at, :] = sum(dot(x, wq[me ^ j]) for j, x in enumerate(left)).astype(BF16)
+        kv_ref[at, :] = sum(dot(x, wkv[me ^ j]) for j, x in enumerate(left)).astype(BF16)
 
 
 def attend_kernel(
     share, block_rows, start_row, rows, held_ref, span_ref, q_ref, kv_ref, c0, c1, c2, c3, *refs
 ):
     wout_hbm, far_refs, near_refs = refs[0], refs[1:3], refs[3:5]
-    keys, values, context, wout, sem = refs[5:]
+    keys, values, stacked, total, high, context, wout, sem = refs[5:]
     pieces = (c0, c1, c2, c3)
     me = lax.axis_index("tp")
     held, span = held_ref[0], span_ref[0]
@@ -137,58 +119,93 @@
     load = pltpu.make_async_copy(wout_hbm, wout, sem)
     load.start()
 
+    group = KEY_TILE * len(pieces)
+    tiles = (held + group - 1) // group
     spare = kv_ref[0:1, :hd].astype(F32)
     row = lax.broadcasted_iota(jnp.int32, (KEY_TILE, hd), 0)
     place = row // share * block_rows + row % share
-    group = KEY_TILE * len(pieces)
+    longest = jnp.zeros((KEY_TILE, 1), F32)
     for i in range(piece_rows // KEY_TILE):
         for j, piece in enumerate(pieces):
             at = pl.ds(i * group + j * KEY_TILE, KEY_TILE)
             source = pl.ds(i * KEY_TILE, KEY_TILE)
             used = place + (me ^ j) * share + i * group < held
-            keys[at, :] = jnp.where(used, piece[source, :hd].astype(F32), spare).astype(BF16)
+            key = jnp.where(used, piece[source, :hd].astype(F32), spare)
+            longest = jnp.maximum(longest, jnp.sum(key * key, axis=1, keepdims=True))
+            keys[at, :] = key.astype(BF16)
             values[at, hd:] = jnp.where(used, piece[source, hd:].astype(F32), 0.0).astype(BF16)
             values[at, :hd] = jnp.where(used, 1.0, 0.0).astype(BF16)
-    at = pl.ds(cached, known)
-    keys[at, :] = kv_ref[:known, :hd]
-    values[at, hd:] = kv_ref[:known, hd:]
-    values[at, :hd] = jnp.ones((known, hd), BF16)
-
+    for start in range(0, known, KEY_TILE):
+        at = pl.ds(cached + start, KEY_TILE)
+        source = pl.ds(start, KEY_TILE)
+        key = kv_ref[source, :hd].astype(F32)
+        longest = jnp.maximum(longest, jnp.sum(key * key, axis=1, keepdims=True))
+        keys[at, :] = kv_ref[source, :hd]
+        values[at, hd:] = kv_ref[source, hd:]
+        values[at, :hd] = jnp.ones((KEY_TILE, hd), BF16)
+
+    tile = min(ROW_TILE, rows)
+    for start in range(0, rows, tile):
+        for h in range(heads):
+            stacked[pl.ds(start * heads + h * tile, tile), :] = q_ref[
+                pl.ds(start_row + start, tile), h * hd : (h + 1) * hd
+            ]
+    query = stacked[...].astype(F32)
+    widest = jnp.max(jnp.sum(query * query, axis=1, keepdims=True))
     factor = hd ** (-0.5) * math.log2(math.e)
-    tile = min(ROW_TILE, rows)
-
-    def soften(start, used):
-        parts = [pl.ds(0, used)]
-        if start_row + start:
-            parts.append(pl.ds(cached, start_row + start))
-        own = pl.ds(cached + start_row + start, tile)
-        q4 = jnp.concatenate(
-            [
-                q_ref[pl.ds(start_row + start, tile), h * hd : (h + 1) * hd]
-                for h in range(heads)
-            ],
-            axis=0,
-        )
-        scores = [dot_t(q4, keys[part, :]) for part in parts]
-        last = dot_t(q4, keys[own, :])
-        to = lax.broadcasted_iota(jnp.int32, (heads * tile, tile), 0) % tile
-        by = lax.broadcasted_iota(jnp.int32, (heads * tile, tile), 1)
-        scores.append(jnp.where(by <= to, last, MASKED))
-        high = functools.reduce(jnp.maximum, [jnp.max(s, axis=1, keepdims=True) for s in scores])
-        both = sum(
-            dot(jnp.exp2((s - high) * factor).astype(BF16), values[part, :])
-            for s, part in zip(scores, parts + [own])
-        )
-        out = (both[:, hd:] / both[:, :hd]).astype(BF16)
+    small = widest * jnp.max(longest) * (1.0 / hd) < SAFE * SAFE
+
+    total[...] = jnp.zeros_like(total)
+    all_rows = rows * heads
+
+    def weigh(at, part, shifted, mask=None):
+        scores = dot_t(stacked[at, :], keys[part, :])
+        if mask is not None:
+            scores = jnp.where(mask, scores, MASKED)
+        if shifted:
+            scores = scores - high[at, :1]
+        weights = jnp.exp2(scores * factor).astype(BF16)
+        total[at, :] += dot(weights, values[part, :])
+
+    def raise_high(at, part, mask=None):
+        scores = dot_t(stacked[at, :], keys[part, :])
+        if mask is not None:
+            scores = jnp.where(mask, scores, MASKED)
+        high[at, :] = jnp.maximum(high[at, :], jnp.max(scores, axis=1, keepdims=True))
+
+    def over_keys(use):
+        def one(i, carry):
+            use(pl.ds(0, all_rows), pl.ds(pl.multiple_of(i * group, group), group))
+            return carry
+
+        lax.fori_loop(0, tiles, one, 0)
+        if start_row:
+            use(pl.ds(0, all_rows), pl.ds(cached, start_row))
+        for start in range(0, rows, tile):
+            at = pl.ds(start * heads, tile * heads)
+            if start:
+                use(at, pl.ds(cached + start_row, start))
+            to = lax.broadcasted_iota(jnp.int32, (heads * tile, tile), 0) % tile
+            by = lax.broadcasted_iota(jnp.int32, (heads * tile, tile), 1)
+            use(at, pl.ds(cached + start_row + start, tile), mask=by <= to)
+
+    busy = start_row < span
+
+    @pl.when(busy & small)
+    def _():
+        over_keys(functools.partial(weigh, shifted=False))
+
+    @pl.when(busy & jnp.logical_not(small))
+    def _():
+        high[...] = jnp.full_like(high, MASKED)
+        over_keys(raise_high)
+        over_keys(functools.partial(weigh, shifted=True))
+
+    for start in range(0, rows, tile):
         for h in range(heads):
-            context[pl.ds(start, tile), h * hd : (h + 1) * hd] = out[h * tile : (h + 1) * tile]
-
-    context[...] = jnp.zeros_like(context)
-    for start in range(0, rows, tile):
-        for used in range(group, cached + 1, group):
-            fits = held <= used if used < cached else True
-            needed = (held > used - group) & fits & (start_row + start < span)
-            pl.when(needed)(functools.partial(soften, start, used))
+            both = total[pl.ds(start * heads + h * tile, tile), :]
+            out = both[:, hd:] / both[:, :hd]
+            context[pl.ds(start, tile), h * hd : (h + 1) * hd] = out.astype(BF16)
 
     load.wait()
     cols = wout.shape[1] // 4
@@ -213,15 +230,17 @@
         out_ref[at, :] = jnp.where(row < span_ref[0], total, 0.0).astype(BF16)
 
 
-def call(kernel, out_shape, in_specs, args, mib, scratch=(), name=None):
+def call(kernel, out_shape, in_specs, args, flops, scratch=(), exps=0, name=None):
+    outs = out_shape if isinstance(out_shape, (list, tuple)) else [out_shape]
+    moved = sum(a.size * a.dtype.itemsize for a in list(args) + list(outs))
     return pl.pallas_call(
         kernel,
         out_shape=out_shape,
         in_specs=in_specs,
         out_specs=jax.tree.map(lambda _: VMEM, out_shape),
         scratch_shapes=list(scratch),
-        cost_estimate=pl.CostEstimate(flops=1024, bytes_accessed=1024, transcendentals=0),
-        compiler_params=pltpu.CompilerParams(vmem_limit_bytes=mib * 1024 * 1024),
+        cost_estimate=pl.CostEstimate(flops=flops, bytes_accessed=moved, transcendentals=exps),
+        compiler_params=pltpu.CompilerParams(vmem_limit_bytes=51 * 1024 * 1024),
         name=name,
     )(*args)
 
@@ -258,13 +277,24 @@
     with jax.named_scope("tokens_gather"):
         across = swap(tokens, 2)
         beside = swap(tokens, 1)
-        corner = swap(across, 1)
 
     with jax.named_scope("cache_gather"):
         beside, stored = lax.optimization_barrier((beside, old_cache))
         arrived = exchange(stored).reshape(groups * share, width)
+        arrived, across = lax.optimization_barrier((arrived, across))
+        ordered = call(
+            functools.partial(order_kernel, share),
+            jax.ShapeDtypeStruct((piece_rows, width), BF16),
+            [SMEM, VMEM],
+            (old_table, arrived),
+            flops=2 * piece_rows * groups * share * width,
+            name="order",
+        )
+        c_across = swap(ordered, 2)
+        c_beside = swap(ordered, 1)
 
     with jax.named_scope("project"):
+        corner = swap(across, 1)
         query, keyval = call(
             project_kernel,
             [
@@ -281,44 +311,28 @@
                 w_query.reshape(tp, cols, q_cols),
                 w_keyval.reshape(tp, cols, width),
             ),
-            mib=24,
+            flops=2 * rows * features * (q_cols + width),
             scratch=[
                 pltpu.VMEM((tp, rows, cols), BF16),
                 pltpu.VMEM((tp, cols, q_cols), BF16),
                 pltpu.VMEM((tp, cols, width), BF16),
-                pltpu.VMEM((rows // 2, q_cols), F32),
-                pltpu.VMEM((rows // 2, width), F32),
                 pltpu.SemaphoreType.DMA((2,)),
             ],
             name="project",
         )
-
-    with jax.named_scope("cache_gather"):
-        keyval, arrived = lax.optimization_barrier((keyval, arrived))
-        ordered = call(
-            functools.partial(order_kernel, share),
-            jax.ShapeDtypeStruct((piece_rows, width), BF16),
-            [SMEM, VMEM],
-            (old_table, arrived),
-            mib=8,
-            name="order",
-        )
-        c_across = swap(ordered, 2)
-        c_beside = swap(ordered, 1)
+        keyval, c_across = lax.optimization_barrier((keyval, c_across))
+        cached = (ordered, c_beside, c_across, swap(c_across, 1))
 
     with jax.named_scope("extend"):
-        kv_later, c_beside = lax.optimization_barrier((keyval, c_beside))
         sent = call(
             functools.partial(extend_kernel, share, block_rows),
             jax.ShapeDtypeStruct((groups * share, width), BF16),
             [SMEM] * 4 + [VMEM] * 2,
-            (old_table, new_table, cached_lens, span_lens, arrived, kv_later),
-            mib=8,
+            (old_table, new_table, cached_lens, span_lens, arrived, keyval),
+            flops=4 * groups * share * groups * share * width,
             name="extend",
         )
-        sent, c_across = lax.optimization_barrier((sent, c_across))
         new_cache = exchange(sent.reshape(groups, share, width))
-        cached = (ordered, c_beside, c_across, swap(c_across, 1))
 
     part = rows // CHUNKS
     sums = []
@@ -330,10 +344,14 @@
                 [jax.ShapeDtypeStruct((part, cols), BF16)] * 4,
                 [SMEM] * 2 + [VMEM] * 6 + [HBM],
                 (cached_lens, span_lens, query, keyval, *cached, w_out),
-                    mib=24,
+                flops=4 * part * seen * q_cols + 2 * part * q_cols * features,
+                exps=part * seen * (q_cols // hd),
                 scratch=[
                     pltpu.VMEM((seen, hd), BF16),
                     pltpu.VMEM((seen, width), BF16),
+                    pltpu.VMEM((part * (q_cols // hd), hd), BF16),
+                    pltpu.VMEM((part * (q_cols // hd), width), F32),
+                    pltpu.VMEM((part * (q_cols // hd), hd), F32),
                     pltpu.VMEM((part, q_cols), BF16),
                     pltpu.VMEM(w_out.shape, BF16),
                     pltpu.SemaphoreType.DMA,
@@ -351,7 +369,7 @@
             jax.ShapeDtypeStruct((rows, cols), BF16),
             [SMEM] + [VMEM] * (1 + len(sums)),
             (span_lens, tokens, *sums),
-            mib=8,
+            flops=4 * rows * cols,
             name="finish",
         )
     return (mixed, new_cache)

time: 86.1 us -> 67.4 us (0.78); the launches traced: 86.5 us -> 66.2 us
  local copies, waits for them, and re-layouts: 14.1 us -> 3.12 us
  waiting for transfers between devices: 29.3 us -> 21.5 us
  Pallas kernels: 17 us -> 14.8 us
    unnamed x41 -> x13, local copies, waits for them, and re-layouts: 14.1 us -> 3.12 us
    ppermute x12, waiting for transfers between devices: 22.5 us -> 12.7 us  [swap(): return lax.ppermute(x, 'tp', [(i, i ^ bit) for i in range(tp)])]
    pallas_call x6, Pallas kernels: 17 us -> 14.8 us  [call(): pl.pallas_call(kernel, out_shape=out_shape, in_specs=in_specs, out_specs=...]
    all_to_all x2, waiting for transfers between devices: 6.77 us -> 8.84 us  [exchange(): return lax.all_to_all(x, 'seq', split_axis=0, concat_axis=0, tiled=True)]
  transfers between devices with their start and end apart: 14 -> 14, of which waited for: 7 -> 5; matrix products, arithmetic and copies ran while one was open for 0% -> 2% of each run, Pallas kernels for 8% -> 10%
where the time goes in v4:
time: 67.4 us; the launch traced here: 66.2 us
  starting transfers between devices  23.7 us (35%)
  waiting for transfers between devices  21.5 us (32%)
  Pallas kernels  14.8 us (22%)
  local copies, waits for them, and re-layouts  3.12 us (5%)
  between operations  2.04 us (3%)
  other arithmetic  1.08 us (2%)
    all_to_all x2, starting transfers between devices, exchange(): return lax.all_to_all(x, 'seq', split_axis=0, concat_axis=0, tiled=True)  15.5 us
    pallas_call x6, Pallas kernels, call(): pl.pallas_call(kernel, out_shape=out_shape, in_specs=in_specs, out_specs=...  14.8 us
    ppermute x12, waiting for transfers between devices, swap(): return lax.ppermute(x, 'tp', [(i, i ^ bit) for i in range(tp)])  12.7 us
    all_to_all x2, waiting for transfers between devices, exchange(): return lax.all_to_all(x, 'seq', split_axis=0, concat_axis=0, tiled=True)  8.84 us
    ppermute x12, starting transfers between devices, swap(): return lax.ppermute(x, 'tp', [(i, i ^ bit) for i in range(tp)])  8.18 us
    unnamed x13, local copies, waits for them, and re-layouts  3.12 us
  transfers between devices with their start and end apart: 14, of which 5 were waited for; matrix products, arithmetic and copies ran while one was open for 2% of the time, Pallas kernels for 10%

profile of v4, /device:TPU:0, one launch (start us, length us, event | category | flops | bytes accessed | tf_op | source)
XLA Modules:
  0.0 66.2 jit_solution(16334526108883088596)
XLA Ops:
  0.6 0.5 collective-permute-start
  1.1 2.6 %collective-permute-start.1 = (bf16[512,512]{1,0:T(8,128)(2,1)}, bf16[512,512]{1,0:T(8,128)(2,1)S(1)}, u32[]{:S(2)}, u32[]{:S(2)}) collective-permute-start(bf16[512,512]{1,0:T(8,128)(2,1)} %tokens_ref.1), channel_id=1, source_target_pairs={{0,2},{1,3},{2,0},{3,1},{4,6},{5,7},{6,4},{7,5},{8,10},{9,11},{10,... | collective-permute-start | bytes 1572872 | tf_op jit(solution)/shard_map/tokens_gather/ppermute | solution.py:272
  3.7 6.3 %all-to-all-start = ((bf16[8,64,256]{2,1,0:T(8,128)(2,1)}), bf16[8,64,256]{2,1,0:T(8,128)(2,1)S(1)}, u32[]{:S(2)}, u32[]{:S(2)}) async-start(bf16[8,64,256]{2,1,0:T(8,128)(2,1)} %param.19), calls=%async_computation | async-start | bytes 524288 | tf_op jit(solution)/shard_map/cache_gather/all_to_all | solution.py:275
  10.1 6.4 %collective-permute-done.1.x2 = bf16[512,512]{1,0:T(8,128)(2,1)S(1)} collective-permute-done((bf16[512,512]{1,0:T(8,128)(2,1)}, bf16[512,512]{1,0:T(8,128)(2,1)S(1)}, u32[]{:S(2)}, u32[]{:S(2)}) %collective-permute-start.1) | collective-permute-done | bytes 524320 | tf_op jit(solution)/shard_map/tokens_gather/ppermute | solution.py:272
  16.5 2.8 %all-to-all-done = bf16[8,64,256]{2,1,0:T(8,128)(2,1)S(1)} async-done(((bf16[8,64,256]{2,1,0:T(8,128)(2,1)}), bf16[8,64,256]{2,1,0:T(8,128)(2,1)S(1)}, u32[]{:S(2)}, u32[]{:S(2)}) %all-to-all-start) | async-done | bytes 262176 | tf_op jit(solution)/shard_map/cache_gather/all_to_all | solution.py:275
  19.3 0.7 copy-done.2
  19.9 0.8 %order.1.c0 = bf16[384,256]{1,0:T(8,128)(2,1)S(1)} custom-call(s32[1,8]{1,0:T(1,128)S(1)} %copy-done.2, bf16[512,256]{1,0:T(8,128)(2,1)S(1)} %bitcast.5), custom_call_target="tpu_custom_call" | custom-call | flops 100663296 | bytes 458784 | tf_op jit(solution)/shard_map/cache_gather/order/pallas_call | solution.py:236
  20.8 1.6 %collective-permute-start.3 = (bf16[384,256]{1,0:T(8,128)(2,1)S(1)}, bf16[384,256]{1,0:T(8,128)(2,1)S(1)}, u32[]{:S(2)}, u32[]{:S(2)}) collective-permute-start(bf16[384,256]{1,0:T(8,128)(2,1)S(1)} %order.1.c0), channel_id=1, source_target_pairs={{0,2},{1,3},{2,0},{3,1},{4,6},{5,7},{6,4},{7,5},{8,10},{9,11},{10,... | collective-permute-start | bytes 589832 | tf_op jit(solution)/shard_map/cache_gather/ppermute | solution.py:272
  22.6 1.0 %copy-done = bf16[512,512]{1,0:T(8,128)(2,1)S(1)} copy-done((bf16[512,512]{1,0:T(8,128)(2,1)S(1)}, bf16[512,512]{1,0:T(8,128)(2,1)}, u32[]{:S(2)}) %copy-start) | copy-done | bytes 524312
  23.6 0.7 %copy-done.4 = f32[2048]{0:T(1024)S(1)} copy-done((f32[2048]{0:T(1024)S(1)}, f32[2048]{0:T(1024)}, u32[]{:S(2)}) %copy-start.4) | copy-done | bytes 8216
  24.3 4.0 %project.1 = (bf16[512,512]{1,0:T(8,128)(2,1)S(1)}, bf16[512,256]{1,0:T(8,128)(2,1)S(1)}) custom-call(bf16[512,512]{1,0:T(8,128)(2,1)S(1)} %copy-done, bf16[512,512]{1,0:T(8,128)(2,1)S(1)} %collective-permute-done.x1, bf16[512,512]{1,0:T(8,128)(2,1)S(1)} %collective-permute-done.1.x2, bf16[512,512]{1,0:T(8,128)(2,1)S(1)} %collective-permute-done.2.x3, ...), custom_call_target="tpu_custom_call" | custom-call | flops 1610612736 | bytes 6037504 | tf_op jit(solution)/shard_map/project/project/pallas_call | solution.py:236
  28.3 0.3 collective-permute-start.5
  30.0 4.1 %attend.2 = (bf16[256,512]{1,0:T(8,128)(2,1)S(1)}, bf16[256,512]{1,0:T(8,128)(2,1)S(1)}, bf16[256,512]{1,0:T(8,128)(2,1)S(1)}, bf16[256,512]{1,0:T(8,128)(2,1)S(1)}) custom-call(s32[1]{0:T(128)S(6)} %copy.14.held_ref, s32[1]{0:T(128)S(6)} %copy.13.span_ref, bf16[512,512]{1,0:T(8,128)(2,1)S(1)} %get-tuple-element.34.q_ref, ...), custom_call_target="tpu_custom_call" | custom-call | flops 1476395008 | bytes 4718600 | tf_op jit(solution)/shard_map/attend/attend/pallas_call | solution.py:236
  34.4 1.3 %collective-permute-done.7 = bf16[256,512]{1,0:T(8,128)(2,1)S(1)} collective-permute-done((bf16[256,512]{1,0:T(8,128)(2,1)S(1)}, bf16[256,512]{1,0:T(8,128)(2,1)S(1)}, u32[]{:S(2)}, u32[]{:S(2)}) %collective-permute-start.7) | collective-permute-done | bytes 262176 | tf_op jit(solution)/shard_map/reduce/ppermute | solution.py:272
  35.8 2.9 %attend.3 = (bf16[256,512]{1,0:T(8,128)(2,1)S(1)}, bf16[256,512]{1,0:T(8,128)(2,1)S(1)}, bf16[256,512]{1,0:T(8,128)(2,1)S(1)}, bf16[256,512]{1,0:T(8,128)(2,1)S(1)}) custom-call(s32[1]{0:T(128)S(6)} %copy.14.held_ref, s32[1]{0:T(128)S(6)} %copy.13.span_ref, bf16[512,512]{1,0:T(8,128)(2,1)S(1)} %get-tuple-element.34.q_ref, ...), custom_call_target="tpu_custom_call" | custom-call | flops 1610612736 | bytes 4718600 | tf_op jit(solution)/shard_map/attend/attend/pallas_call | solution.py:236
  39.0 1.9 %extend.1 = bf16[512,256]{1,0:T(8,128)(2,1)} custom-call(s32[1,8]{1,0:T(1,128)S(1)} %copy-done.3, s32[1,8]{1,0:T(1,128)S(1)} %copy-done.5, s32[1]{0:T(128)S(6)} %copy.14.held_ref, s32[1]{0:T(128)S(6)} %copy.13.span_ref, bf16[512,256]{1,0:T(8,128)(2,1)S(1)} %bitcast.6, bf16[512,256]{1,0:T(8,128)(2,1)S(1)} %get-tuple-element.27.kv_ref), custom_call_target="tpu_custom_call" | custom-call | flops 268435456 | bytes 786504 | tf_op jit(solution)/shard_map/extend/extend/pallas_call | solution.py:236
  40.9 9.2 %all-to-all-start.1 = ((bf16[8,64,256]{2,1,0:T(8,128)(2,1)}), bf16[8,64,256]{2,1,0:T(8,128)(2,1)S(1)}, u32[]{:S(2)}, u32[]{:S(2)}) async-start(bf16[8,64,256]{2,1,0:T(8,128)(2,1)} %bitcast.4), calls=%async_computation.1 | async-start | bytes 524288 | tf_op jit(solution)/shard_map/extend/all_to_all | solution.py:275
  50.1 1.3 %collective-permute-start.8 = (bf16[256,512]{1,0:T(8,128)(2,1)S(1)}, bf16[256,512]{1,0:T(8,128)(2,1)S(1)}, u32[]{:S(2)}, u32[]{:S(2)}) collective-permute-start(bf16[256,512]{1,0:T(8,128)(2,1)S(1)} %add_convert_fusion.1), channel_id=1, source_target_pairs={{0,2},{1,3},{2,0},{3,1},{4,6},{5,7},{6,4},{7,5},{8,10},{9,11},{10,... | collective-permute-start | bytes 786440 | tf_op jit(solution)/shard_map/reduce/ppermute | solution.py:272
  51.6 1.0 %add_convert_fusion = bf16[256,512]{1,0:T(8,128)(2,1)S(1)} fusion(bf16[256,512]{1,0:T(8,128)(2,1)} %collective-permute-done.10, bf16[256,512]{1,0:T(8,128)(2,1)S(1)} %get-tuple-element.37), kind=kLoop, calls=%fused_computation | loop fusion | flops 524288 | bytes 786432 | tf_op jit(solution)/shard_map/reduce/convert_element_type | solution.py:363
  52.6 0.8 %collective-permute-start.11 = (bf16[256,512]{1,0:T(8,128)(2,1)S(1)}, bf16[256,512]{1,0:T(8,128)(2,1)S(1)}, u32[]{:S(2)}, u32[]{:S(2)}) collective-permute-start(bf16[256,512]{1,0:T(8,128)(2,1)S(1)} %add_convert_fusion), channel_id=1, source_target_pairs={{0,2},{1,3},{2,0},{3,1},{4,6},{5,7},{6,4},{7,5},{8,10},{9,11},{10,... | collective-permute-start | bytes 786440 | tf_op jit(solution)/shard_map/reduce/ppermute | solution.py:272
  53.4 6.0 %all-to-all-done.1 = bf16[8,64,256]{2,1,0:T(8,128)(2,1)S(1)} async-done(((bf16[8,64,256]{2,1,0:T(8,128)(2,1)}), bf16[8,64,256]{2,1,0:T(8,128)(2,1)S(1)}, u32[]{:S(2)}, u32[]{:S(2)}) %all-to-all-start.1) | async-done | bytes 262176 | tf_op jit(solution)/shard_map/extend/all_to_all | solution.py:275
  59.4 5.0 %collective-permute-done.11.refs_5_ = bf16[256,512]{1,0:T(8,128)(2,1)S(1)} collective-permute-done((bf16[256,512]{1,0:T(8,128)(2,1)S(1)}, bf16[256,512]{1,0:T(8,128)(2,1)S(1)}, u32[]{:S(2)}, u32[]{:S(2)}) %collective-permute-start.11) | collective-permute-done | bytes 262176 | tf_op jit(solution)/shard_map/reduce/ppermute | solution.py:272
  64.4 1.1 %finish.1 = bf16[512,512]{1,0:T(8,128)(2,1)} custom-call(s32[1]{0:T(128)S(6)} %copy.13.span_ref, bf16[512,512]{1,0:T(8,128)(2,1)S(1)} %copy-done.1, bf16[256,512]{1,0:T(8,128)(2,1)S(1)} %get-tuple-element.29.refs_0_, bf16[256,512]{1,0:T(8,128)(2,1)S(1)} %collective-permute-done.6.refs_1_, bf16[256,512]{1,0:T(8,128)(2,1)S(1)} %collective-permute-done.8.refs_2_, ...), custom_call_target="tpu_custom_call" | custom-call | flops 1048576 | bytes 2621444 | tf_op jit(solution)/shard_map/finish/finish/pallas_call | solution.py:236
  65.5 0.7 %copy.15 = bf16[8,64,256]{2,1,0:T(8,128)(2,1)} copy(bf16[8,64,256]{2,1,0:T(8,128)(2,1)S(1)} %all-to-all-done.1) | data formatting | bytes 524288
  (25 shorter events, 1.1 us)
Async XLA Ops:
  0.6 3.1 %collective-permute-start = (bf16[512,512]{1,0:T(8,128)(2,1)}, bf16[512,512]{1,0:T(8,128)(2,1)S(1)}, u32[]{:S(2)}, u32[]{:S(2)}) collective-permute-start(bf16[512,512]{1,0:T(8,128)(2,1)} %tokens_ref.1), channel_id=1, source_target_pairs={{0,1},{1,0},{2,3},{3,2},{4,5},{5,4},{6,7},{7,6},{8,9},{9,8},{10,11... | collective-permute-start | bytes 1572872 | tf_op jit(solution)/shard_map/tokens_gather/ppermute | solution.py:272
  1.1 15.3 %collective-permute-start.1 = (bf16[512,512]{1,0:T(8,128)(2,1)}, bf16[512,512]{1,0:T(8,128)(2,1)S(1)}, u32[]{:S(2)}, u32[]{:S(2)}) collective-permute-start(bf16[512,512]{1,0:T(8,128)(2,1)} %tokens_ref.1), channel_id=1, source_target_pairs={{0,2},{1,3},{2,0},{3,1},{4,6},{5,7},{6,4},{7,5},{8,10},{9,11},{10,... | collective-permute-start | bytes 1572872 | tf_op jit(solution)/shard_map/tokens_gather/ppermute | solution.py:272
  3.7 15.5 %all-to-all-start = ((bf16[8,64,256]{2,1,0:T(8,128)(2,1)}), bf16[8,64,256]{2,1,0:T(8,128)(2,1)S(1)}, u32[]{:S(2)}, u32[]{:S(2)}) async-start(bf16[8,64,256]{2,1,0:T(8,128)(2,1)} %param.19), calls=%async_computation | async-start | bytes 524288 | tf_op jit(solution)/shard_map/cache_gather/all_to_all | solution.py:275
  19.3 3.3 %collective-permute-start.2 = (bf16[512,512]{1,0:T(8,128)(2,1)S(1)}, bf16[512,512]{1,0:T(8,128)(2,1)S(1)}, u32[]{:S(2)}, u32[]{:S(2)}) collective-permute-start(bf16[512,512]{1,0:T(8,128)(2,1)S(1)} %collective-permute-done.1.x2), channel_id=1, source_target_pairs={{0,1},{1,0},{2,3},{3,2},{4,5},{5,4},{6,7},{7,6},{8,9},{9,8},{10,11... | collective-permute-start | bytes 1572872 | tf_op jit(solution)/shard_map/project/ppermute | solution.py:272
  19.3 0.7 copy-start.2
  20.8 7.6 %collective-permute-start.3 = (bf16[384,256]{1,0:T(8,128)(2,1)S(1)}, bf16[384,256]{1,0:T(8,128)(2,1)S(1)}, u32[]{:S(2)}, u32[]{:S(2)}) collective-permute-start(bf16[384,256]{1,0:T(8,128)(2,1)S(1)} %order.1.c0), channel_id=1, source_target_pairs={{0,2},{1,3},{2,0},{3,1},{4,6},{5,7},{6,4},{7,5},{8,10},{9,11},{10,... | collective-permute-start | bytes 589832 | tf_op jit(solution)/shard_map/cache_gather/ppermute | solution.py:272
  22.3 7.6 %collective-permute-start.4 = (bf16[384,256]{1,0:T(8,128)(2,1)S(1)}, bf16[384,256]{1,0:T(8,128)(2,1)S(1)}, u32[]{:S(2)}, u32[]{:S(2)}) collective-permute-start(bf16[384,256]{1,0:T(8,128)(2,1)S(1)} %order.1.c0), channel_id=1, source_target_pairs={{0,1},{1,0},{2,3},{3,2},{4,5},{5,4},{6,7},{7,6},{8,9},{9,8},{10,11... | collective-permute-start | bytes 589832 | tf_op jit(solution)/shard_map/cache_gather/ppermute | solution.py:272
  22.6 1.0 %copy-start = (bf16[512,512]{1,0:T(8,128)(2,1)S(1)}, bf16[512,512]{1,0:T(8,128)(2,1)}, u32[]{:S(2)}) copy-start(bf16[512,512]{1,0:T(8,128)(2,1)} %tokens_ref.1) | copy-start | bytes 1572868
  23.6 0.7 %copy-start.4 = (f32[2048]{0:T(1024)S(1)}, f32[2048]{0:T(1024)}, u32[]{:S(2)}) copy-start(f32[2048]{0:T(1024)} %param.11) | copy-start | bytes 24580
  28.3 1.7 %collective-permute-start.5 = (bf16[384,256]{1,0:T(8,128)(2,1)S(1)}, bf16[384,256]{1,0:T(8,128)(2,1)S(1)}, u32[]{:S(2)}, u32[]{:S(2)}) collective-permute-start(bf16[384,256]{1,0:T(8,128)(2,1)S(1)} %collective-permute-done.3.c2), channel_id=1, source_target_pairs={{0,1},{1,0},{2,3},{3,2},{4,5},{5,4},{6,7},{7,6},{8,9},{9,8},{10,11... | collective-permute-start | bytes 589832 | tf_op jit(solution)/shard_map/project/ppermute | solution.py:272
  34.1 1.6 %collective-permute-start.7 = (bf16[256,512]{1,0:T(8,128)(2,1)S(1)}, bf16[256,512]{1,0:T(8,128)(2,1)S(1)}, u32[]{:S(2)}, u32[]{:S(2)}) collective-permute-start(bf16[256,512]{1,0:T(8,128)(2,1)S(1)} %get-tuple-element.32), channel_id=1, source_target_pairs={{0,1},{1,0},{2,3},{3,2},{4,5},{5,4},{6,7},{7,6},{8,9},{9,8},{10,11... | collective-permute-start | bytes 786440 | tf_op jit(solution)/shard_map/reduce/ppermute | solution.py:272
  35.7 3.3 %copy-start.3 = (s32[1,8]{1,0:T(1,128)S(1)}, s32[1,8]{1,0:T(1,128)}, u32[]{:S(2)}) copy-start(s32[1,8]{1,0:T(1,128)} %old_ref.1) | copy-start | bytes 100
  35.7 3.2 %copy-start.5 = (s32[1,8]{1,0:T(1,128)S(1)}, s32[1,8]{1,0:T(1,128)}, u32[]{:S(2)}) copy-start(s32[1,8]{1,0:T(1,128)} %new_ref.1) | copy-start | bytes 100
  38.7 25.7 %copy-start.1 = (bf16[512,512]{1,0:T(8,128)(2,1)S(1)}, bf16[512,512]{1,0:T(8,128)(2,1)}, u32[]{:S(2)}) copy-start(bf16[512,512]{1,0:T(8,128)(2,1)} %tokens_ref.1) | copy-start | bytes 1572868
  38.7 12.9 %collective-permute-start.10 = (bf16[256,512]{1,0:T(8,128)(2,1)S(1)}, bf16[256,512]{1,0:T(8,128)(2,1)}, u32[]{:S(2)}, u32[]{:S(2)}) collective-permute-start(bf16[256,512]{1,0:T(8,128)(2,1)S(1)} %get-tuple-element.38), channel_id=1, source_target_pairs={{0,1},{1,0},{2,3},{3,2},{4,5},{5,4},{6,7},{7,6},{8,9},{9,8},{10,11... | collective-permute-start | bytes 786440 | tf_op jit(solution)/shard_map/reduce/ppermute | solution.py:272
  40.9 18.5 %all-to-all-start.1 = ((bf16[8,64,256]{2,1,0:T(8,128)(2,1)}), bf16[8,64,256]{2,1,0:T(8,128)(2,1)S(1)}, u32[]{:S(2)}, u32[]{:S(2)}) async-start(bf16[8,64,256]{2,1,0:T(8,128)(2,1)} %bitcast.4), calls=%async_computation.1 | async-start | bytes 524288 | tf_op jit(solution)/shard_map/extend/all_to_all | solution.py:275
  50.1 9.4 %collective-permute-start.6 = (bf16[256,512]{1,0:T(8,128)(2,1)S(1)}, bf16[256,512]{1,0:T(8,128)(2,1)S(1)}, u32[]{:S(2)}, u32[]{:S(2)}) collective-permute-start(bf16[256,512]{1,0:T(8,128)(2,1)S(1)} %get-tuple-element.30), channel_id=1, source_target_pairs={{0,1},{1,0},{2,3},{3,2},{4,5},{5,4},{6,7},{7,6},{8,9},{9,8},{10,11... | collective-permute-start | bytes 786440 | tf_op jit(solution)/shard_map/reduce/ppermute | solution.py:272
  50.1 9.4 %collective-permute-start.8 = (bf16[256,512]{1,0:T(8,128)(2,1)S(1)}, bf16[256,512]{1,0:T(8,128)(2,1)S(1)}, u32[]{:S(2)}, u32[]{:S(2)}) collective-permute-start(bf16[256,512]{1,0:T(8,128)(2,1)S(1)} %add_convert_fusion.1), channel_id=1, source_target_pairs={{0,2},{1,3},{2,0},{3,1},{4,6},{5,7},{6,4},{7,5},{8,10},{9,11},{10,... | collective-permute-start | bytes 786440 | tf_op jit(solution)/shard_map/reduce/ppermute | solution.py:272
  51.4 8.0 %collective-permute-start.9 = (bf16[256,512]{1,0:T(8,128)(2,1)S(1)}, bf16[256,512]{1,0:T(8,128)(2,1)S(1)}, u32[]{:S(2)}, u32[]{:S(2)}) collective-permute-start(bf16[256,512]{1,0:T(8,128)(2,1)S(1)} %get-tuple-element.36), channel_id=1, source_target_pairs={{0,1},{1,0},{2,3},{3,2},{4,5},{5,4},{6,7},{7,6},{8,9},{9,8},{10,11... | collective-permute-start | bytes 786440 | tf_op jit(solution)/shard_map/reduce/ppermute | solution.py:272
  52.6 11.8 %collective-permute-start.11 = (bf16[256,512]{1,0:T(8,128)(2,1)S(1)}, bf16[256,512]{1,0:T(8,128)(2,1)S(1)}, u32[]{:S(2)}, u32[]{:S(2)}) collective-permute-start(bf16[256,512]{1,0:T(8,128)(2,1)S(1)} %add_convert_fusion), channel_id=1, source_target_pairs={{0,2},{1,3},{2,0},{3,1},{4,6},{5,7},{6,4},{7,5},{8,10},{9,11},{10,... | collective-permute-start | bytes 786440 | tf_op jit(solution)/shard_map/reduce/ppermute | solution.py:272

commit v5 on v4

v5 whole, which is shorter than its diff:
```python
import functools
import math

import jax
import jax.numpy as jnp
from jax import lax
from jax.experimental import pallas as pl
from jax.experimental.pallas import tpu as pltpu
from jax.sharding import PartitionSpec as P

EPSILON = 1e-05
MASKED = -1e30
PART_ROWS = 256
ROW_TILE = 128
KEY_TILE = 128
NORM_ROWS = 128
SAFE = 60.0
F32 = jnp.float32
BF16 = jnp.bfloat16

VMEM = pl.BlockSpec(memory_space=pltpu.VMEM)
SMEM = pl.BlockSpec(memory_space=pltpu.SMEM)
HBM = pl.BlockSpec(memory_space=pltpu.HBM)


def dot(a, b):
    return lax.dot_general(a, b, (((1,), (0,)), ((), ())), preferred_element_type=F32)


def dot_t(a, b):
    return lax.dot_general(a, b, (((1,), (1,)), ((), ())), preferred_element_type=F32)


def order_kernel(share, plan_ref, arrived_ref, out_ref):
    rows, count = out_ref.shape[0], arrived_ref.shape[0]
    row = lax.broadcasted_iota(jnp.int32, (rows, 128), 0)
    block = row // share
    holder = jnp.zeros_like(block)
    for b in range(rows // share):
        holder = jnp.where(block == b, plan_ref[2 + b], holder)
    index = (holder * share + row % share)[:, :1]
    column = lax.broadcasted_iota(jnp.int32, (rows, count), 1)
    pick = jnp.where(column == index, 1.0, 0.0).astype(BF16)
    out_ref[...] = dot(pick, arrived_ref[...]).astype(BF16)


def extend_kernel(share, block_rows, plan_ref, arrived_ref, kv_ref, out_ref):
    rows = arrived_ref.shape[0]
    groups = rows // share
    held, span = plan_ref[0], plan_ref[1]
    row = lax.broadcasted_iota(jnp.int32, (rows, 128), 0)
    target = row // share
    block, holder = jnp.zeros_like(row), jnp.zeros_like(row)
    for b in range(groups):
        hit = target == plan_ref[2 + groups + b]
        block = jnp.where(hit, b, block)
        holder = jnp.where(hit, plan_ref[2 + b], holder)
    position = block * block_rows + lax.axis_index("tp") * share + row % share
    old_row = jnp.where(position < held, holder * share + row % share, -1)[:, :1]
    fresh = position - held
    new_row = jnp.where((fresh >= 0) & (fresh < span), fresh, -1)[:, :1]
    column = lax.broadcasted_iota(jnp.int32, (rows, rows), 1)
    total = dot(jnp.where(column == old_row, 1.0, 0.0).astype(BF16), arrived_ref[...])
    column = lax.broadcasted_iota(jnp.int32, (rows, kv_ref.shape[0]), 1)
    total += dot(jnp.where(column == new_row, 1.0, 0.0).astype(BF16), kv_ref[...])
    out_ref[...] = total.astype(BF16)


def project_kernel(
    x0, x1, x2, x3, gain_ref, wq_hbm, wkv_hbm, q_ref, kv_ref, normed, weights, sems
):
    pieces = (x0, x1, x2, x3)
    me = lax.axis_index("tp")
    rows, width = x0.shape
    features = width * len(pieces)
    q_cols = q_ref.shape[1]
    loads = []
    for j in range(len(pieces)):
        at = pl.ds(j * width, width)
        for hbm, to in ((wq_hbm, pl.ds(0, q_cols)), (wkv_hbm, pl.ds(q_cols, kv_ref.shape[1]))):
            loads.append(
                pltpu.make_async_copy(hbm.at[me ^ j], weights.at[at, to], sems.at[len(loads)])
            )
            loads[-1].start()

    for step in range(0, rows, NORM_ROWS):
        at = pl.ds(step, NORM_ROWS)
        values = [piece[at, :].astype(F32) for piece in pieces]
        average = jnp.sum(sum(values), axis=1, keepdims=True) / features
        centred = [v - average for v in values]
        spread = jnp.sum(sum(v * v for v in centred), axis=1, keepdims=True) / features
        scale = lax.rsqrt(spread + EPSILON)
        for j, v in enumerate(centred):
            normed[at, j * width : (j + 1) * width] = (v * scale * gain_ref[j]).astype(BF16)
    for load in loads:
        load.wait()
    q_ref[...] = dot(normed[...], weights[:, :q_cols]).astype(BF16)
    kv_ref[...] = dot(normed[...], weights[:, q_cols:]).astype(BF16)


def attend_kernel(share, block_rows, plan_ref, q_ref, kv_ref, c0, c1, c2, c3, *refs):
    wout_hbm, far_refs, near_refs = refs[0], refs[1:3], refs[3:5]
    keys, values, stacked, total, high, context, wout, sem = refs[5:]
    pieces = (c0, c1, c2, c3)
    me = lax.axis_index("tp")
    held, span = plan_ref[0], plan_ref[1]
    rows = q_ref.shape[0]
    piece_rows, width = c0.shape
    hd = width // 2
    heads = q_ref.shape[1] // hd
    cached = piece_rows * len(pieces)
    load = pltpu.make_async_copy(wout_hbm, wout, sem)
    load.start()

    ones = jnp.ones((hd, hd), BF16)

    def lengths(x):
        return dot((x * x).astype(BF16), ones)

    group = KEY_TILE * len(pieces)
    tiles = (held + group - 1) // group
    spare = kv_ref[0:1, :hd].astype(F32)
    row = lax.broadcasted_iota(jnp.int32, (KEY_TILE, hd), 0)
    place = row // share * block_rows + row % share
    longest = jnp.zeros((KEY_TILE, hd), F32)
    for i in range(piece_rows // KEY_TILE):
        for j, piece in enumerate(pieces):
            at = pl.ds(i * group + j * KEY_TILE, KEY_TILE)
            source = pl.ds(i * KEY_TILE, KEY_TILE)
            used = place + (me ^ j) * share + i * group < held
            key = jnp.where(used, piece[source, :hd].astype(F32), spare)
            longest = jnp.maximum(longest, lengths(key))
            keys[at, :] = key.astype(BF16)
            values[at, hd:] = jnp.where(used, piece[source, hd:].astype(F32), 0.0).astype(BF16)
            values[at, :hd] = jnp.where(used, 1.0, 0.0).astype(BF16)
    for start in range(0, rows, KEY_TILE):
        at = pl.ds(cached + start, KEY_TILE)
        source = pl.ds(start, KEY_TILE)
        longest = jnp.maximum(longest, lengths(kv_ref[source, :hd].astype(F32)))
        keys[at, :] = kv_ref[source, :hd]
        values[at, hd:] = kv_ref[source, hd:]
        values[at, :hd] = jnp.ones((KEY_TILE, hd), BF16)

    tile = min(ROW_TILE, rows)
    widest = jnp.zeros((tile, hd), F32)
    for start in range(0, rows, tile):
        for h in range(heads):
            piece = q_ref[pl.ds(start, tile), h * hd : (h + 1) * hd]
            widest = jnp.maximum(widest, lengths(piece.astype(F32)))
            stacked[pl.ds(start * heads + h * tile, tile), :] = piece
    factor = hd ** (-0.5) * math.log2(math.e)
    small = jnp.max(widest) * jnp.max(longest) * (1.05 / hd) < SAFE * SAFE

    def weigh(at, part, shifted, mask=None, first=False):
        scores = dot_t(stacked[at, :], keys[part, :])
        if mask is not None:
            scores = jnp.where(mask, scores, MASKED)
        if shifted:
            scores = scores - high[at, :1]
        weights = jnp.exp2(scores * factor).astype(BF16)
        total[at, :] += dot(weights, values[part, :])

    def raise_high(at, part, mask=None):
        scores = dot_t(stacked[at, :], keys[part, :])
        if mask is not None:
            scores = jnp.where(mask, scores, MASKED)
        high[at, :] = jnp.maximum(high[at, :], jnp.max(scores, axis=1, keepdims=True))

    span_rows = tile * heads

    def over_keys(use, begin, end):
        blocks = [pl.ds(start * heads, span_rows) for start in range(begin, end, tile)]

        def one(i, carry):
            for at in blocks:
                use(at, pl.ds(pl.multiple_of(i * group, group), group))
            return carry

        lax.fori_loop(0, tiles, one, 0)
        to = lax.broadcasted_iota(jnp.int32, (span_rows, tile), 0) % tile
        by = lax.broadcasted_iota(jnp.int32, (span_rows, tile), 1)
        for start, at in zip(range(begin, end, tile), blocks):
            if start:
                use(at, pl.ds(cached, start))
            use(at, pl.ds(cached + start, tile), mask=by <= to)

    total[...] = jnp.zeros_like(total)
    for begin in range(0, rows, PART_ROWS):
        end = min(begin + PART_ROWS, rows)
        busy = begin < span

        @pl.when(busy & small)
        def _():
            over_keys(functools.partial(weigh, shifted=False), begin, end)

        @pl.when(busy & jnp.logical_not(small))
        def _():
            high[...] = jnp.full_like(high, MASKED)
            over_keys(raise_high, begin, end)
            over_keys(functools.partial(weigh, shifted=True), begin, end)

    for start in range(0, rows, tile):
        for h in range(heads):
            both = total[pl.ds(start * heads + h * tile, tile), :]
            out = both[:, hd:] / both[:, :hd]
            context[pl.ds(start, tile), h * hd : (h + 1) * hd] = out.astype(BF16)

    load.wait()
    cols = wout.shape[1] // 4
    for k in (3, 1, 2, 0):
        columns = pl.ds(pl.multiple_of((me ^ k) * cols, cols), cols)
        part = dot(context[...], wout[:, columns]).astype(BF16)
        if k & 1:
            far_refs[k >> 1][...] = part
        else:
            near_refs[k >> 1][...] = part


def finish_kernel(plan_ref, tokens_ref, near_ref, got_ref, crossed_ref, out_ref):
    kept = near_ref[...].astype(F32) + got_ref[...].astype(F32)
    total = tokens_ref[...].astype(F32) + (kept + crossed_ref[...].astype(F32))
    row = lax.broadcasted_iota(jnp.int32, total.shape, 0)
    out_ref[...] = jnp.where(row < plan_ref[1], total, 0.0).astype(BF16)


def call(kernel, out_shape, in_specs, args, flops, mib=51, scratch=(), exps=0, name=None):
    outs = out_shape if isinstance(out_shape, (list, tuple)) else [out_shape]
    moved = sum(a.size * a.dtype.itemsize for a in list(args) + list(outs))
    return pl.pallas_call(
        kernel,
        out_shape=out_shape,
        in_specs=in_specs,
        out_specs=jax.tree.map(lambda _: VMEM, out_shape),
        scratch_shapes=list(scratch),
        cost_estimate=pl.CostEstimate(flops=flops, bytes_accessed=moved, transcendentals=exps),
        compiler_params=pltpu.CompilerParams(vmem_limit_bytes=mib * 1024 * 1024),
        name=name,
    )(*args)


def body(
    tokens,
    norm_gain,
    w_query,
    w_keyval,
    w_out,
    span_lens,
    cached_lens,
    old_table,
    new_table,
    old_cache,
):
    tp = lax.axis_size("tp")
    groups, share, width = old_cache.shape
    block_rows = share * tp
    capacity = groups * block_rows
    rows, cols = tokens.shape
    q_cols = w_query.shape[1]
    features = w_query.shape[0]
    hd = width // 2
    most_held = capacity - rows
    piece_rows = most_held // tp

    def swap(x, bit):
        return lax.ppermute(x, "tp", [(i, i ^ bit) for i in range(tp)])

    def exchange(x):
        return lax.all_to_all(x, "seq", split_axis=0, concat_axis=0, tiled=True)

    with jax.named_scope("tokens_gather"):
        plan = jnp.concatenate([cached_lens, span_lens, old_table[0], new_table[0]])
        gain = norm_gain.reshape(tp, cols)
        gain = jnp.concatenate(
            [lax.dynamic_slice_in_dim(gain, lax.axis_index("tp") ^ j, 1) for j in range(tp)]
        ).reshape(tp, 1, cols)
        in_span = lax.broadcasted_iota(jnp.int32, (rows, 1), 0) < span_lens[0]
        own = jnp.where(in_span, tokens, jnp.zeros_like(tokens))
        across = swap(tokens, 2)
        beside = swap(tokens, 1)

    with jax.named_scope("cache_gather"):
        beside, stored, plan = lax.optimization_barrier((beside, old_cache, plan))
        arrived = exchange(stored).reshape(groups * share, width)
        arrived, across, own, gain = lax.optimization_barrier((arrived, across, own, gain))
        ordered = call(
            functools.partial(order_kernel, share),
            jax.ShapeDtypeStruct((piece_rows, width), BF16),
            [SMEM, VMEM],
            (plan, arrived),
            flops=2 * piece_rows * groups * share * width,
            name="order",
        )
        c_across = swap(ordered, 2)
        c_beside = swap(ordered, 1)

    with jax.named_scope("project"):
        corner = swap(across, 1)
        query, keyval = call(
            project_kernel,
            [
                jax.ShapeDtypeStruct((rows, q_cols), BF16),
                jax.ShapeDtypeStruct((rows, width), BF16),
            ],
            [VMEM] * 5 + [HBM] * 2,
            (
                own,
                beside,
                across,
                corner,
                gain,
                w_query.reshape(tp, cols, q_cols),
                w_keyval.reshape(tp, cols, width),
            ),
            flops=2 * rows * features * (q_cols + width),
            scratch=[
                pltpu.VMEM((rows, features), BF16),
                pltpu.VMEM((features, q_cols + width), BF16),
                pltpu.SemaphoreType.DMA((2 * tp,)),
            ],
            name="project",
        )

    with jax.named_scope("extend"):
        sent = call(
            functools.partial(extend_kernel, share, block_rows),
            jax.ShapeDtypeStruct((groups * share, width), BF16),
            [SMEM] + [VMEM] * 2,
            (plan, arrived, keyval),
            flops=4 * groups * share * groups * share * width,
            name="extend",
        )
        sent, c_across = lax.optimization_barrier((sent, c_across))
        cached = (ordered, c_beside, c_across, swap(c_across, 1))

    with jax.named_scope("attend"):
        stacked = rows * (q_cols // hd)
        far0, far1, near0, near1 = call(
            functools.partial(attend_kernel, share, block_rows),
            [jax.ShapeDtypeStruct((rows, cols), BF16)] * 4,
            [SMEM] + [VMEM] * 6 + [HBM],
            (plan, query, keyval, *cached, w_out),
            flops=4 * rows * capacity * q_cols + 2 * rows * q_cols * features,
            exps=stacked * capacity,
            mib=50,
            scratch=[
                pltpu.VMEM((capacity, hd), BF16),
                pltpu.VMEM((capacity, width), BF16),
                pltpu.VMEM((stacked, hd), BF16),
                pltpu.VMEM((stacked, width), F32),
                pltpu.VMEM((stacked, hd), F32),
                pltpu.VMEM((rows, q_cols), BF16),
                pltpu.VMEM(w_out.shape, BF16),
                pltpu.SemaphoreType.DMA,
            ],
            name="attend",
        )

    with jax.named_scope("reduce"):
        got1 = swap(far1, 1)
        pair = (near1.astype(F32) + got1.astype(F32)).astype(BF16)
        pair, sent = lax.optimization_barrier((pair, sent))
        crossed = swap(pair, 2)
        new_cache = exchange(sent.reshape(groups, share, width))

    with jax.named_scope("finish"):
        mixed = call(
            finish_kernel,
            jax.ShapeDtypeStruct((rows, cols), BF16),
            [SMEM] + [VMEM] * 4,
            (plan, own, near0, swap(far0, 1), crossed),
            flops=4 * rows * cols,
            name="finish",
        )
    return (mixed, new_cache)


def solution(mesh):
    in_specs = (
        P("seq", "tp"),
        P(),
        P(None, "tp"),
        P(),
        P("tp", None),
        P("seq"),
        P("seq"),
        P("seq", None),
        P("seq", None),
        P("seq", "tp", None),
    )
    out_specs = (P("seq", "tp"), P("seq", "tp", None))
    return jax.shard_map(body, mesh=mesh, in_specs=in_specs, out_specs=out_specs, check_vma=False)
```

time: 67.4 us -> 62.2 us (0.923); the launches traced: 66.2 us -> 61.7 us
  blocking collectives: 0 us -> 14.1 us
  starting transfers between devices: 23.7 us -> 10.9 us
  waiting for transfers between devices: 21.5 us -> 12.2 us
  Pallas kernels: 14.8 us -> 19 us
  local copies, waits for them, and re-layouts: 3.12 us -> 1.43 us
  other arithmetic: 1.08 us -> 2.09 us
    all_to_all x0 -> x1, blocking collectives: none -> 14.1 us  [exchange(): return lax.all_to_all(x, 'seq', split_axis=0, concat_axis=0, tiled=True)]
    all_to_all x2 -> x1, starting transfers between devices: 15.5 us -> 5.81 us  [exchange(): return lax.all_to_all(x, 'seq', split_axis=0, concat_axis=0, tiled=True)]
    ppermute x12 -> x9, waiting for transfers between devices: 12.7 us -> 7.1 us  [swap(): return lax.ppermute(x, 'tp', [(i, i ^ bit) for i in range(tp)])]
    pallas_call x6 -> x5, Pallas kernels: 14.8 us -> 19 us  [call(): pl.pallas_call(kernel, out_shape=out_shape, in_specs=in_specs, out_specs=...]
    all_to_all x2 -> x1, waiting for transfers between devices: 8.84 us -> 5.1 us  [exchange(): return lax.all_to_all(x, 'seq', split_axis=0, concat_axis=0, tiled=True)]
    ppermute x12 -> x9, starting transfers between devices: 8.18 us -> 5.06 us  [swap(): return lax.ppermute(x, 'tp', [(i, i ^ bit) for i in range(tp)])]
    unnamed x13 -> x1, local copies, waits for them, and re-layouts: 3.12 us -> 0.7 us
    select_n x0 -> x1, other arithmetic: none -> 1.18 us  [body(): own = jnp.where(in_span, tokens, jnp.zeros_like(tokens))]
  transfers between devices with their start and end apart: 14 -> 10, of which waited for: 5 -> 6; matrix products, arithmetic and copies ran while one was open for 2% -> 5% of each run, Pallas kernels for 10% -> 10%
where the time goes in v5:
time: 62.2 us; the launch traced here: 61.7 us
  Pallas kernels  19 us (31%)
  blocking collectives  14.1 us (23%)
  waiting for transfers between devices  12.2 us (20%)
  starting transfers between devices  10.9 us (18%)
  other arithmetic  2.09 us (3%)
  between operations  2 us (3%)
  local copies, waits for them, and re-layouts  1.43 us (2%)
    pallas_call x5, Pallas kernels, call(): pl.pallas_call(kernel, out_shape=out_shape, in_specs=in_specs, out_specs=...  19 us
    all_to_all x1, blocking collectives, exchange(): return lax.all_to_all(x, 'seq', split_axis=0, concat_axis=0, tiled=True)  14.1 us
    ppermute x9, waiting for transfers between devices, swap(): return lax.ppermute(x, 'tp', [(i, i ^ bit) for i in range(tp)])  7.1 us
    all_to_all x1, starting transfers between devices, exchange(): return lax.all_to_all(x, 'seq', split_axis=0, concat_axis=0, tiled=True)  5.81 us
    all_to_all x1, waiting for transfers between devices, exchange(): return lax.all_to_all(x, 'seq', split_axis=0, concat_axis=0, tiled=True)  5.1 us
    ppermute x9, starting transfers between devices, swap(): return lax.ppermute(x, 'tp', [(i, i ^ bit) for i in range(tp)])  5.06 us
  transfers between devices with their start and end apart: 10, of which 6 were waited for; matrix products, arithmetic and copies ran while one was open for 5% of the time, Pallas kernels for 10%

profile of v5, /device:TPU:0, one launch (start us, length us, event | category | flops | bytes accessed | tf_op | source)
XLA Modules:
  0.0 61.7 jit_solution(15511039537799813165)
XLA Ops:
  0.6 0.5 collective-permute-start
  1.1 2.6 %collective-permute-start.1 = (bf16[512,512]{1,0:T(8,128)(2,1)}, bf16[512,512]{1,0:T(8,128)(2,1)S(1)}, u32[]{:S(2)}, u32[]{:S(2)}) collective-permute-start(bf16[512,512]{1,0:T(8,128)(2,1)} %param.10), channel_id=1, source_target_pairs={{0,2},{1,3},{2,0},{3,1},{4,6},{5,7},{6,4},{7,5},{8,10},{9,11},{10,... | collective-permute-start | bytes 1572872 | tf_op jit(solution)/shard_map/tokens_gather/ppermute | solution.py:265
  5.0 0.7 %reshape.28 = f32[4,512]{1,0:T(4,128)S(1)} reshape(f32[2048]{0:T(1024)} %param.11) | data formatting | bytes 16384 | tf_op jit(solution)/shard_map/tokens_gather/reshape | solution.py:272
  5.8 0.8 %pad_add_fusion.plan_ref = s32[18]{0:T(128)S(1)} fusion(s32[8]{0:T(128)} %bitcast.11, s32[8]{0:T(128)} %bitcast.12, s32[1]{0:T(128)} %copy.13, s32[1]{0:T(128)S(6)} %copy.14), kind=kLoop, calls=%fused_computation.8 | loop fusion | flops 54 | bytes 144 | tf_op jit(solution)/shard_map/tokens_gather/concatenate | solution.py:271
  6.5 5.8 %all-to-all-start = ((bf16[8,64,256]{2,1,0:T(8,128)(2,1)}), bf16[8,64,256]{2,1,0:T(8,128)(2,1)S(1)}, u32[]{:S(2)}, u32[]{:S(2)}) async-start(bf16[8,64,256]{2,1,0:T(8,128)(2,1)} %param.19), calls=%async_computation | async-start | bytes 524288 | tf_op jit(solution)/shard_map/cache_gather/all_to_all | solution.py:268
  12.4 1.2 %broadcast_select_fusion.x0.tokens_ref = bf16[512,512]{1,0:T(8,128)(2,1)S(1)} fusion(bf16[512,512]{1,0:T(8,128)(2,1)} %param.10, pred[512]{0:T(512)(128)(4,1)S(1)} %iota_compare_fusion), kind=kLoop, calls=%fused_computation.1 | loop fusion | flops 262144 | bytes 1049088 | tf_op jit(solution)/shard_map/tokens_gather/jit(_where)/select_n | solution.py:277
  13.6 2.9 %collective-permute-done.1.x2 = bf16[512,512]{1,0:T(8,128)(2,1)S(1)} collective-permute-done((bf16[512,512]{1,0:T(8,128)(2,1)}, bf16[512,512]{1,0:T(8,128)(2,1)S(1)}, u32[]{:S(2)}, u32[]{:S(2)}) %collective-permute-start.1) | collective-permute-done | bytes 524320 | tf_op jit(solution)/shard_map/tokens_gather/ppermute | solution.py:265
  16.5 5.1 %all-to-all-done = bf16[8,64,256]{2,1,0:T(8,128)(2,1)S(1)} async-done(((bf16[8,64,256]{2,1,0:T(8,128)(2,1)}), bf16[8,64,256]{2,1,0:T(8,128)(2,1)S(1)}, u32[]{:S(2)}, u32[]{:S(2)}) %all-to-all-start) | async-done | bytes 262176 | tf_op jit(solution)/shard_map/cache_gather/all_to_all | solution.py:268
  21.6 0.8 %order.1.c0 = bf16[384,256]{1,0:T(8,128)(2,1)S(1)} custom-call(s32[18]{0:T(128)S(1)} %pad_add_fusion.plan_ref, bf16[512,256]{1,0:T(8,128)(2,1)S(1)} %bitcast.8), custom_call_target="tpu_custom_call" | custom-call | flops 100663296 | bytes 458824 | tf_op jit(solution)/shard_map/cache_gather/order/pallas_call | solution.py:229
  22.4 0.6 collective-permute-start.4
  23.0 0.2 collective-permute-start.3
  23.2 0.3 collective-permute-done.2.x3
  23.5 4.0 %project.1 = (bf16[512,512]{1,0:T(8,128)(2,1)S(1)}, bf16[512,256]{1,0:T(8,128)(2,1)S(1)}) custom-call(bf16[512,512]{1,0:T(8,128)(2,1)S(1)} %broadcast_select_fusion.x0.tokens_ref, bf16[512,512]{1,0:T(8,128)(2,1)S(1)} %collective-permute-done.x1, bf16[512,512]{1,0:T(8,128)(2,1)S(1)} %collective-permute-done.1.x2, ...), custom_call_target="tpu_custom_call" | custom-call | flops 1610612736 | bytes 6037504 | tf_op jit(solution)/shard_map/project/project/pallas_call | solution.py:229
  27.5 1.2 %extend.1 = bf16[512,256]{1,0:T(8,128)(2,1)S(1)} custom-call(s32[18]{0:T(128)S(1)} %pad_add_fusion.plan_ref, bf16[512,256]{1,0:T(8,128)(2,1)S(1)} %bitcast.9, bf16[512,256]{1,0:T(8,128)(2,1)S(1)} %get-tuple-element.26.kv_ref), custom_call_target="tpu_custom_call" | custom-call | flops 268435456 | bytes 786504 | tf_op jit(solution)/shard_map/extend/extend/pallas_call | solution.py:229
  28.7 1.0 %collective-permute-done.4.c2 = bf16[384,256]{1,0:T(8,128)(2,1)S(1)} collective-permute-done((bf16[384,256]{1,0:T(8,128)(2,1)S(1)}, bf16[384,256]{1,0:T(8,128)(2,1)S(1)}, u32[]{:S(2)}, u32[]{:S(2)}) %collective-permute-start.4) | collective-permute-done | bytes 196640 | tf_op jit(solution)/shard_map/cache_gather/ppermute | solution.py:265
  29.8 1.4 %collective-permute-done.5.c3 = bf16[384,256]{1,0:T(8,128)(2,1)S(1)} collective-permute-done((bf16[384,256]{1,0:T(8,128)(2,1)S(1)}, bf16[384,256]{1,0:T(8,128)(2,1)S(1)}, u32[]{:S(2)}, u32[]{:S(2)}) %collective-permute-start.5) | collective-permute-done | bytes 196640 | tf_op jit(solution)/shard_map/extend/ppermute | solution.py:265
  31.2 11.4 %attend.1 = (bf16[512,512]{1,0:T(8,128)(2,1)S(1)}, bf16[512,512]{1,0:T(8,128)(2,1)S(1)}, bf16[512,512]{1,0:T(8,128)(2,1)S(1)}, bf16[512,512]{1,0:T(8,128)(2,1)S(1)}) custom-call(s32[18]{0:T(128)S(1)} %pad_add_fusion.plan_ref, bf16[512,512]{1,0:T(8,128)(2,1)S(1)} %get-tuple-element.25.q_ref, bf16[512,256]{1,0:T(8,128)(2,1)S(1)} %get-tuple-element.26.kv_ref, ...), custom_call_target="tpu_custom_call" | custom-call | flops 3221225472 | bytes 5767240 | tf_op jit(solution)/shard_map/attend/attend/pallas_call | solution.py:229
  42.6 0.2 collective-permute-start.7
  42.8 0.4 collective-permute-start.6
  43.2 1.4 %collective-permute-done.7 = bf16[512,512]{1,0:T(8,128)(2,1)S(1)} collective-permute-done((bf16[512,512]{1,0:T(8,128)(2,1)S(1)}, bf16[512,512]{1,0:T(8,128)(2,1)S(1)}, u32[]{:S(2)}, u32[]{:S(2)}) %collective-permute-start.7) | collective-permute-done | bytes 524320 | tf_op jit(solution)/shard_map/reduce/ppermute | solution.py:265
  44.7 0.6 collective-permute-start.8
  45.3 14.1 %all_to_all.10 = bf16[8,64,256]{2,1,0:T(8,128)(2,1)S(1)} all-to-all(bf16[8,64,256]{2,1,0:T(8,128)(2,1)S(1)} %bitcast.10), channel_id=1, replica_groups=mesh['seq'=8,'tp'=4] {'seq'}, dimensions={0} | all-to-all | bytes 524288 | tf_op jit(solution)/shard_map/reduce/all_to_all | solution.py:268
  59.4 1.6 %finish.1 = bf16[512,512]{1,0:T(8,128)(2,1)} custom-call(s32[18]{0:T(128)S(1)} %pad_add_fusion.plan_ref, bf16[512,512]{1,0:T(8,128)(2,1)S(1)} %broadcast_select_fusion.x0.tokens_ref, bf16[512,512]{1,0:T(8,128)(2,1)S(1)} %get-tuple-element.29.near_ref, bf16[512,512]{1,0:T(8,128)(2,1)S(1)} %collective-permute-done.6.got_ref, ...), custom_call_target="tpu_custom_call" | custom-call | flops 1048576 | bytes 2621512 | tf_op jit(solution)/shard_map/finish/finish/pallas_call | solution.py:229
  61.0 0.7 %copy.15 = bf16[8,64,256]{2,1,0:T(8,128)(2,1)} copy(bf16[8,64,256]{2,1,0:T(8,128)(2,1)S(1)} %all_to_all.10) | data formatting | bytes 524288
  (11 shorter events, 0.2 us)
Async XLA Ops:
  0.6 5.9 %collective-permute-start = (bf16[512,512]{1,0:T(8,128)(2,1)}, bf16[512,512]{1,0:T(8,128)(2,1)S(1)}, u32[]{:S(2)}, u32[]{:S(2)}) collective-permute-start(bf16[512,512]{1,0:T(8,128)(2,1)} %param.10), channel_id=1, source_target_pairs={{0,1},{1,0},{2,3},{3,2},{4,5},{5,4},{6,7},{7,6},{8,9},{9,8},{10,11... | collective-permute-start | bytes 1572872 | tf_op jit(solution)/shard_map/tokens_gather/ppermute | solution.py:265
  1.1 15.3 %collective-permute-start.1 = (bf16[512,512]{1,0:T(8,128)(2,1)}, bf16[512,512]{1,0:T(8,128)(2,1)S(1)}, u32[]{:S(2)}, u32[]{:S(2)}) collective-permute-start(bf16[512,512]{1,0:T(8,128)(2,1)} %param.10), channel_id=1, source_target_pairs={{0,2},{1,3},{2,0},{3,1},{4,6},{5,7},{6,4},{7,5},{8,10},{9,11},{10,... | collective-permute-start | bytes 1572872 | tf_op jit(solution)/shard_map/tokens_gather/ppermute | solution.py:265
  6.5 15.1 %all-to-all-start = ((bf16[8,64,256]{2,1,0:T(8,128)(2,1)}), bf16[8,64,256]{2,1,0:T(8,128)(2,1)S(1)}, u32[]{:S(2)}, u32[]{:S(2)}) async-start(bf16[8,64,256]{2,1,0:T(8,128)(2,1)} %param.19), calls=%async_computation | async-start | bytes 524288 | tf_op jit(solution)/shard_map/cache_gather/all_to_all | solution.py:268
  21.6 1.9 %collective-permute-start.2 = (bf16[512,512]{1,0:T(8,128)(2,1)S(1)}, bf16[512,512]{1,0:T(8,128)(2,1)S(1)}, u32[]{:S(2)}, u32[]{:S(2)}) collective-permute-start(bf16[512,512]{1,0:T(8,128)(2,1)S(1)} %collective-permute-done.1.x2), channel_id=1, source_target_pairs={{0,1},{1,0},{2,3},{3,2},{4,5},{5,4},{6,7},{7,6},{8,9},{9,8},{10,11... | collective-permute-start | bytes 1572872 | tf_op jit(solution)/shard_map/project/ppermute | solution.py:265
  22.4 7.4 %collective-permute-start.4 = (bf16[384,256]{1,0:T(8,128)(2,1)S(1)}, bf16[384,256]{1,0:T(8,128)(2,1)S(1)}, u32[]{:S(2)}, u32[]{:S(2)}) collective-permute-start(bf16[384,256]{1,0:T(8,128)(2,1)S(1)} %order.1.c0), channel_id=1, source_target_pairs={{0,2},{1,3},{2,0},{3,1},{4,6},{5,7},{6,4},{7,5},{8,10},{9,11},{10,... | collective-permute-start | bytes 589832 | tf_op jit(solution)/shard_map/cache_gather/ppermute | solution.py:265
  23.0 6.8 %collective-permute-start.3 = (bf16[384,256]{1,0:T(8,128)(2,1)S(1)}, bf16[384,256]{1,0:T(8,128)(2,1)S(1)}, u32[]{:S(2)}, u32[]{:S(2)}) collective-permute-start(bf16[384,256]{1,0:T(8,128)(2,1)S(1)} %order.1.c0), channel_id=1, source_target_pairs={{0,1},{1,0},{2,3},{3,2},{4,5},{5,4},{6,7},{7,6},{8,9},{9,8},{10,11... | collective-permute-start | bytes 589832 | tf_op jit(solution)/shard_map/cache_gather/ppermute | solution.py:265
  29.8 1.4 %collective-permute-start.5 = (bf16[384,256]{1,0:T(8,128)(2,1)S(1)}, bf16[384,256]{1,0:T(8,128)(2,1)S(1)}, u32[]{:S(2)}, u32[]{:S(2)}) collective-permute-start(bf16[384,256]{1,0:T(8,128)(2,1)S(1)} %collective-permute-done.4.c2), channel_id=1, source_target_pairs={{0,1},{1,0},{2,3},{3,2},{4,5},{5,4},{6,7},{7,6},{8,9},{9,8},{10,11... | collective-permute-start | bytes 589832 | tf_op jit(solution)/shard_map/extend/ppermute | solution.py:265
  42.6 2.0 %collective-permute-start.7 = (bf16[512,512]{1,0:T(8,128)(2,1)S(1)}, bf16[512,512]{1,0:T(8,128)(2,1)S(1)}, u32[]{:S(2)}, u32[]{:S(2)}) collective-permute-start(bf16[512,512]{1,0:T(8,128)(2,1)S(1)} %get-tuple-element.32), channel_id=1, source_target_pairs={{0,1},{1,0},{2,3},{3,2},{4,5},{5,4},{6,7},{7,6},{8,9},{9,8},{10,11... | collective-permute-start | bytes 1572872 | tf_op jit(solution)/shard_map/reduce/ppermute | solution.py:265
  42.8 16.6 %collective-permute-start.6 = (bf16[512,512]{1,0:T(8,128)(2,1)S(1)}, bf16[512,512]{1,0:T(8,128)(2,1)S(1)}, u32[]{:S(2)}, u32[]{:S(2)}) collective-permute-start(bf16[512,512]{1,0:T(8,128)(2,1)S(1)} %get-tuple-element.30), channel_id=1, source_target_pairs={{0,1},{1,0},{2,3},{3,2},{4,5},{5,4},{6,7},{7,6},{8,9},{9,8},{10,11... | collective-permute-start | bytes 1572872 | tf_op jit(solution)/shard_map/finish/ppermute | solution.py:265
  44.7 14.7 %collective-permute-start.8 = (bf16[512,512]{1,0:T(8,128)(2,1)S(1)}, bf16[512,512]{1,0:T(8,128)(2,1)S(1)}, u32[]{:S(2)}, u32[]{:S(2)}) collective-permute-start(bf16[512,512]{1,0:T(8,128)(2,1)S(1)} %add_convert_fusion), channel_id=1, source_target_pairs={{0,2},{1,3},{2,0},{3,1},{4,6},{5,7},{6,4},{7,5},{8,10},{9,11},{10,... | collective-permute-start | bytes 1572872 | tf_op jit(solution)/shard_map/reduce/ppermute | solution.py:265

commit v6 on v5

v6 whole, which is shorter than its diff:
```python
import functools
import math

import jax
import jax.numpy as jnp
from jax import lax
from jax.experimental import pallas as pl
from jax.experimental.pallas import tpu as pltpu
from jax.sharding import PartitionSpec as P

EPSILON = 1e-05
MASKED = -1e30
CHUNKS = 1
PART_ROWS = 256
ROW_TILE = 128
KEY_TILE = 128
NORM_ROWS = 128
MIB = 51
PROJECT_MIB = 50.375
ATTEND_MIB = 49.75
SAFE = 60.0
F32 = jnp.float32
BF16 = jnp.bfloat16

VMEM = pl.BlockSpec(memory_space=pltpu.VMEM)
SMEM = pl.BlockSpec(memory_space=pltpu.SMEM)
HBM = pl.BlockSpec(memory_space=pltpu.HBM)


def dot(a, b):
    return lax.dot_general(a, b, (((1,), (0,)), ((), ())), preferred_element_type=F32)


def dot_t(a, b):
    return lax.dot_general(a, b, (((1,), (1,)), ((), ())), preferred_element_type=F32)


def order_kernel(share, plan_ref, arrived_ref, out_ref):
    rows, count = out_ref.shape[0], arrived_ref.shape[0]
    row = lax.broadcasted_iota(jnp.int32, (rows, 128), 0)
    block = row // share
    holder = jnp.zeros_like(block)
    for b in range(rows // share):
        holder = jnp.where(block == b, plan_ref[2 + b], holder)
    index = (holder * share + row % share)[:, :1]
    column = lax.broadcasted_iota(jnp.int32, (rows, count), 1)
    pick = jnp.where(column == index, 1.0, 0.0).astype(BF16)
    out_ref[...] = dot(pick, arrived_ref[...]).astype(BF16)


def extend_kernel(share, block_rows, plan_ref, arrived_ref, kv_ref, out_ref):
    rows = arrived_ref.shape[0]
    groups = rows // share
    held, span = plan_ref[0], plan_ref[1]
    row = lax.broadcasted_iota(jnp.int32, (rows, 128), 0)
    target = row // share
    block, holder = jnp.zeros_like(row), jnp.zeros_like(row)
    for b in range(groups):
        hit = target == plan_ref[2 + groups + b]
        block = jnp.where(hit, b, block)
        holder = jnp.where(hit, plan_ref[2 + b], holder)
    position = block * block_rows + lax.axis_index("tp") * share + row % share
    old_row = jnp.where(position < held, holder * share + row % share, -1)[:, :1]
    fresh = position - held
    new_row = jnp.where((fresh >= 0) & (fresh < span), fresh, -1)[:, :1]
    column = lax.broadcasted_iota(jnp.int32, (rows, rows), 1)
    total = dot(jnp.where(column == old_row, 1.0, 0.0).astype(BF16), arrived_ref[...])
    column = lax.broadcasted_iota(jnp.int32, (rows, kv_ref.shape[0]), 1)
    total += dot(jnp.where(column == new_row, 1.0, 0.0).astype(BF16), kv_ref[...])
    out_ref[...] = total.astype(BF16)


def project_kernel(
    x0,
    x1,
    x2,
    x3,
    gain_ref,
    wq_hbm,
    wkv_hbm,
    q_ref,
    kv_ref,
    values_ref,
    limits_ref,
    normed,
    weights,
    sems,
):
    pieces = (x0, x1, x2, x3)
    me = lax.axis_index("tp")
    rows, width = x0.shape
    features = width * len(pieces)
    kv_cols = kv_ref.shape[1]
    hd = kv_cols // 2
    q_cols = weights.shape[1] - kv_cols
    heads = q_cols // hd
    loads = []
    for j in range(len(pieces)):
        at = pl.ds(j * width, width)
        for hbm, to in ((wq_hbm, pl.ds(0, q_cols)), (wkv_hbm, pl.ds(q_cols, kv_cols))):
            loads.append(
                pltpu.make_async_copy(hbm.at[me ^ j], weights.at[at, to], sems.at[len(loads)])
            )
            loads[-1].start()

    for step in range(0, rows, NORM_ROWS):
        at = pl.ds(step, NORM_ROWS)
        values = [piece[at, :].astype(F32) for piece in pieces]
        average = jnp.sum(sum(values), axis=1, keepdims=True) / features
        centred = [v - average for v in values]
        spread = jnp.sum(sum(v * v for v in centred), axis=1, keepdims=True) / features
        scale = lax.rsqrt(spread + EPSILON)
        for j, v in enumerate(centred):
            normed[at, j * width : (j + 1) * width] = (v * scale * gain_ref[j]).astype(BF16)
    for load in loads:
        load.wait()
    query = dot(normed[...], weights[:, :q_cols]).astype(BF16)
    keyval = dot(normed[...], weights[:, q_cols:]).astype(BF16)
    kv_ref[...] = keyval
    values_ref[:, hd:] = keyval[:, hd:]
    values_ref[:, :hd] = jnp.ones((rows, hd), BF16)
    limits_ref[0] = longest(keyval[:, :hd])
    for start in range(0, rows, ROW_TILE):
        for h in range(heads):
            q_ref[pl.ds(start * heads + h * ROW_TILE, ROW_TILE), :] = query[
                start : start + ROW_TILE, h * hd : (h + 1) * hd
            ]
    limits_ref[1] = longest(q_ref[...])


def longest(x):
    x = x.astype(F32)
    squares = dot((x * x).astype(BF16), jnp.ones((x.shape[1], 128), BF16))
    return jnp.max(squares.reshape(-1, 8, 128), axis=0)


def attend_kernel(share, block_rows, start_row, rows, plan_ref, q_ref, kv_ref, new_ref, *refs):
    limits_ref, pieces, wout_hbm = refs[0], refs[1:5], refs[5]
    if start_row:
        old_ref, old_limit_ref = refs[6:8]
    else:
        old_ref, old_limit_ref = refs[10:12]
    at = 8 if start_row else 6
    far_refs, near_refs = refs[at : at + 2], refs[at + 2 : at + 4]
    total, high, context, wout, sem = refs[-5:]
    me = lax.axis_index("tp")
    held, span = plan_ref[0], plan_ref[1]
    piece_rows, width = pieces[0].shape
    hd = width // 2
    heads = q_ref.shape[0] // kv_ref.shape[0]
    load = pltpu.make_async_copy(wout_hbm, wout, sem)
    load.start()

    group = KEY_TILE * len(pieces)
    most = piece_rows // KEY_TILE
    tiles = (held + group - 1) // group
    if not start_row:
        row = lax.broadcasted_iota(jnp.int32, (KEY_TILE, hd), 0)
        place = row // share * block_rows + row % share
        limit = jnp.zeros((8, 128), F32)
        for i in range(most):
            source = pl.ds(i * KEY_TILE, KEY_TILE)
            for j, piece in enumerate(pieces):
                at = pl.ds(i * group + j * KEY_TILE, KEY_TILE)
                used = place + (me ^ j) * share + i * group < held
                old_ref[at, hd:] = jnp.where(used, piece[source, hd:].astype(F32), 0.0).astype(BF16)
                old_ref[at, :hd] = jnp.where(used, 1.0, 0.0).astype(BF16)
        for piece in pieces:
            limit = jnp.maximum(limit, longest(piece[:, :hd]))
        old_limit_ref[...] = limit

    factor = hd ** (-0.5) * math.log2(math.e)
    key_limit = jnp.max(jnp.maximum(old_limit_ref[...], limits_ref[0]))
    small = key_limit * jnp.max(limits_ref[1]) * (1.05 / hd) < SAFE * SAFE

    tile_rows = ROW_TILE * heads

    def queries(t):
        return q_ref[pl.ds(start_row * heads + t * tile_rows, tile_rows), :]

    def old_keys(i):
        source = pl.ds(i * KEY_TILE, KEY_TILE)
        return jnp.concatenate([piece[source, :hd] for piece in pieces], axis=0)

    def new_scores(t):
        known = start_row + t * ROW_TILE
        scores = dot_t(queries(t), kv_ref[pl.ds(0, known + ROW_TILE), :hd])
        to = lax.broadcasted_iota(jnp.int32, (tile_rows, ROW_TILE), 0) % ROW_TILE
        by = lax.broadcasted_iota(jnp.int32, (tile_rows, ROW_TILE), 1)
        last = jnp.where(by <= to, scores[:, known:], MASKED)
        return jnp.concatenate([scores[:, :known], last], axis=1) if known else last

    def new_values(t):
        return new_ref[pl.ds(0, start_row + (t + 1) * ROW_TILE), :]

    def put(t, both):
        out = (both[:, hd:] / both[:, :hd]).astype(BF16)
        for h in range(heads):
            context[pl.ds(t * ROW_TILE, ROW_TILE), h * hd : (h + 1) * hd] = out[
                h * ROW_TILE : (h + 1) * ROW_TILE
            ]

    def fast(used, begin):
        row_tiles = range(begin // ROW_TILE, min(begin + PART_ROWS, rows) // ROW_TILE)
        steps = [(t, i) for t in row_tiles for i in range(used + 1)]

        def score(t, i):
            return new_scores(t) if i == used else dot_t(queries(t), old_keys(i))

        ahead, both = score(*steps[0]), None
        for at, (t, i) in enumerate(steps):
            scores = ahead
            if at + 1 < len(steps):
                ahead = score(*steps[at + 1])
            weights = jnp.exp2(scores * factor).astype(BF16)
            values = new_values(t) if i == used else old_ref[pl.ds(i * group, group), :]
            part = dot(weights, values)
            both = part if i == 0 else both + part
            if i == used:
                put(t, both)

    def exact(t):
        column = lax.broadcasted_iota(jnp.int32, (tile_rows, group), 1)
        within = column % KEY_TILE
        owner = me ^ (column // KEY_TILE)
        place = within // share * block_rows + within % share + owner * share

        def old_scores(i):
            scores = dot_t(queries(t), old_keys(pl.multiple_of(i, 1)))
            return jnp.where(place + i * group < held, scores, MASKED)

        def raise_high(i, carry):
            top = jnp.max(old_scores(i), axis=1, keepdims=True)
            high[...] = jnp.maximum(high[...], top)
            return carry

        def add(i, carry):
            weights = jnp.exp2((old_scores(i) - high[:, :1]) * factor).astype(BF16)
            total[...] += dot(weights, old_ref[pl.ds(pl.multiple_of(i * group, group), group), :])
            return carry

        high[...] = jnp.zeros_like(high) + jnp.max(new_scores(t), axis=1, keepdims=True)
        lax.fori_loop(0, tiles, raise_high, 0)
        weights = jnp.exp2((new_scores(t) - high[:, :1]) * factor).astype(BF16)
        total[...] = dot(weights, new_values(t))
        lax.fori_loop(0, tiles, add, 0)
        put(t, total[...])

    for begin in range(0, rows, PART_ROWS):
        busy = start_row + begin < span
        for used in range(1, most + 1):
            pl.when(busy & small & (tiles == used))(functools.partial(fast, used, begin))

        @pl.when(busy & jnp.logical_not(small))
        def _():
            for t in range(begin // ROW_TILE, min(begin + PART_ROWS, rows) // ROW_TILE):
                exact(t)

        @pl.when(jnp.logical_not(busy))
        def _():
            context[pl.ds(begin, PART_ROWS), :] = jnp.zeros((PART_ROWS, context.shape[1]), BF16)

    load.wait()
    cols = wout.shape[1] // 4
    for k in (3, 1, 2, 0):
        columns = pl.ds(pl.multiple_of((me ^ k) * cols, cols), cols)
        part = dot(context[...], wout[:, columns]).astype(BF16)
        if k & 1:
            far_refs[k >> 1][...] = part
        else:
            near_refs[k >> 1][...] = part


def finish_kernel(at, plan_ref, tokens_ref, near_ref, got_ref, crossed_ref, *refs):
    out_hbm, done, sems = refs[-3:]
    rows = near_ref.shape[0]
    half = rows // 2
    stores = []
    for i in range(2):
        here = pl.ds(i * half, half)
        there = pl.ds(at + i * half, half)
        kept = near_ref[here, :].astype(F32) + got_ref[here, :].astype(F32)
        total = tokens_ref[there, :].astype(F32) + (kept + crossed_ref[here, :].astype(F32))
        row = lax.broadcasted_iota(jnp.int32, total.shape, 0) + (at + i * half)
        done[here, :] = jnp.where(row < plan_ref[1], total, 0.0).astype(BF16)
        stores.append(pltpu.make_async_copy(done.at[here], out_hbm.at[there], sems.at[i]))
        stores[-1].start()
    for store in stores:
        store.wait()


def call(
    kernel, out_shape, in_specs, args, flops, mib=MIB, scratch=(), exps=0, name=None, into=None
):
    outs = out_shape if isinstance(out_shape, (list, tuple)) else [out_shape]
    moved = sum(a.size * a.dtype.itemsize for a in list(args) + list(outs))
    return pl.pallas_call(
        kernel,
        out_shape=out_shape,
        in_specs=in_specs,
        out_specs=jax.tree.map(lambda _: VMEM if into is None else HBM, out_shape),
        input_output_aliases=into or {},
        scratch_shapes=list(scratch),
        cost_estimate=pl.CostEstimate(flops=flops, bytes_accessed=moved, transcendentals=exps),
        compiler_params=pltpu.CompilerParams(vmem_limit_bytes=int(mib * 1024 * 1024)),
        name=name,
    )(*args)


def body(
    tokens,
    norm_gain,
    w_query,
    w_keyval,
    w_out,
    span_lens,
    cached_lens,
    old_table,
    new_table,
    old_cache,
):
    tp = lax.axis_size("tp")
    groups, share, width = old_cache.shape
    block_rows = share * tp
    capacity = groups * block_rows
    rows, cols = tokens.shape
    q_cols = w_query.shape[1]
    features = w_query.shape[0]
    hd = width // 2
    most_held = capacity - rows
    piece_rows = most_held // tp

    def swap(x, bit):
        return lax.ppermute(x, "tp", [(i, i ^ bit) for i in range(tp)])

    def exchange(x):
        return lax.all_to_all(x, "seq", split_axis=0, concat_axis=0, tiled=True)

    with jax.named_scope("tokens_gather"):
        plan = jnp.concatenate([cached_lens, span_lens, old_table[0], new_table[0]])
        gain = norm_gain.reshape(tp, cols)
        gain = jnp.concatenate(
            [lax.dynamic_slice_in_dim(gain, lax.axis_index("tp") ^ j, 1) for j in range(tp)]
        ).reshape(tp, 1, cols)
        in_span = lax.broadcasted_iota(jnp.int32, (rows, 1), 0) < span_lens[0]
        own = jnp.where(in_span, tokens, jnp.zeros_like(tokens))
        across = swap(tokens, 2)
        beside = swap(tokens, 1)

    with jax.named_scope("cache_gather"):
        beside, stored = lax.optimization_barrier((beside, old_cache))
        arrived = exchange(stored).reshape(groups * share, width)
        arrived, across, own, gain, plan = lax.optimization_barrier(
            (arrived, across, own, gain, plan)
        )
        ordered = call(
            functools.partial(order_kernel, share),
            jax.ShapeDtypeStruct((piece_rows, width), BF16),
            [SMEM, VMEM],
            (plan, arrived),
            flops=2 * piece_rows * groups * share * width,
            name="order",
        )
        c_across = swap(ordered, 2)
        c_beside = swap(ordered, 1)

    with jax.named_scope("project"):
        corner = swap(across, 1)
        stacked = rows * (q_cols // hd)
        query, keyval, values, limits = call(
            project_kernel,
            [
                jax.ShapeDtypeStruct((stacked, hd), BF16),
                jax.ShapeDtypeStruct((rows, width), BF16),
                jax.ShapeDtypeStruct((rows, width), BF16),
                jax.ShapeDtypeStruct((2, 8, 128), F32),
            ],
            [VMEM] * 5 + [HBM] * 2,
            (
                own,
                beside,
                across,
                corner,
                gain,
                w_query.reshape(tp, cols, q_cols),
                w_keyval.reshape(tp, cols, width),
            ),
            flops=2 * rows * features * (q_cols + width),
            mib=PROJECT_MIB,
            scratch=[
                pltpu.VMEM((rows, features), BF16),
                pltpu.VMEM((features, q_cols + width), BF16),
                pltpu.SemaphoreType.DMA((2 * tp,)),
            ],
            name="project",
        )

    with jax.named_scope("extend"):
        sent = call(
            functools.partial(extend_kernel, share, block_rows),
            jax.ShapeDtypeStruct((groups * share, width), BF16),
            [SMEM] + [VMEM] * 2,
            (plan, arrived, keyval),
            flops=4 * groups * share * groups * share * width,
            name="extend",
        )
        sent, c_across = lax.optimization_barrier((sent, c_across))
        cached = (ordered, c_beside, c_across, swap(c_across, 1))

    part = rows // CHUNKS
    tile_rows = ROW_TILE * (q_cols // hd)
    old = []
    mixed = None
    for c in range(CHUNKS):
        with jax.named_scope("attend"):
            outs = [jax.ShapeDtypeStruct((part, cols), BF16)] * 4
            if not old:
                outs += [
                    jax.ShapeDtypeStruct((most_held, width), BF16),
                    jax.ShapeDtypeStruct((8, 128), F32),
                ]
            seen = most_held + (c + 1) * part
            far0, far1, near0, near1, *made = call(
                functools.partial(attend_kernel, share, block_rows, c * part, part),
                outs,
                [SMEM] + [VMEM] * 8 + [HBM] + [VMEM] * len(old),
                (plan, query, keyval, values, limits, *cached, w_out, *old),
                flops=4 * part * seen * q_cols + 2 * part * q_cols * features,
                exps=part * seen * (q_cols // hd),
                mib=ATTEND_MIB,
                scratch=[
                    pltpu.VMEM((tile_rows, width), F32),
                    pltpu.VMEM((tile_rows, hd), F32),
                    pltpu.VMEM((part, q_cols), BF16),
                    pltpu.VMEM(w_out.shape, BF16),
                    pltpu.SemaphoreType.DMA,
                ],
                name="attend",
            )
            old = old or made
        with jax.named_scope("reduce"):
            got1 = swap(far1, 1)
            pair = (near1.astype(F32) + got1.astype(F32)).astype(BF16)
            query, pair = lax.optimization_barrier((query, pair))
            if c == CHUNKS - 1:
                pair, sent = lax.optimization_barrier((pair, sent))
            crossed = swap(pair, 2)
            got0 = swap(far0, 1)
        with jax.named_scope("finish"):
            mixed = call(
                functools.partial(finish_kernel, c * part),
                jax.ShapeDtypeStruct((rows, cols), BF16),
                [SMEM] + [VMEM] * 4 + [HBM] * (c > 0),
                (plan, own, near0, got0, crossed, *([mixed] if c else [])),
                flops=4 * part * cols,
                scratch=[pltpu.VMEM((part, cols), BF16), pltpu.SemaphoreType.DMA((2,))],
                name="finish",
                into={5: 0} if c else {},
            )
    with jax.named_scope("exchange"):
        new_cache = exchange(sent.reshape(groups, share, width))
    return (mixed, new_cache)


def solution(mesh):
    in_specs = (
        P("seq", "tp"),
        P(),
        P(None, "tp"),
        P(),
        P("tp", None),
        P("seq"),
        P("seq"),
        P("seq", None),
        P("seq", None),
        P("seq", "tp", None),
    )
    out_specs = (P("seq", "tp"), P("seq", "tp", None))
    return jax.shard_map(body, mesh=mesh, in_specs=in_specs, out_specs=out_specs, check_vma=False)
```

time: 62.2 us -> 67 us (1.077)
  Pallas kernels: 19 us -> 25.7 us
  blocking collectives: 14.1 us -> 11.8 us
    pallas_call x5, Pallas kernels: 19 us -> 25.7 us  [call(): pl.pallas_call(kernel, out_shape=out_shape, in_specs=in_specs, out_specs=...]
    all_to_all x1, blocking collectives: 14.1 us -> 11.8 us  [exchange(): return lax.all_to_all(x, 'seq', split_axis=0, concat_axis=0, tiled=True)]
    ppermute x9, waiting for transfers between devices: 7.1 us -> 7.94 us  [swap(): return lax.ppermute(x, 'tp', [(i, i ^ bit) for i in range(tp)])]
    all_to_all x1, waiting for transfers between devices: 5.1 us -> 4.4 us  [exchange(): return lax.all_to_all(x, 'seq', split_axis=0, concat_axis=0, tiled=True)]
  transfers between devices with their start and end apart: 10 -> 10, of which waited for: 6 -> 7; matrix products, arithmetic and copies ran while one was open for 5% -> 4% of each run, Pallas kernels for 10% -> 10%
where the time goes in v6:
time: 67 us; the launch traced here: 66.6 us
  Pallas kernels  25.7 us (38%)
  waiting for transfers between devices  12.3 us (18%)
  blocking collectives  11.8 us (18%)
  starting transfers between devices  11.2 us (17%)
  other arithmetic  2.08 us (3%)
  between operations  2.01 us (3%)
  local copies, waits for them, and re-layouts  1.43 us (2%)
    pallas_call x5, Pallas kernels, call(): pl.pallas_call(kernel, out_shape=out_shape, in_specs=in_specs, out_specs=...  25.7 us
    all_to_all x1, blocking collectives, exchange(): return lax.all_to_all(x, 'seq', split_axis=0, concat_axis=0, tiled=True)  11.8 us
    ppermute x9, waiting for transfers between devices, swap(): return lax.ppermute(x, 'tp', [(i, i ^ bit) for i in range(tp)])  7.94 us
    all_to_all x1, starting transfers between devices, exchange(): return lax.all_to_all(x, 'seq', split_axis=0, concat_axis=0, tiled=True)  5.82 us
    ppermute x9, starting transfers between devices, swap(): return lax.ppermute(x, 'tp', [(i, i ^ bit) for i in range(tp)])  5.37 us
    all_to_all x1, waiting for transfers between devices, exchange(): return lax.all_to_all(x, 'seq', split_axis=0, concat_axis=0, tiled=True)  4.4 us
  transfers between devices with their start and end apart: 10, of which 7 were waited for; matrix products, arithmetic and copies ran while one was open for 4% of the time, Pallas kernels for 10%

profile of v6, /device:TPU:0, one launch (start us, length us, event | category | flops | bytes accessed | tf_op | source)
XLA Modules:
  0.0 66.6 jit_solution(7405283361082831575)
XLA Ops:
  0.6 0.5 collective-permute-start
  1.1 2.6 %collective-permute-start.1 = (bf16[512,512]{1,0:T(8,128)(2,1)}, bf16[512,512]{1,0:T(8,128)(2,1)S(1)}, u32[]{:S(2)}, u32[]{:S(2)}) collective-permute-start(bf16[512,512]{1,0:T(8,128)(2,1)} %param.10), channel_id=1, source_target_pairs={{0,2},{1,3},{2,0},{3,1},{4,6},{5,7},{6,4},{7,5},{8,10},{9,11},{10,... | collective-permute-start | bytes 1572872 | tf_op jit(solution)/shard_map/tokens_gather/ppermute | solution.py:334
  3.7 0.7 %reshape.28 = f32[4,512]{1,0:T(4,128)S(1)} reshape(f32[2048]{0:T(1024)} %param.11) | data formatting | bytes 16384 | tf_op jit(solution)/shard_map/tokens_gather/reshape | solution.py:341
  5.8 5.8 %all-to-all-start = ((bf16[8,64,256]{2,1,0:T(8,128)(2,1)}), bf16[8,64,256]{2,1,0:T(8,128)(2,1)S(1)}, u32[]{:S(2)}, u32[]{:S(2)}) async-start(bf16[8,64,256]{2,1,0:T(8,128)(2,1)} %param.19), calls=%async_computation | async-start | bytes 524288 | tf_op jit(solution)/shard_map/cache_gather/all_to_all | solution.py:337
  11.6 0.8 %pad_add_fusion.plan_ref = s32[18]{0:T(128)S(1)} fusion(s32[8]{0:T(128)} %bitcast.11, s32[8]{0:T(128)} %bitcast.12, s32[1]{0:T(128)} %copy.13, s32[1]{0:T(128)S(6)} %copy.14), kind=kLoop, calls=%fused_computation.8 | loop fusion | flops 54 | bytes 144 | tf_op jit(solution)/shard_map/tokens_gather/concatenate | solution.py:340
  12.4 1.2 %broadcast_select_fusion.x0.tokens_ref = bf16[512,512]{1,0:T(8,128)(2,1)S(1)} fusion(bf16[512,512]{1,0:T(8,128)(2,1)} %param.10, pred[512]{0:T(512)(128)(4,1)S(1)} %iota_compare_fusion), kind=kLoop, calls=%fused_computation.1 | loop fusion | flops 262144 | bytes 1049088 | tf_op jit(solution)/shard_map/tokens_gather/jit(_where)/select_n | solution.py:346
  13.6 2.9 %collective-permute-done.1.x2 = bf16[512,512]{1,0:T(8,128)(2,1)S(1)} collective-permute-done((bf16[512,512]{1,0:T(8,128)(2,1)}, bf16[512,512]{1,0:T(8,128)(2,1)S(1)}, u32[]{:S(2)}, u32[]{:S(2)}) %collective-permute-start.1) | collective-permute-done | bytes 524320 | tf_op jit(solution)/shard_map/tokens_gather/ppermute | solution.py:334
  16.5 4.4 %all-to-all-done = bf16[8,64,256]{2,1,0:T(8,128)(2,1)S(1)} async-done(((bf16[8,64,256]{2,1,0:T(8,128)(2,1)}), bf16[8,64,256]{2,1,0:T(8,128)(2,1)S(1)}, u32[]{:S(2)}, u32[]{:S(2)}) %all-to-all-start) | async-done | bytes 262176 | tf_op jit(solution)/shard_map/cache_gather/all_to_all | solution.py:337
  20.9 0.8 %order.1.refs_1_ = bf16[384,256]{1,0:T(8,128)(2,1)S(1)} custom-call(s32[18]{0:T(128)S(1)} %pad_add_fusion.plan_ref, bf16[512,256]{1,0:T(8,128)(2,1)S(1)} %bitcast.8), custom_call_target="tpu_custom_call" | custom-call | flops 100663296 | bytes 458824 | tf_op jit(solution)/shard_map/cache_gather/order/pallas_call | solution.py:297
  21.7 0.6 collective-permute-start.4
  22.3 0.2 collective-permute-start.3
  22.5 0.3 collective-permute-done.2.x3
  22.8 4.6 %project.1 = (bf16[2048,128]{1,0:T(8,128)(2,1)S(1)}, bf16[512,256]{1,0:T(8,128)(2,1)S(1)}, bf16[512,256]{1,0:T(8,128)(2,1)S(1)}, f32[2,8,128]{2,1,0:T(8,128)S(1)}) custom-call(bf16[512,512]{1,0:T(8,128)(2,1)S(1)} %broadcast_select_fusion.x0.tokens_ref, bf16[512,512]{1,0:T(8,128)(2,1)S(1)} %collective-permute-done.x1, ...), custom_call_target="tpu_custom_call" | custom-call | flops 1610612736 | bytes 6307840 | tf_op jit(solution)/shard_map/project/project/pallas_call | solution.py:297
  27.4 1.2 %extend.1 = bf16[512,256]{1,0:T(8,128)(2,1)S(1)} custom-call(s32[18]{0:T(128)S(1)} %pad_add_fusion.plan_ref, bf16[512,256]{1,0:T(8,128)(2,1)S(1)} %bitcast.9, bf16[512,256]{1,0:T(8,128)(2,1)S(1)} %get-tuple-element.29.kv_ref), custom_call_target="tpu_custom_call" | custom-call | flops 268435456 | bytes 786504 | tf_op jit(solution)/shard_map/extend/extend/pallas_call | solution.py:297
  28.6 0.5 collective-permute-done.4.refs_3_
  29.1 1.4 %collective-permute-done.5.refs_4_ = bf16[384,256]{1,0:T(8,128)(2,1)S(1)} collective-permute-done((bf16[384,256]{1,0:T(8,128)(2,1)S(1)}, bf16[384,256]{1,0:T(8,128)(2,1)S(1)}, u32[]{:S(2)}, u32[]{:S(2)}) %collective-permute-start.5) | collective-permute-done | bytes 196640 | tf_op jit(solution)/shard_map/extend/ppermute | solution.py:334
  30.5 17.6 %attend.1 = (bf16[512,512]{1,0:T(8,128)(2,1)S(1)}, bf16[512,512]{1,0:T(8,128)(2,1)S(1)}, bf16[512,512]{1,0:T(8,128)(2,1)S(1)}, bf16[512,512]{1,0:T(8,128)(2,1)S(...) custom-call(s32[18]{0:T(128)S(1)} %pad_add_fusion.plan_ref, bf16[2048,128]{1,0:T(8,128)(2,1)S(1)} %get-tuple-element.28.q_ref, ...), custom_call_target="tpu_custom_call" | custom-call | flops 3221225472 | bytes 6828104 | tf_op jit(solution)/shard_map/attend/attend/pallas_call | solution.py:297
  48.3 0.4 collective-permute-start.6
  48.7 1.4 %collective-permute-done.7 = bf16[512,512]{1,0:T(8,128)(2,1)S(1)} collective-permute-done((bf16[512,512]{1,0:T(8,128)(2,1)S(1)}, bf16[512,512]{1,0:T(8,128)(2,1)S(1)}, u32[]{:S(2)}, u32[]{:S(2)}) %collective-permute-start.7) | collective-permute-done | bytes 524320 | tf_op jit(solution)/shard_map/reduce/ppermute | solution.py:334
  50.2 0.9 %collective-permute-start.8 = (bf16[512,512]{1,0:T(8,128)(2,1)S(1)}, bf16[512,512]{1,0:T(8,128)(2,1)S(1)}, u32[]{:S(2)}, u32[]{:S(2)}) collective-permute-start(bf16[512,512]{1,0:T(8,128)(2,1)S(1)} %add_convert_fusion), channel_id=1, source_target_pairs={{0,2},{1,3},{2,0},{3,1},{4,6},{5,7},{6,4},{7,5},{8,10},{9,11},{10,... | collective-permute-start | bytes 1572872 | tf_op jit(solution)/shard_map/reduce/ppermute | solution.py:334
  51.1 11.8 %all_to_all.10 = bf16[8,64,256]{2,1,0:T(8,128)(2,1)S(1)} all-to-all(bf16[8,64,256]{2,1,0:T(8,128)(2,1)S(1)} %bitcast.10), channel_id=1, replica_groups=mesh['seq'=8,'tp'=4] {'seq'}, dimensions={0} | all-to-all | bytes 524288 | tf_op jit(solution)/shard_map/exchange/all_to_all | solution.py:337
  62.9 1.4 %collective-permute-done.8.crossed_ref = bf16[512,512]{1,0:T(8,128)(2,1)S(1)} collective-permute-done((bf16[512,512]{1,0:T(8,128)(2,1)S(1)}, bf16[512,512]{1,0:T(8,128)(2,1)S(1)}, u32[]{:S(2)}, u32[]{:S(2)}) %collective-permute-start.8) | collective-permute-done | bytes 524320 | tf_op jit(solution)/shard_map/reduce/ppermute | solution.py:334
  64.3 1.6 %finish.1 = bf16[512,512]{1,0:T(8,128)(2,1)} custom-call(s32[18]{0:T(128)S(1)} %pad_add_fusion.plan_ref, bf16[512,512]{1,0:T(8,128)(2,1)S(1)} %broadcast_select_fusion.x0.tokens_ref, bf16[512,512]{1,0:T(8,128)(2,1)S(1)} %get-tuple-element.34.near_ref, bf16[512,512]{1,0:T(8,128)(2,1)S(1)} %collective-permute-done.6.got_ref, ...), custom_call_target="tpu_custom_call" | custom-call | flops 1048576 | bytes 2621512 | tf_op jit(solution)/shard_map/finish/finish/pallas_call | solution.py:297
  65.9 0.7 %copy.15 = bf16[8,64,256]{2,1,0:T(8,128)(2,1)} copy(bf16[8,64,256]{2,1,0:T(8,128)(2,1)S(1)} %all_to_all.10) | data formatting | bytes 524288
  (11 shorter events, 0.4 us)
Async XLA Ops:
  0.6 5.2 %collective-permute-start = (bf16[512,512]{1,0:T(8,128)(2,1)}, bf16[512,512]{1,0:T(8,128)(2,1)S(1)}, u32[]{:S(2)}, u32[]{:S(2)}) collective-permute-start(bf16[512,512]{1,0:T(8,128)(2,1)} %param.10), channel_id=1, source_target_pairs={{0,1},{1,0},{2,3},{3,2},{4,5},{5,4},{6,7},{7,6},{8,9},{9,8},{10,11... | collective-permute-start | bytes 1572872 | tf_op jit(solution)/shard_map/tokens_gather/ppermute | solution.py:334
  1.1 15.3 %collective-permute-start.1 = (bf16[512,512]{1,0:T(8,128)(2,1)}, bf16[512,512]{1,0:T(8,128)(2,1)S(1)}, u32[]{:S(2)}, u32[]{:S(2)}) collective-permute-start(bf16[512,512]{1,0:T(8,128)(2,1)} %param.10), channel_id=1, source_target_pairs={{0,2},{1,3},{2,0},{3,1},{4,6},{5,7},{6,4},{7,5},{8,10},{9,11},{10,... | collective-permute-start | bytes 1572872 | tf_op jit(solution)/shard_map/tokens_gather/ppermute | solution.py:334
  5.8 15.1 %all-to-all-start = ((bf16[8,64,256]{2,1,0:T(8,128)(2,1)}), bf16[8,64,256]{2,1,0:T(8,128)(2,1)S(1)}, u32[]{:S(2)}, u32[]{:S(2)}) async-start(bf16[8,64,256]{2,1,0:T(8,128)(2,1)} %param.19), calls=%async_computation | async-start | bytes 524288 | tf_op jit(solution)/shard_map/cache_gather/all_to_all | solution.py:337
  20.9 1.9 %collective-permute-start.2 = (bf16[512,512]{1,0:T(8,128)(2,1)S(1)}, bf16[512,512]{1,0:T(8,128)(2,1)S(1)}, u32[]{:S(2)}, u32[]{:S(2)}) collective-permute-start(bf16[512,512]{1,0:T(8,128)(2,1)S(1)} %collective-permute-done.1.x2), channel_id=1, source_target_pairs={{0,1},{1,0},{2,3},{3,2},{4,5},{5,4},{6,7},{7,6},{8,9},{9,8},{10,11... | collective-permute-start | bytes 1572872 | tf_op jit(solution)/shard_map/project/ppermute | solution.py:334
  21.7 7.4 %collective-permute-start.4 = (bf16[384,256]{1,0:T(8,128)(2,1)S(1)}, bf16[384,256]{1,0:T(8,128)(2,1)S(1)}, u32[]{:S(2)}, u32[]{:S(2)}) collective-permute-start(bf16[384,256]{1,0:T(8,128)(2,1)S(1)} %order.1.refs_1_), channel_id=1, source_target_pairs={{0,2},{1,3},{2,0},{3,1},{4,6},{5,7},{6,4},{7,5},{8,10},{9,11},{10,... | collective-permute-start | bytes 589832 | tf_op jit(solution)/shard_map/cache_gather/ppermute | solution.py:334
  22.3 6.8 %collective-permute-start.3 = (bf16[384,256]{1,0:T(8,128)(2,1)S(1)}, bf16[384,256]{1,0:T(8,128)(2,1)S(1)}, u32[]{:S(2)}, u32[]{:S(2)}) collective-permute-start(bf16[384,256]{1,0:T(8,128)(2,1)S(1)} %order.1.refs_1_), channel_id=1, source_target_pairs={{0,1},{1,0},{2,3},{3,2},{4,5},{5,4},{6,7},{7,6},{8,9},{9,8},{10,11... | collective-permute-start | bytes 589832 | tf_op jit(solution)/shard_map/cache_gather/ppermute | solution.py:334
  29.1 1.4 %collective-permute-start.5 = (bf16[384,256]{1,0:T(8,128)(2,1)S(1)}, bf16[384,256]{1,0:T(8,128)(2,1)S(1)}, u32[]{:S(2)}, u32[]{:S(2)}) collective-permute-start(bf16[384,256]{1,0:T(8,128)(2,1)S(1)} %collective-permute-done.4.refs_3_), channel_id=1, source_target_pairs={{0,1},{1,0},{2,3},{3,2},{4,5},{5,4},{6,7},{7,6},{8,9},{9,8},{10,11... | collective-permute-start | bytes 589832 | tf_op jit(solution)/shard_map/extend/ppermute | solution.py:334
  48.1 2.0 %collective-permute-start.7 = (bf16[512,512]{1,0:T(8,128)(2,1)S(1)}, bf16[512,512]{1,0:T(8,128)(2,1)S(1)}, u32[]{:S(2)}, u32[]{:S(2)}) collective-permute-start(bf16[512,512]{1,0:T(8,128)(2,1)S(1)} %get-tuple-element.37), channel_id=1, source_target_pairs={{0,1},{1,0},{2,3},{3,2},{4,5},{5,4},{6,7},{7,6},{8,9},{9,8},{10,11... | collective-permute-start | bytes 1572872 | tf_op jit(solution)/shard_map/reduce/ppermute | solution.py:334
  48.3 14.5 %collective-permute-start.6 = (bf16[512,512]{1,0:T(8,128)(2,1)S(1)}, bf16[512,512]{1,0:T(8,128)(2,1)S(1)}, u32[]{:S(2)}, u32[]{:S(2)}) collective-permute-start(bf16[512,512]{1,0:T(8,128)(2,1)S(1)} %get-tuple-element.35), channel_id=1, source_target_pairs={{0,1},{1,0},{2,3},{3,2},{4,5},{5,4},{6,7},{7,6},{8,9},{9,8},{10,11... | collective-permute-start | bytes 1572872 | tf_op jit(solution)/shard_map/reduce/ppermute | solution.py:334
  50.2 14.0 %collective-permute-start.8 = (bf16[512,512]{1,0:T(8,128)(2,1)S(1)}, bf16[512,512]{1,0:T(8,128)(2,1)S(1)}, u32[]{:S(2)}, u32[]{:S(2)}) collective-permute-start(bf16[512,512]{1,0:T(8,128)(2,1)S(1)} %add_convert_fusion), channel_id=1, source_target_pairs={{0,2},{1,3},{2,0},{3,1},{4,6},{5,7},{6,4},{7,5},{8,10},{9,11},{10,... | collective-permute-start | bytes 1572872 | tf_op jit(solution)/shard_map/reduce/ppermute | solution.py:334
